TPU v7x, 256 devices: a whole 4x4x8 slice. The times are simulated.
256 devices in a mesh: sect: 64 (over x, z, core), blk: 4 (over y).
Axes of the slice: x: 4, y: 4, z: 8, core: 2. Of those that a mesh axis runs over, the one named last changes fastest.
Arguments:
- psi_guess: bfloat16 [64, 32, 128, 128], P('sect', 'blk'), may hold values from -6 to 6
- sector_sizes: int32 [64, 32], P('sect'), may hold values from 1 to 128, 2048 in all within a row
- slot_sector: int32 [32], replicated, may hold values from 0 to 31, each once
- pair_table: int32 [32, 16], replicated, may hold values from 0 to 31
- left_ops: bfloat16 [64, 32, 16, 128, 128], P('sect', 'blk'), may hold values from -0.5 to 0.5
- right_ops: bfloat16 [64, 32, 16, 128, 128], P('sect', 'blk'), may hold values from -0.5 to 0.5
- decay: float32 [64, 32, 128], P('sect', 'blk'), may hold values from 0.9 to 0.999
- source_h: float32 [64, 32, 128, 128], P('sect', 'blk'), may hold values from -1 to 1
- precond: float32 [64, 32, 128, 128], P('sect', 'blk'), may hold values from 1 to 10
- inv_sv: float32 [64, 32, 128], P('sect', 'blk'), may hold values from 1 to 10
- ranks: int32 [64, 32], P('sect'), may hold values from 1 to 128
Outputs:
- ground: bfloat16 [64, 32, 128, 128], P('sect', 'blk')
- energies: float32 [64], P('sect')
- merged: bfloat16 [64, 32, 128, 128], P('sect', 'blk')
Inputs may be any that keep to these rules, and one draw needn't show every extreme that they name: `slot_sector`: each sector appears in exactly one slot. `sector_sizes`: each row sums to 2048.
All inputs are finite; a program needn't handle non-finite values.
Results may differ from a plain program's by a relative error of at most 0.02.
Values may be sent and summed in bfloat16 or wider, within the bound.
No kernel may reach another device: no remote copies, remote signals or barrier semaphores. Data moves between devices by JAX's collectives and lax.ppermute only.
A program may use at most 128 MiB of HBM per device.

v0:
```python
import jax
import jax.numpy as jnp
from jax import lax
from jax.sharding import PartitionSpec as P

STEPS = 3


damping = 0.5


def prefix_2(part, axis, combine, identity):
    place = lax.axis_index(axis)
    gathered = jax.tree.map(lambda a: lax.all_gather(a, axis), part)
    state = jax.tree.map(lambda a, e: jnp.zeros_like(a) + jnp.asarray(e, a.dtype), part, identity)

    def one(lap, state):
        return combine(
            state, jax.tree.map(lambda a: lax.dynamic_index_in_dim(a, lap, 0, False), gathered)
        )

    return lax.fori_loop(0, place, one, state)


def from_behind(value, axis, steps):
    count = lax.axis_size(axis)
    leading, last = (max(0, -steps), min(count, count - steps))
    return lax.ppermute(value, axis, [(source, source + steps) for source in range(leading, last)])


def compose(earlier, later):
    factor_one, source_one = earlier
    factor_two, source_two = later
    return (
        factor_one * factor_two,
        factor_two[:, :, None] * source_one * factor_two[:, None, :] + source_two,
    )


def shards(
    psi_guess,
    sector_sizes,
    slot_sector,
    pair_table,
    left_ops,
    right_ops,
    decay,
    source_h,
    precond,
    inv_sv,
    ranks,
):
    sec_dev = psi_guess.shape[1]
    capacity = psi_guess.shape[2]
    sector_count = slot_sector.shape[0]
    terms_count = pair_table.shape[1]
    positions = jnp.arange(capacity, dtype=jnp.int32)
    sector_ids = jnp.arange(sector_count, dtype=jnp.int32)
    first_slot = lax.axis_index("blk") * sec_dev
    own_sectors = lax.dynamic_slice_in_dim(slot_sector, first_slot, sec_dev)
    sector_pick = (own_sectors[:, None] == sector_ids[None, :]).astype(jnp.int32)
    own_sizes = jnp.sum(sector_pick * sector_sizes[0][None, :], axis=1)
    own_ranks = jnp.sum(sector_pick * ranks[0][None, :], axis=1)
    own_pairs = jnp.sum(sector_pick[:, :, None] * pair_table[None, :, :], axis=1)
    slot_of = jnp.sum(
        jnp.where(slot_sector[:, None] == sector_ids[None, :], sector_ids[:, None], 0), axis=0
    )
    source_slot = jnp.sum(
        jnp.where(own_pairs[:, :, None] == sector_ids[None, None, :], slot_of[None, None, :], 0),
        axis=2,
    ).reshape(-1)
    inside = positions[None, :] < own_sizes[:, None]
    support = (inside[:, :, None] & inside[:, None, :]).astype(jnp.float32)
    psi_now = (psi_guess[0].astype(jnp.float32) * support).astype(jnp.bfloat16)
    prefix = prefix_2(
        (decay[0], source_h[0]),
        "sect",
        compose,
        (jnp.ones_like(decay[0]), jnp.zeros_like(source_h[0])),
    )
    env_low = prefix[1].astype(jnp.bfloat16)
    left_now = left_ops[0]
    right_now = right_ops[0]
    precond_now = precond[0]
    entry_count = float(sector_count * capacity * capacity)
    rayleigh = jnp.float32(0.0)
    for iteration in range(STEPS):
        gathered = lax.all_gather(psi_now, "blk", axis=0, tiled=True)
        sources = jnp.take(gathered, source_slot, axis=0)
        sources = sources.reshape(sec_dev, terms_count, capacity, capacity)
        inner_left = jnp.einsum(
            "jwik,jwkl->jwil", left_now, sources, preferred_element_type=jnp.float32
        ).astype(jnp.bfloat16)
        operator_terms = jnp.einsum(
            "jwil,jwml->jim", inner_left, right_now, preferred_element_type=jnp.float32
        )
        env_term = jnp.einsum("jik,jkl->jil", env_low, psi_now, preferred_element_type=jnp.float32)
        applied = (env_term + operator_terms) * support
        current = psi_now.astype(jnp.float32)
        numerator, intersection = lax.psum(
            (jnp.sum(current * applied), jnp.sum(current * current)), "blk"
        )
        rayleigh = numerator / intersection
        updated = current - damping * (applied - rayleigh * current) / precond_now
        square_sum = lax.psum(jnp.sum(updated * updated), "blk")
        psi_now = (updated * lax.rsqrt(square_sum / entry_count + 1e-06)).astype(jnp.bfloat16)
    following = from_behind(psi_now, "sect", -1)
    kept_mask = (positions[None, :] < own_ranks[:, None]).astype(jnp.float32)
    weight = inv_sv[0] * kept_mask / capacity
    scaled = (psi_now.astype(jnp.float32) * weight[:, None, :]).astype(jnp.bfloat16)
    merged = jnp.einsum(
        "jik,jkl->jil", scaled, following, preferred_element_type=jnp.float32
    ).astype(jnp.bfloat16)
    return (psi_now[None], jnp.reshape(rayleigh, (1,)), merged[None])


def solution(mesh):
    in_specs = (
        P("sect", "blk", None, None),
        P("sect", None),
        P(),
        P(),
        P("sect", "blk", None, None, None),
        P("sect", "blk", None, None, None),
        P("sect", "blk", None),
        P("sect", "blk", None, None),
        P("sect", "blk", None, None),
        P("sect", "blk", None),
        P("sect", None),
    )
    out_specs = (P("sect", "blk", None, None), P("sect"), P("sect", "blk", None, None))
    return jax.shard_map(shards, mesh=mesh, in_specs=in_specs, out_specs=out_specs, check_vma=False)
```

profile of v0, /device:TPU:1, one launch (start us, length us, event | category | flops | bytes accessed | tf_op | source)
XLA Modules:
  0.0 448.0 jit_solution(15139575061420545096)
XLA Ops:
  8.9 1.9 fusion.70
  13.7 48.6 %all_gather.15 = f32[64,8,128]{2,1,0:T(8,128)S(1)} all-gather(f32[1,8,128]{2,1,0:T(8,128)} %param.21), channel_id=1, replica_groups=mesh['sect'=64,'blk'=4] {'sect'}, dimensions={0}, use_global_device_ids=true | all-gather | bytes 266240 | tf_op jit(solution)/shard_map/all_gather | solution.py:14
  62.3 4.4 gather_fusion
  66.7 4.7 %broadcast_select_fusion.2 = bf16[128,128,128]{2,1,0:T(8,128)(2,1)} fusion(bf16[128,128,128]{2,1,0:T(8,128)(2,1)} %gather_fusion, pred[128]{0:T(512)(128)(4,1)S(1)} %compare_and_fusion), kind=kLoop, calls=%fused_computation.25 | loop fusion | flops 2097152 | bytes 8388736 | tf_op jit(solution)/shard_map/jit(_take)/select_n | solution.py:89
  71.4 8.8 %fusion.30 = f32[8,128,128]{2,1,0:T(8,128)S(1)} fusion(bf16[1,8,16,128,128]{4,3,2,1,0:T(8,128)(2,1)} %param.20, bf16[8,16,128,128]{3,2,1,0:T(8,128)(2,1)} %bitcast.110, bf16[1,8,16,128,128]{4,3,2,1,0:T(8,128)(2,1)} %param.19), kind=kOutput, calls=%fused_computation.26 | convolution fusion | flops 1075838976 | bytes 13107200 | tf_op jit(solution)/shard_map/jwil,jwml->jim/dot_general | solution.py:94
  80.2 107.2 %all-gather.5.cloned.1.call-done = f32[64,8,128,128]{3,2,1,0:T(8,128)} async-done(((f32[1,8,128,128]{3,2,1,0:T(8,128)}), f32[64,8,128,128]{3,2,1,0:T(8,128)}) %all-gather.5.cloned.1.call-update) | async-done | bytes 33554448 | tf_op jit(solution)/shard_map/all_gather | solution.py:14
  187.4 1.5 while.12
  189.0 1.6 fusion.56
  190.6 9.1 %all-reduce.2 = (f32[]{:T(128)}, f32[]{:T(128)}) all-reduce(f32[]{:T(128)} %get-tuple-element.54, f32[]{:T(128)} %get-tuple-element.53), channel_id=1, replica_groups=mesh['sect'=64,'blk'=4] {'blk'}, use_global_device_ids=true, to_apply=%region_7.9 | all-reduce | flops 2 | bytes 16 | tf_op jit(solution)/shard_map/psum | solution.py:100
  201.9 6.6 %psum.65 = f32[]{:T(128)} all-reduce(f32[]{:T(128)} %get-tuple-element.77), channel_id=1, replica_groups=mesh['sect'=64,'blk'=4] {'blk'}, use_global_device_ids=true, to_apply=%region_11.13 | all-reduce | flops 1 | bytes 8 | tf_op jit(solution)/shard_map/psum | solution.py:105
  210.2 112.8 %all-gather.9.cloned.1.call-done = bf16[32,128,128]{2,1,0:T(8,128)(2,1)} async-done(((bf16[8,128,128]{2,1,0:T(8,128)(2,1)}), bf16[32,128,128]{2,1,0:T(8,128)(2,1)}) %all-gather.9.cloned.1.call-update) | async-done | bytes 1048592 | tf_op jit(solution)/shard_map/all_gather | solution.py:88
  323.0 4.2 gather_fusion.1
  327.3 4.6 %broadcast_select_fusion.1 = bf16[128,128,128]{2,1,0:T(8,128)(2,1)} fusion(bf16[128,128,128]{2,1,0:T(8,128)(2,1)} %gather_fusion.1, pred[128]{0:T(512)(128)(4,1)S(1)} %compare_and_fusion), kind=kLoop, calls=%fused_computation.24 | loop fusion | flops 2097152 | bytes 8388736 | tf_op jit(solution)/shard_map/jit(_take)/select_n | solution.py:89
  331.8 8.7 %fusion.37 = f32[8,128,128]{2,1,0:T(8,128)S(1)} fusion(bf16[1,8,16,128,128]{4,3,2,1,0:T(8,128)(2,1)} %param.20, bf16[8,16,128,128]{3,2,1,0:T(8,128)(2,1)} %bitcast.111, bf16[1,8,16,128,128]{4,3,2,1,0:T(8,128)(2,1)} %param.19), kind=kOutput, calls=%fused_computation.27 | convolution fusion | flops 1075838976 | bytes 13107200 | tf_op jit(solution)/shard_map/jwil,jwml->jim/dot_general | solution.py:94
  341.6 7.9 %all-reduce.1 = (f32[]{:T(128)}, f32[]{:T(128)}) all-reduce(f32[]{:T(128)} %get-tuple-element.52, f32[]{:T(128)} %get-tuple-element.51), channel_id=1, replica_groups=mesh['sect'=64,'blk'=4] {'blk'}, use_global_device_ids=true, to_apply=%region_13.15 | all-reduce | flops 2 | bytes 16 | tf_op jit(solution)/shard_map/psum | solution.py:100
  351.6 6.9 %psum.68 = f32[]{:T(128)} all-reduce(f32[]{:T(128)} %get-tuple-element.75), channel_id=1, replica_groups=mesh['sect'=64,'blk'=4] {'blk'}, use_global_device_ids=true, to_apply=%region_17.19 | all-reduce | flops 1 | bytes 8 | tf_op jit(solution)/shard_map/psum | solution.py:105
  360.0 30.6 %all-gather.11.cloned.1.call-done = bf16[32,128,128]{2,1,0:T(8,128)(2,1)} async-done(((bf16[8,128,128]{2,1,0:T(8,128)(2,1)}), bf16[32,128,128]{2,1,0:T(8,128)(2,1)}) %all-gather.11.cloned.1.call-update) | async-done | bytes 1048592 | tf_op jit(solution)/shard_map/all_gather | solution.py:88
  390.6 4.2 gather_fusion.2
  394.8 4.6 %broadcast_select_fusion = bf16[128,128,128]{2,1,0:T(8,128)(2,1)} fusion(bf16[128,128,128]{2,1,0:T(8,128)(2,1)} %gather_fusion.2, pred[128]{0:T(512)(128)(4,1)S(1)} %compare_and_fusion), kind=kLoop, calls=%fused_computation.23 | loop fusion | flops 2097152 | bytes 8388736 | tf_op jit(solution)/shard_map/jit(_take)/select_n | solution.py:89
  399.4 8.7 %fusion.44 = f32[8,128,128]{2,1,0:T(8,128)S(1)} fusion(bf16[1,8,16,128,128]{4,3,2,1,0:T(8,128)(2,1)} %param.20, bf16[8,16,128,128]{3,2,1,0:T(8,128)(2,1)} %bitcast.109, bf16[1,8,16,128,128]{4,3,2,1,0:T(8,128)(2,1)} %param.19), kind=kOutput, calls=%fused_computation.28 | convolution fusion | flops 1075838976 | bytes 13107200 | tf_op jit(solution)/shard_map/jwil,jwml->jim/dot_general | solution.py:94
  409.1 7.9 %all-reduce = (f32[]{:T(128)}, f32[]{:T(128)}) all-reduce(f32[]{:T(128)} %get-tuple-element.50, f32[]{:T(128)} %get-tuple-element.49), channel_id=1, replica_groups=mesh['sect'=64,'blk'=4] {'blk'}, use_global_device_ids=true, to_apply=%region_19.21 | all-reduce | flops 2 | bytes 16 | tf_op jit(solution)/shard_map/psum | solution.py:100
  419.2 6.9 %psum.71 = f32[]{:T(128)} all-reduce(f32[]{:T(128)} %get-tuple-element.73), channel_id=1, replica_groups=mesh['sect'=64,'blk'=4] {'blk'}, use_global_device_ids=true, to_apply=%region_23.25 | all-reduce | flops 1 | bytes 8 | tf_op jit(solution)/shard_map/psum | solution.py:105
  426.8 7.4 %collective-permute-start = (bf16[8,128,128]{2,1,0:T(8,128)(2,1)S(1)}, bf16[8,128,128]{2,1,0:T(8,128)(2,1)S(1)}, u32[]{:S(2)}, u32[]{:S(2)}) collective-permute-start(bf16[8,128,128]{2,1,0:T(8,128)(2,1)S(1)} %multiply_convert_fusion.1), channel_id=1, source_target_pairs={{4,0},{8,4},{12,8},{16,12},{20,16},{24,20},{28,24},{32,28},{36,32}... | collective-permute-start | bytes 786440 | tf_op jit(solution)/shard_map/ppermute | solution.py:28
  435.0 4.4 collective-permute-done
  (44 shorter events, 14.3 us)
Async XLA Ops:
  7.2 55.2 %all-gather.7.cloned.1.call-start = ((), (), s32[]{:S(2)}) async-start(), calls=%async_computation.1 | async-start | bytes 1310720 | tf_op jit(solution)/shard_map/all_gather | solution.py:88
  10.8 176.6 %all-gather.5.cloned.1.call-start = ((), (), s32[]{:S(2)}) async-start(), calls=%async_computation | async-start | bytes 34078720 | tf_op jit(solution)/shard_map/all_gather | solution.py:14
  11.5 311.5 %all-gather.9.cloned.1.call-start = ((), (), s32[]{:S(2)}) async-start(), calls=%async_computation.2 | async-start | bytes 1310720 | tf_op jit(solution)/shard_map/all_gather | solution.py:88
  187.4 1.6 copy-start.3
  187.4 13.6 %copy-start = (f32[1,8,128,128]{3,2,1,0:T(8,128)S(1)}, f32[1,8,128,128]{3,2,1,0:T(8,128)}, u32[]{:S(2)}) copy-start(f32[1,8,128,128]{3,2,1,0:T(8,128)} %param.23) | copy-start | bytes 1572868
  210.0 180.6 %all-gather.11.cloned.1.call-start = ((), (), s32[]{:S(2)}) async-start(), calls=%async_computation.3 | async-start | bytes 1310720 | tf_op jit(solution)/shard_map/all_gather | solution.py:88
  331.8 8.7 %copy-start.2 = (bf16[8,128,128]{2,1,0:T(8,128)(2,1)S(1)}, bf16[8,128,128]{2,1,0:T(8,128)(2,1)}, u32[]{:S(2)}) copy-start(bf16[8,128,128]{2,1,0:T(8,128)(2,1)} %multiply_convert_fusion.3) | copy-start | bytes 786436
  399.4 8.7 %copy-start.1 = (bf16[8,128,128]{2,1,0:T(8,128)(2,1)S(1)}, bf16[8,128,128]{2,1,0:T(8,128)(2,1)}, u32[]{:S(2)}) copy-start(bf16[8,128,128]{2,1,0:T(8,128)(2,1)} %multiply_convert_fusion.2) | copy-start | bytes 786436
  408.1 26.1 %copy-start.4 = (f32[1,8,128]{2,1,0:T(8,128)S(1)}, f32[1,8,128]{2,1,0:T(8,128)}, u32[]{:S(2)}) copy-start(f32[1,8,128]{2,1,0:T(8,128)} %param.24) | copy-start | bytes 12292
  426.8 12.6 %collective-permute-start = (bf16[8,128,128]{2,1,0:T(8,128)(2,1)S(1)}, bf16[8,128,128]{2,1,0:T(8,128)(2,1)S(1)}, u32[]{:S(2)}, u32[]{:S(2)}) collective-permute-start(bf16[8,128,128]{2,1,0:T(8,128)(2,1)S(1)} %multiply_convert_fusion.1), channel_id=1, source_target_pairs={{4,0},{8,4},{12,8},{16,12},{20,16},{24,20},{28,24},{32,28},{36,32}... | collective-permute-start | bytes 786440 | tf_op jit(solution)/shard_map/ppermute | solution.py:28
Sparse Core Ops, SparseCore 0:
  10.9 29.4 all-gather.6
  43.2 144.1 all-gather.4
  210.1 112.8 all-gather.8
  360.1 30.4 all-gather.10
where the time goes:
time: 452 us; the launch traced here: 448 us
  waiting for transfers between devices  256 us (57%)
  blocking collectives  93.9 us (21%)
  matrix products  30.8 us (7%)
  other arithmetic  24.9 us (6%)
  between operations  21.1 us (5%)
  local copies, waits for them, and re-layouts  13.7 us (3%)
  starting transfers between devices  7.71 us (2%)
    all_gather x3, waiting for transfers between devices, shards(): gathered = lax.all_gather(psi_now, 'blk', axis=0, tiled=True)  143 us
    all_gather x1, waiting for transfers between devices, prefix_2(): gathered = jax.tree.map(lambda a: lax.all_gather(a, axis), part)  107 us
    all_gather x1, blocking collectives, prefix_2(): gathered = jax.tree.map(lambda a: lax.all_gather(a, axis), part)  48.6 us
    dot_general x3, matrix products, shards(): jnp.einsum('jwil,jwml->jim', inner_left, right_now, preferred_element_typ...  26.1 us
    psum x3, blocking collectives, shards(): lax.psum((jnp.sum(current * applied), jnp.sum(current * current)), 'blk')  24.9 us
    psum x3, blocking collectives, shards(): square_sum = lax.psum(jnp.sum(updated * updated), 'blk')  20.4 us
    select_n x4, other arithmetic, shards(): sources = jnp.take(gathered, source_slot, axis=0)  13.8 us
    gather x3, local copies, waits for them, and re-layouts, shards(): sources = jnp.take(gathered, source_slot, axis=0)  12.8 us
  transfers between devices with their start and end apart: 5, of which 4 were waited for; matrix products, arithmetic and copies ran while one was open for 5% of the time, Pallas kernels for 0%

commit v1 on v0

v1 whole, which is shorter than its diff:
```python
import functools

import jax
import jax.numpy as jnp
from jax import lax
from jax.experimental import pallas as pl
from jax.experimental.pallas import tpu as pltpu
from jax.sharding import PartitionSpec as P

STEPS = 3
DAMPING = 0.5
F32 = jnp.float32
BF16 = jnp.bfloat16
VMEM = pltpu.VMEM
SMEM = pltpu.SMEM
LIMIT = 32 * 1024 * 1024


def params(**more):
    return pltpu.CompilerParams(vmem_limit_bytes=LIMIT, **more)


def whole(space=VMEM):
    return pl.BlockSpec(memory_space=space)


def cost(flops, bytes_accessed):
    return pl.CostEstimate(flops=flops, bytes_accessed=bytes_accessed, transcendentals=0)


def start_kernel(psi_ref, precond_ref, out_ref):
    rows = psi_ref.shape[0]
    out_ref[0:rows, :] = psi_ref[...]
    out_ref[rows : 2 * rows, :] = (DAMPING / precond_ref[...]).astype(BF16)


def start_message(psi_guess, precond):
    rows, cap = psi_guess.shape
    return pl.pallas_call(
        start_kernel,
        out_shape=jax.ShapeDtypeStruct((2 * rows, cap), BF16),
        in_specs=[whole(), whole()],
        out_specs=whole(),
        compiler_params=params(),
        cost_estimate=cost(2 * rows * cap, 10 * rows * cap),
        name="start_message",
    )(psi_guess, precond)


def chip_kernel(core_ref, own_h, other_h, own_d, other_d, out_ref, late_t):
    slots, cap = own_d.shape
    chunk = out_ref.shape[1] - 16
    cuts = cap // chunk

    def emit(first_h, second_h, first_d, second_d):
        late_t[...] = jnp.transpose(second_d[...])
        total = first_d[...] * second_d[...]
        high = total.astype(BF16)
        low = (total - high.astype(F32)).astype(BF16)
        row = lax.broadcasted_iota(jnp.int32, (16, cap), 0)
        for j in range(slots):
            columns = late_t[:, j : j + 1]
            both = columns * first_h[j] * second_d[j : j + 1, :] + second_h[j]
            tail = jnp.where(
                row == 0,
                high[j : j + 1, :].astype(F32),
                jnp.where(row == 1, low[j : j + 1, :].astype(F32), 0.0),
            ).astype(BF16)
            for cut in range(cuts):
                out_ref[j * cuts + cut, 0:chunk, :] = both[cut * chunk : (cut + 1) * chunk].astype(BF16)
                out_ref[j * cuts + cut, chunk : chunk + 16, :] = tail

    @pl.when(core_ref[0] == 0)
    def _():
        emit(own_h, other_h, own_d, other_d)

    @pl.when(core_ref[0] != 0)
    def _():
        emit(other_h, own_h, other_d, own_d)


def chip_maps(core, own_h, other_h, own_d, other_d, chips):
    slots, cap = own_d.shape
    chunk = slots * cap // chips
    return pl.pallas_call(
        chip_kernel,
        out_shape=jax.ShapeDtypeStruct((chips, chunk + 16, cap), BF16),
        in_specs=[whole(SMEM)] + [whole()] * 4,
        out_specs=whole(),
        scratch_shapes=[pltpu.VMEM((cap, slots), F32)],
        compiler_params=params(),
        cost_estimate=cost(4 * slots * cap * cap, 12 * slots * cap * cap),
        name="chip_maps",
    )(core, own_h, other_h, own_d, other_d)


def scan_kernel(chip_ref, maps_ref, out_ref, factor, factor_t):
    chips, chunk, cap = out_ref.shape
    cuts = cap // chunk
    for z in range(chips):
        tail = maps_ref[z, chunk : chunk + 16, :].astype(F32)
        factor[z : z + 1, :] = tail[0:1, :] + tail[1:2, :]
    factor_t[...] = jnp.transpose(factor[...])
    first = pl.multiple_of(lax.rem(chip_ref[0], cuts) * chunk, chunk)
    columns = factor_t[pl.ds(first, chunk), :]
    state = jnp.zeros((chunk, cap), F32)
    for z in range(chips):
        out_ref[z] = state.astype(BF16)
        source = maps_ref[z, 0:chunk, :].astype(F32)
        state = columns[:, z : z + 1] * state * factor[z : z + 1, :] + source


def scan_maps(chip, maps):
    chips, rows, cap = maps.shape
    chunk = rows - 16
    return pl.pallas_call(
        scan_kernel,
        out_shape=jax.ShapeDtypeStruct((chips, chunk, cap), BF16),
        in_specs=[whole(SMEM), whole()],
        out_specs=whole(),
        scratch_shapes=[pltpu.VMEM((chips, cap), F32), pltpu.VMEM((cap, chips), F32)],
        compiler_params=params(),
        cost_estimate=cost(4 * chips * chunk * cap, 5 * chips * chunk * cap),
        name="scan_maps",
    )(chip, maps)


def pack_sums(values, cap):
    row = lax.broadcasted_iota(jnp.int32, (16, cap), 0)
    tile = jnp.zeros((16, cap), F32)
    for k, value in enumerate(values):
        rest = jnp.broadcast_to(value, (16, cap))
        for piece in range(3):
            part = rest.astype(BF16).astype(F32)
            tile = jnp.where(row == 3 * k + piece, part, tile)
            rest = rest - part
    return tile.astype(BF16)


def unpack_sums(tile):
    tile = tile.astype(F32)
    return [
        tile[3 * k : 3 * k + 1] + tile[3 * k + 1 : 3 * k + 2] + tile[3 * k + 2 : 3 * k + 3]
        for k in range(5)
    ]


def local_quotient(numerator, overlap):
    return jnp.where(overlap > 0.0, numerator / jnp.where(overlap > 0.0, overlap, 1.0), 0.0)


def paired(values):
    return (values[0] + values[2]) + (values[1] + values[3])


def resolve(tiles, entries):
    sums = [unpack_sums(tile) for tile in tiles]
    rayleigh = paired([s[0] for s in sums]) / paired([s[1] for s in sums])
    deltas = [rayleigh - local_quotient(s[0], s[1]) for s in sums]
    squares = paired(
        [s[2] + delta * (2.0 * s[3] + delta * s[4]) for s, delta in zip(sums, deltas)]
    )
    scale = lax.rsqrt(squares / entries + 1e-06)
    return rayleigh, deltas, scale


def total(x):
    return jnp.sum(jnp.sum(x, axis=0, keepdims=True), axis=1, keepdims=True)


def products(j, me, slot_sector, pair_table, slot_of, left_ref, right_ref, psi_ref, inner):
    slots = psi_ref.shape[0] // 4
    terms, cap = left_ref.shape[1], left_ref.shape[2]
    sector = slot_sector[me * slots + j]
    for w in range(terms):
        source = slot_of[pair_table[sector, w]]
        owner = source // slots
        place = lax.rem(me - owner + 4, 4) * slots + lax.rem(source, slots)
        inner[:, w * cap : (w + 1) * cap] = jnp.dot(
            left_ref[0, w], psi_ref[place], preferred_element_type=F32
        ).astype(BF16)
    result = jnp.zeros((cap, cap), F32)
    for w in range(0, terms, 2):
        pair = jnp.concatenate([right_ref[0, w], right_ref[0, w + 1]], axis=1)
        result = result + lax.dot_general(
            inner[:, w * cap : (w + 2) * cap],
            pair,
            (((1,), (1,)), ((), ())),
            preferred_element_type=F32,
        )
    return result


def invert_slots(slot_sector, slot_of):
    def one(slot, carry):
        slot_of[slot_sector[slot]] = slot
        return carry

    lax.fori_loop(0, slot_sector.shape[0], one, 0)


def support_of(size, cap):
    row = lax.broadcasted_iota(jnp.int32, (cap, cap), 0)
    column = lax.broadcasted_iota(jnp.int32, (cap, cap), 1)
    return (row < size) & (column < size)


def close_step(slots, psi_ref, precond_ref, applied, a_ref, message_ref):
    cap = applied.shape[1]
    zero = jnp.zeros((cap, cap), F32)
    numerator, overlap = zero, zero
    for j in range(slots):
        current = psi_ref[j].astype(F32)
        numerator = numerator + current * applied[j]
        overlap = overlap + current * current
    numerator, overlap = total(numerator), total(overlap)
    quotient = local_quotient(numerator, overlap)
    aa, ab, bb = zero, zero, zero
    for j in range(slots):
        current = psi_ref[j].astype(F32)
        half = DAMPING / precond_ref[j]
        a = current - half * (applied[j] - quotient * current)
        b = half * current
        a_ref[j] = a
        if message_ref.shape[0] > 16:
            message_ref[j * cap : (j + 1) * cap, :] = a.astype(BF16)
        aa = aa + a * a
        ab = ab + a * b
        bb = bb + b * b
    sums = [numerator, overlap, total(aa), total(ab), total(bb)]
    rows = message_ref.shape[0]
    message_ref[rows - 16 : rows, :] = pack_sums(sums, cap)


def first_kernel(
    place_ref,
    slot_sector,
    pair_table,
    sizes,
    own_ref,
    psi_1,
    psi_2,
    psi_3,
    env_ref,
    other_h,
    other_d,
    precond_ref,
    left_ref,
    right_ref,
    psi_ref,
    env_low,
    a_ref,
    message_ref,
    applied,
    inner,
    other_t,
    slot_of,
):
    j = pl.program_id(0)
    slots, cap = applied.shape[0], applied.shape[1]
    me, core = place_ref[0], place_ref[1]

    @pl.when(j == 0)
    def _():
        invert_slots(slot_sector, slot_of)
        other_t[...] = jnp.transpose(other_d[...])
        for k, part in enumerate((own_ref, psi_1, psi_2, psi_3)):
            owner = lax.rem(me - k + 4, 4)
            for i in range(slots):
                size = sizes[0, slot_sector[owner * slots + i]]
                block = part[i * cap : (i + 1) * cap, :].astype(F32)
                psi_ref[k * slots + i] = jnp.where(support_of(size, cap), block, 0.0).astype(BF16)
        for i in range(slots):
            env = env_ref[i].astype(F32)
            further = other_t[:, i : i + 1] * env * other_d[i : i + 1, :] + other_h[i]
            env_low[i] = jnp.where(core == 0, env, further).astype(BF16)

    result = products(j, me, slot_sector, pair_table, slot_of, left_ref, right_ref, psi_ref, inner)
    result = result + jnp.dot(env_low[j], psi_ref[j], preferred_element_type=F32)
    size = sizes[0, slot_sector[me * slots + j]]
    applied[j] = jnp.where(support_of(size, cap), result, 0.0)

    @pl.when(j == slots - 1)
    def _():
        close_step(slots, psi_ref, precond_ref, applied, a_ref, message_ref)


def later_kernel(
    entries,
    place_ref,
    slot_sector,
    pair_table,
    sizes,
    a_own,
    tile_0,
    msg_1,
    msg_2,
    msg_3,
    half_1,
    half_2,
    half_3,
    before,
    env_low,
    precond_ref,
    left_ref,
    right_ref,
    psi_ref,
    a_ref,
    message_ref,
    applied,
    inner,
    slot_of,
):
    j = pl.program_id(0)
    slots, cap = applied.shape[0], applied.shape[1]
    me = place_ref[0]

    @pl.when(j == 0)
    def _():
        invert_slots(slot_sector, slot_of)
        rows = msg_1.shape[0]
        tiles = [tile_0[...]] + [m[rows - 16 : rows, :] for m in (msg_1, msg_2, msg_3)]
        _, deltas, scale = resolve(tiles, entries)
        for i in range(slots):
            b = (DAMPING / precond_ref[i]) * before[i].astype(F32)
            psi_ref[i] = (scale * (a_own[i] + deltas[0] * b)).astype(BF16)
        for k, (message, half) in enumerate(((msg_1, half_1), (msg_2, half_2), (msg_3, half_3)), 1):
            for i in range(slots):
                a = message[i * cap : (i + 1) * cap, :].astype(F32)
                b = half[i * cap : (i + 1) * cap, :].astype(F32) * before[k * slots + i].astype(F32)
                psi_ref[k * slots + i] = (scale * (a + deltas[k] * b)).astype(BF16)

    result = products(j, me, slot_sector, pair_table, slot_of, left_ref, right_ref, psi_ref, inner)
    result = result + jnp.dot(env_low[j], psi_ref[j], preferred_element_type=F32)
    size = sizes[0, slot_sector[me * slots + j]]
    applied[j] = jnp.where(support_of(size, cap), result, 0.0)

    @pl.when(j == slots - 1)
    def _():
        close_step(slots, psi_ref, precond_ref, applied, a_ref, message_ref)


def fixed(shape):
    return pl.BlockSpec(shape, lambda j: (0,) * len(shape))


def step_cost(left):
    slots, terms, cap, _ = left.shape
    return cost(4 * slots * terms * cap**3, 6 * slots * terms * cap * cap)


def first_step(place, slot_sector, pair_table, sizes, own, got, env, other_h, other_d, precond, left, right):
    slots, terms, cap, _ = left.shape
    rows = slots * cap
    ops = pl.BlockSpec((1, terms, cap, cap), lambda j: (j, 0, 0, 0))
    top = fixed((rows, cap))
    return pl.pallas_call(
        first_kernel,
        grid=(slots,),
        out_shape=[
            jax.ShapeDtypeStruct((4 * slots, cap, cap), BF16),
            jax.ShapeDtypeStruct((slots, cap, cap), BF16),
            jax.ShapeDtypeStruct((slots, cap, cap), F32),
            jax.ShapeDtypeStruct((rows + 16, cap), BF16),
        ],
        in_specs=[whole(SMEM)] * 4
        + [top] * 4
        + [fixed(env.shape), fixed(other_h.shape), fixed(other_d.shape), fixed(precond.shape)]
        + [ops, ops],
        out_specs=[
            fixed((4 * slots, cap, cap)),
            fixed((slots, cap, cap)),
            fixed((slots, cap, cap)),
            fixed((rows + 16, cap)),
        ],
        scratch_shapes=[
            pltpu.VMEM((slots, cap, cap), F32),
            pltpu.VMEM((cap, terms * cap), BF16),
            pltpu.VMEM((cap, slots), F32),
            pltpu.SMEM((slot_sector.shape[0],), jnp.int32),
        ],
        compiler_params=params(),
        cost_estimate=step_cost(left),
        name="first_step",
    )(place, slot_sector, pair_table, sizes, own, *got, env, other_h, other_d, precond, left, right)


def later_step(
    place, slot_sector, pair_table, sizes, a_own, tile, messages, halves, before, env, precond, left, right, last
):
    slots, terms, cap, _ = left.shape
    rows = slots * cap
    ops = pl.BlockSpec((1, terms, cap, cap), lambda j: (j, 0, 0, 0))
    bottom = pl.BlockSpec((rows, cap), lambda j: (1, 0))
    out_rows = 16 if last else rows + 16
    return pl.pallas_call(
        functools.partial(later_kernel, float(slot_sector.shape[0] * cap * cap)),
        grid=(slots,),
        out_shape=[
            jax.ShapeDtypeStruct((4 * slots, cap, cap), BF16),
            jax.ShapeDtypeStruct((slots, cap, cap), F32),
            jax.ShapeDtypeStruct((out_rows, cap), BF16),
        ],
        in_specs=[whole(SMEM)] * 4
        + [fixed(a_own.shape), pl.BlockSpec((16, cap), lambda j: (rows // 16, 0))]
        + [fixed((rows + 16, cap))] * 3
        + [bottom] * 3
        + [fixed(before.shape), fixed(env.shape), fixed(precond.shape)]
        + [ops, ops],
        out_specs=[
            fixed((4 * slots, cap, cap)),
            fixed((slots, cap, cap)),
            fixed((out_rows, cap)),
        ],
        scratch_shapes=[
            pltpu.VMEM((slots, cap, cap), F32),
            pltpu.VMEM((cap, terms * cap), BF16),
            pltpu.SMEM((slot_sector.shape[0],), jnp.int32),
        ],
        compiler_params=params(),
        cost_estimate=step_cost(left),
        name="last_step" if last else "later_step",
    )(place, slot_sector, pair_table, sizes, a_own, tile, *messages, *halves, before, env, precond, left, right)


def ground_kernel(entries, tile_0, tile_1, tile_2, tile_3, a_ref, psi_ref, precond_ref, ground_ref, energy_ref):
    tiles = [t[...] for t in (tile_0, tile_1, tile_2, tile_3)]
    rayleigh, deltas, scale = resolve(tiles, entries)
    energy_ref[0] = rayleigh[0, 0]
    for j in range(a_ref.shape[0]):
        b = (DAMPING / precond_ref[j]) * psi_ref[j].astype(F32)
        ground_ref[j] = (scale * (a_ref[j] + deltas[0] * b)).astype(BF16)


def ground_state(tiles, a_own, psi, precond, entries):
    slots, cap, _ = a_own.shape
    block = fixed((slots, cap, cap))
    return pl.pallas_call(
        functools.partial(ground_kernel, entries),
        grid=(1,),
        out_shape=[
            jax.ShapeDtypeStruct((slots, cap, cap), BF16),
            jax.ShapeDtypeStruct((1,), F32),
        ],
        in_specs=[fixed((16, cap))] * 4 + [block, block, block],
        out_specs=[block, whole(SMEM)],
        compiler_params=params(),
        cost_estimate=cost(4 * slots * cap * cap, 12 * slots * cap * cap),
        name="ground_state",
    )(*tiles, a_own, psi, precond)


def merge_kernel(place_ref, slot_sector, ranks, ground_ref, next_ref, inv_sv, out_ref):
    slots, cap, _ = ground_ref.shape
    lane = lax.broadcasted_iota(jnp.int32, (1, cap), 1)
    live = place_ref[2] != 0
    for j in range(slots):
        rank = ranks[0, slot_sector[place_ref[0] * slots + j]]
        weight = jnp.where(lane < rank, inv_sv[j : j + 1, :] / cap, 0.0)
        scaled = (ground_ref[j].astype(F32) * weight).astype(BF16)
        merged = jnp.dot(scaled, next_ref[j], preferred_element_type=F32)
        out_ref[j] = jnp.where(live, merged, 0.0).astype(BF16)


def merge(place, slot_sector, ranks, ground, following, inv_sv):
    slots, cap, _ = ground.shape
    return pl.pallas_call(
        merge_kernel,
        out_shape=jax.ShapeDtypeStruct((slots, cap, cap), BF16),
        in_specs=[whole(SMEM)] * 3 + [whole()] * 3,
        out_specs=whole(),
        compiler_params=params(),
        cost_estimate=cost(2 * slots * cap**3, 6 * slots * cap * cap),
        name="merge",
    )(place, slot_sector, ranks, ground, following, inv_sv)


def around(value, shift):
    count = lax.axis_size("blk")
    return lax.ppermute(value, "blk", [(i, (i + shift) % count) for i in range(count)])


def three(value):
    return [around(value, shift) for shift in (1, 2, 3)]


def shards(
    psi_guess,
    sector_sizes,
    slot_sector,
    pair_table,
    left_ops,
    right_ops,
    decay,
    source_h,
    precond,
    inv_sv,
    ranks,
):
    sections = lax.axis_size("sect")
    chips = sections // 2
    slots, cap = psi_guess.shape[1], psi_guess.shape[2]
    rows = slots * cap
    entries = float(slot_sector.shape[0] * cap * cap)
    section = lax.axis_index("sect")
    place = jnp.stack(
        [lax.axis_index("blk"), section % 2, (section < sections - 1).astype(jnp.int32), section // 2]
    )
    chip, core = place[3:4], place[1:2]
    left, right = left_ops[0], right_ops[0]

    swap = [(i, i ^ 1) for i in range(sections)]
    other_h = lax.ppermute(source_h[0], "sect", swap)
    other_d = lax.ppermute(decay[0], "sect", swap)

    own_start = start_message(psi_guess.reshape(rows, cap), precond.reshape(rows, cap))
    got_start = three(own_start)

    maps = chip_maps(core, source_h[0], other_h, decay[0], other_d, chips)
    groups = [[2 * q + c for q in range(chips)] for c in range(2)]
    maps = lax.all_to_all(maps, "sect", 0, 0, tiled=True, axis_index_groups=groups)
    env = scan_maps(chip, maps)
    env = lax.all_to_all(env, "sect", 0, 0, tiled=True, axis_index_groups=groups)
    env = env.reshape(slots, cap, cap)

    psi, env_low, a_own, message = first_step(
        place, slot_sector, pair_table, sector_sizes, own_start, got_start, env, other_h, other_d, precond[0], left, right
    )
    for step in range(1, STEPS):
        got = three(message)
        psi, a_own, message = later_step(
            place,
            slot_sector,
            pair_table,
            sector_sizes,
            a_own,
            message,
            got,
            got_start,
            psi,
            env_low,
            precond[0],
            left,
            right,
            step == STEPS - 1,
        )
    tiles = [message] + three(message)
    ground, energies = ground_state(tiles, a_own, psi, precond[0], entries)
    following = lax.ppermute(ground, "sect", [(i + 1, i) for i in range(sections - 1)])
    merged = merge(place, slot_sector, ranks, ground, following, inv_sv[0])
    return (ground[None], energies, merged[None])


def solution(mesh):
    in_specs = (
        P("sect", "blk", None, None),
        P("sect", None),
        P(),
        P(),
        P("sect", "blk", None, None, None),
        P("sect", "blk", None, None, None),
        P("sect", "blk", None),
        P("sect", "blk", None, None),
        P("sect", "blk", None, None),
        P("sect", "blk", None),
        P("sect", None),
    )
    out_specs = (P("sect", "blk", None, None), P("sect"), P("sect", "blk", None, None))
    return jax.shard_map(shards, mesh=mesh, in_specs=in_specs, out_specs=out_specs, check_vma=False)
```

time: 452 us -> 125 us (0.28)
  waiting for transfers between devices: 256 us -> 54.8 us
  blocking collectives: 93.9 us -> 0 us
  matrix products: 30.8 us -> 0 us
  starting transfers between devices: 7.71 us -> 34.1 us
  other arithmetic: 24.9 us -> 0.08 us
  Pallas kernels: 0 us -> 24.1 us
  between operations: 21.1 us -> 0.79 us
    all_gather x4 -> x0, waiting for transfers between devices: 251 us -> none  [the longest x3 143 us: shards(): gathered = lax.all_gather(psi_now, 'blk', axis=0, tiled=True)]
    all_gather x1 -> x0, blocking collectives: 48.6 us -> none  [prefix_2(): gathered = jax.tree.map(lambda a: lax.all_gather(a, axis), part)]
    psum x6 -> x0, blocking collectives: 45.3 us -> none  [the longest x3 24.9 us: shards(): lax.psum((jnp.sum(current * applied), jnp.sum(current * current)), 'blk')]
    ppermute x1 -> x15, waiting for transfers between devices: 4.37 us -> 49 us  [the longest x12 39.9 us: around(): lax.ppermute(value, 'blk', [(i, (i + shift) % count) for i in range(count)])]
    dot_general x7 -> x0, matrix products: 30.8 us -> none  [the longest x3 26.1 us: shards(): jnp.einsum('jwil,jwml->jim', inner_left, right_now, preferred_element_typ...]
    pallas_call x0 -> x8, Pallas kernels: none -> 24.1 us  [the longest x2 13.3 us: later_step(): pl.pallas_call(functools.partial(later_kernel, float(slot_sector.shape[0]...]
    all_to_all x0 -> x2, starting transfers between devices: none -> 16.9 us  [the longest x1 9.3 us: shards(): lax.all_to_all(maps, 'sect', 0, 0, tiled=True, axis_index_groups=groups)]
    select_n x4 -> x0, other arithmetic: 13.8 us -> none  [shards(): sources = jnp.take(gathered, source_slot, axis=0)]
  transfers between devices with their start and end apart: 5 -> 17, of which waited for: 4 -> 13; matrix products, arithmetic and copies ran while one was open for 5% -> 1% of each run, Pallas kernels for 0% -> 0%
where the time goes in v1:
time: 125 us; the launch traced here: 124 us
  waiting for transfers between devices  54.8 us (44%)
  starting transfers between devices  34.1 us (27%)
  Pallas kernels  24.1 us (19%)
  local copies, waits for them, and re-layouts  10.5 us (8%)
    ppermute x12, waiting for transfers between devices, around(): lax.ppermute(value, 'blk', [(i, (i + shift) % count) for i in range(count)])  39.9 us
    pallas_call x2, Pallas kernels, later_step(): pl.pallas_call(functools.partial(later_kernel, float(slot_sector.shape[0]...  13.3 us
    unnamed x31, local copies, waits for them, and re-layouts  10.5 us
    ppermute x12, starting transfers between devices, around(): lax.ppermute(value, 'blk', [(i, (i + shift) % count) for i in range(count)])  9.4 us
    all_to_all x1, starting transfers between devices, shards(): lax.all_to_all(maps, 'sect', 0, 0, tiled=True, axis_index_groups=groups)  9.3 us
    all_to_all x1, starting transfers between devices, shards(): lax.all_to_all(env, 'sect', 0, 0, tiled=True, axis_index_groups=groups)  7.6 us
    ppermute x1, waiting for transfers between devices, shards(): lax.ppermute(ground, 'sect', [(i + 1, i) for i in range(sections - 1)])  7.47 us
    pallas_call x1, Pallas kernels, first_step(): pl.pallas_call(first_kernel, grid=(slots,), out_shape=[jax.ShapeDtypeStru...  6.82 us
  transfers between devices with their start and end apart: 17, of which 13 were waited for; matrix products, arithmetic and copies ran while one was open for 1% of the time, Pallas kernels for 0%

profile of v1, /device:TPU:1, one launch (start us, length us, event | category | flops | bytes accessed | tf_op | source)
XLA Modules:
  0.0 124.5 jit_solution(10951054502923707906)
XLA Ops:
  0.6 3.3 %collective-permute-start.3 = (f32[8,128,128]{2,1,0:T(8,128)}, f32[8,128,128]{2,1,0:T(8,128)S(1)}, u32[]{:S(2)}, u32[]{:S(2)}) collective-permute-start(f32[8,128,128]{2,1,0:T(8,128)} %bitcast.27), channel_id=1, source_target_pairs={{0,4},{4,0},{8,12},{12,8},{16,20},{20,16},{24,28},{28,24},{32,36},... | collective-permute-start | bytes 1572872 | tf_op jit(solution)/shard_map/ppermute | solution.py:513
  4.1 1.7 %collective-permute-done.4.other_d = f32[8,128]{1,0:T(8,128)S(1)} collective-permute-done((f32[8,128]{1,0:T(8,128)}, f32[8,128]{1,0:T(8,128)S(1)}, u32[]{:S(2)}, u32[]{:S(2)}) %collective-permute-start.4) | collective-permute-done | bytes 4128 | tf_op jit(solution)/shard_map/ppermute | solution.py:514
  8.6 9.3 %all-to-all-start = ((bf16[32,48,128]{2,1,0:T(8,128)(2,1)}), bf16[32,48,128]{2,1,0:T(8,128)(2,1)S(1)}, u32[]{:S(2)}, u32[]{:S(2)}) async-start(bf16[32,48,128]{2,1,0:T(8,128)(2,1)} %chip_maps.1), calls=%async_computation | async-start | bytes 786432 | tf_op jit(solution)/shard_map/all_to_all | solution.py:521
  20.0 2.8 %collective-permute-start.2 = (bf16[2048,128]{1,0:T(8,128)(2,1)S(1)}, bf16[2048,128]{1,0:T(8,128)(2,1)S(1)}, u32[]{:S(2)}, u32[]{:S(2)}) collective-permute-start(bf16[2048,128]{1,0:T(8,128)(2,1)S(1)} %start_message.1.own_ref), channel_id=1, source_target_pairs={{0,3},{1,0},{2,1},{3,2},{4,7},{5,4},{6,5},{7,6},{8,11},{9,8},{10,9... | collective-permute-start | bytes 1572872 | tf_op jit(solution)/shard_map/ppermute | solution.py:480
  23.8 5.8 %all-to-all-done.maps_ref = bf16[32,48,128]{2,1,0:T(8,128)(2,1)S(1)} async-done(((bf16[32,48,128]{2,1,0:T(8,128)(2,1)}), bf16[32,48,128]{2,1,0:T(8,128)(2,1)S(1)}, u32[]{:S(2)}, u32[]{:S(2)}) %all-to-all-start) | async-done | bytes 393248 | tf_op jit(solution)/shard_map/all_to_all | solution.py:521
  30.7 7.6 %all-to-all-start.1 = ((bf16[32,32,128]{2,1,0:T(8,128)(2,1)}), bf16[32,32,128]{2,1,0:T(8,128)(2,1)S(1)}, u32[]{:S(2)}, u32[]{:S(2)}) async-start(bf16[32,32,128]{2,1,0:T(8,128)(2,1)} %copy-done.6), calls=%async_computation.1 | async-start | bytes 524288 | tf_op jit(solution)/shard_map/all_to_all | solution.py:523
  39.2 10.2 %collective-permute-done.psi_1.half_1 = bf16[2048,128]{1,0:T(8,128)(2,1)S(1)} collective-permute-done((bf16[2048,128]{1,0:T(8,128)(2,1)S(1)}, bf16[2048,128]{1,0:T(8,128)(2,1)S(1)}, u32[]{:S(2)}, u32[]{:S(2)}) %collective-permute-start) | collective-permute-done | bytes 524320 | tf_op jit(solution)/shard_map/ppermute | solution.py:480
  49.4 2.2 %copy-done = bf16[1,8,16,128,128]{4,3,2,1,0:T(8,128)(2,1)S(1)} copy-done((bf16[1,8,16,128,128]{4,3,2,1,0:T(8,128)(2,1)S(1)}, bf16[1,8,16,128,128]{4,3,2,1,0:T(8,128)(2,1)}, u32[]{:S(2)}) %copy-start) | copy-done | bytes 4194328
  51.6 2.2 %copy-done.2 = bf16[1,8,16,128,128]{4,3,2,1,0:T(8,128)(2,1)S(1)} copy-done((bf16[1,8,16,128,128]{4,3,2,1,0:T(8,128)(2,1)S(1)}, bf16[1,8,16,128,128]{4,3,2,1,0:T(8,128)(2,1)}, u32[]{:S(2)}) %copy-start.2) | copy-done | bytes 4194328
  53.8 6.8 %first_step.1 = (bf16[32,128,128]{2,1,0:T(8,128)(2,1)S(1)}, bf16[8,128,128]{2,1,0:T(8,128)(2,1)S(1)}, f32[8,128,128]{2,1,0:T(8,128)S(1)}, bf16[1040,128]{1,0:T(8,128)(2,1)S(1)}) custom-call(s32[4]{0:T(128)S(1)} %pad_add_fusion.place_ref, s32[32]{0:T(128)S(1)} %copy-done.10, s32[32,16]{1,0:T(8,128)S(1)} %copy.16.pair_table, s32[1,32]{1,0:T(1,128)S(1)} %copy-done.11, ...), custom_call_target="tpu_custom_call" | custom-call | flops 1073741824 | bytes 12582912 | tf_op jit(solution)/shard_map/first_step/pallas_call | solution.py:357
  60.6 1.4 %collective-permute-start.7 = (bf16[1040,128]{1,0:T(8,128)(2,1)S(1)}, bf16[1040,128]{1,0:T(8,128)(2,1)S(1)}, u32[]{:S(2)}, u32[]{:S(2)}) collective-permute-start(bf16[1040,128]{1,0:T(8,128)(2,1)S(1)} %get-tuple-element.16.tile_0), channel_id=1, source_target_pairs={{0,3},{1,0},{2,1},{3,2},{4,7},{5,4},{6,5},{7,6},{8,11},{9,8},{10,9... | collective-permute-start | bytes 798728 | tf_op jit(solution)/shard_map/ppermute | solution.py:480
  63.1 3.2 %collective-permute-done.7.msg_3 = bf16[1040,128]{1,0:T(8,128)(2,1)S(1)} collective-permute-done((bf16[1040,128]{1,0:T(8,128)(2,1)S(1)}, bf16[1040,128]{1,0:T(8,128)(2,1)S(1)}, u32[]{:S(2)}, u32[]{:S(2)}) %collective-permute-start.7) | collective-permute-done | bytes 266272 | tf_op jit(solution)/shard_map/ppermute | solution.py:480
  66.3 2.6 %collective-permute-done.6.msg_2 = bf16[1040,128]{1,0:T(8,128)(2,1)S(1)} collective-permute-done((bf16[1040,128]{1,0:T(8,128)(2,1)S(1)}, bf16[1040,128]{1,0:T(8,128)(2,1)S(1)}, u32[]{:S(2)}, u32[]{:S(2)}) %collective-permute-start.6) | collective-permute-done | bytes 266272 | tf_op jit(solution)/shard_map/ppermute | solution.py:480
  68.9 7.0 %collective-permute-done.5.msg_1 = bf16[1040,128]{1,0:T(8,128)(2,1)S(1)} collective-permute-done((bf16[1040,128]{1,0:T(8,128)(2,1)S(1)}, bf16[1040,128]{1,0:T(8,128)(2,1)S(1)}, u32[]{:S(2)}, u32[]{:S(2)}) %collective-permute-start.5) | collective-permute-done | bytes 266272 | tf_op jit(solution)/shard_map/ppermute | solution.py:480
  75.9 6.6 %later_step.1 = (bf16[32,128,128]{2,1,0:T(8,128)(2,1)S(1)}, f32[8,128,128]{2,1,0:T(8,128)S(1)}, bf16[1040,128]{1,0:T(8,128)(2,1)S(1)}) custom-call(s32[4]{0:T(128)S(1)} %pad_add_fusion.place_ref, s32[32]{0:T(128)S(1)} %copy-done.10, s32[32,16]{1,0:T(8,128)S(1)} %copy.16.pair_table, s32[1,32]{1,0:T(1,128)S(1)} %copy-done.11, ...), custom_call_target="tpu_custom_call" | custom-call | flops 1073741824 | bytes 12582912 | tf_op jit(solution)/shard_map/later_step/pallas_call | solution.py:396
  82.7 1.4 %collective-permute-start.8 = (bf16[1040,128]{1,0:T(8,128)(2,1)S(1)}, bf16[1040,128]{1,0:T(8,128)(2,1)S(1)}, u32[]{:S(2)}, u32[]{:S(2)}) collective-permute-start(bf16[1040,128]{1,0:T(8,128)(2,1)S(1)} %get-tuple-element.20.tile_0), channel_id=1, source_target_pairs={{0,1},{1,2},{2,3},{3,0},{4,5},{5,6},{6,7},{7,4},{8,9},{9,10},{10,1... | collective-permute-start | bytes 798728 | tf_op jit(solution)/shard_map/ppermute | solution.py:480
  84.0 4.2 %collective-permute-done.10.msg_3 = bf16[1040,128]{1,0:T(8,128)(2,1)S(1)} collective-permute-done((bf16[1040,128]{1,0:T(8,128)(2,1)S(1)}, bf16[1040,128]{1,0:T(8,128)(2,1)S(1)}, u32[]{:S(2)}, u32[]{:S(2)}) %collective-permute-start.10) | collective-permute-done | bytes 266272 | tf_op jit(solution)/shard_map/ppermute | solution.py:480
  89.6 8.1 %collective-permute-done.8.msg_1 = bf16[1040,128]{1,0:T(8,128)(2,1)S(1)} collective-permute-done((bf16[1040,128]{1,0:T(8,128)(2,1)S(1)}, bf16[1040,128]{1,0:T(8,128)(2,1)S(1)}, u32[]{:S(2)}, u32[]{:S(2)}) %collective-permute-start.8) | collective-permute-done | bytes 266272 | tf_op jit(solution)/shard_map/ppermute | solution.py:480
  97.6 6.7 %last_step.1 = (bf16[32,128,128]{2,1,0:T(8,128)(2,1)S(1)}, f32[8,128,128]{2,1,0:T(8,128)S(1)}, bf16[16,128]{1,0:T(8,128)(2,1)S(1)}) custom-call(s32[4]{0:T(128)S(1)} %pad_add_fusion.place_ref, s32[32]{0:T(128)S(1)} %copy-done.10, s32[32,16]{1,0:T(8,128)S(1)} %copy.16.pair_table, s32[1,32]{1,0:T(1,128)S(1)} %copy-done.11, ...), custom_call_target="tpu_custom_call" | custom-call | flops 1073741824 | bytes 12582912 | tf_op jit(solution)/shard_map/last_step/pallas_call | solution.py:396
  104.5 1.4 %collective-permute-start.11 = (bf16[16,128]{1,0:T(8,128)(2,1)S(1)}, bf16[16,128]{1,0:T(8,128)(2,1)S(1)}, u32[]{:S(2)}, u32[]{:S(2)}) collective-permute-start(bf16[16,128]{1,0:T(8,128)(2,1)S(1)} %get-tuple-element.22.tile_0), channel_id=1, source_target_pairs={{0,1},{1,2},{2,3},{3,0},{4,5},{5,6},{6,7},{7,4},{8,9},{9,10},{10,1... | collective-permute-start | bytes 12296 | tf_op jit(solution)/shard_map/ppermute | solution.py:480
  106.8 1.6 %collective-permute-done.12.tile_2 = bf16[16,128]{1,0:T(8,128)(2,1)S(1)} collective-permute-done((bf16[16,128]{1,0:T(8,128)(2,1)S(1)}, bf16[16,128]{1,0:T(8,128)(2,1)S(1)}, u32[]{:S(2)}, u32[]{:S(2)}) %collective-permute-start.12) | collective-permute-done | bytes 4128 | tf_op jit(solution)/shard_map/ppermute | solution.py:480
  110.1 4.4 %collective-permute-start.14 = (bf16[8,128,128]{2,1,0:T(8,128)(2,1)}, bf16[8,128,128]{2,1,0:T(8,128)(2,1)S(1)}, u32[]{:S(2)}, u32[]{:S(2)}) collective-permute-start(bf16[8,128,128]{2,1,0:T(8,128)(2,1)} %get-tuple-element.25.ground_ref), channel_id=1, source_target_pairs={{4,0},{8,4},{12,8},{16,12},{20,16},{24,20},{28,24},{32,28},{36,32}... | collective-permute-start | bytes 786440 | tf_op jit(solution)/shard_map/ppermute | solution.py:549
  114.5 7.5 %collective-permute-done.14.next_ref = bf16[8,128,128]{2,1,0:T(8,128)(2,1)S(1)} collective-permute-done((bf16[8,128,128]{2,1,0:T(8,128)(2,1)}, bf16[8,128,128]{2,1,0:T(8,128)(2,1)S(1)}, u32[]{:S(2)}, u32[]{:S(2)}) %collective-permute-start.14) | collective-permute-done | bytes 262176 | tf_op jit(solution)/shard_map/ppermute | solution.py:549
  123.0 1.5 %merge.1 = bf16[8,128,128]{2,1,0:T(8,128)(2,1)} custom-call(s32[4]{0:T(128)S(1)} %pad_add_fusion.place_ref, s32[32]{0:T(128)S(1)} %copy-done.10, s32[1,32]{1,0:T(1,128)S(1)} %copy-done.14, bf16[8,128,128]{2,1,0:T(8,128)(2,1)S(1)} %copy-done.9, bf16[8,128,128]{2,1,0:T(8,128)(2,1)S(1)} %collective-permute-done.14.next_ref, f32[8,128]{1,0:T(8,128)S(1)} %bitcast.33), custom_call_target="tpu_custom_call" | custom-call | flops 33554432 | bytes 786432 | tf_op jit(solution)/shard_map/merge/pallas_call | solution.py:467
  (50 shorter events, 14.3 us)
Async XLA Ops:
  0.6 48.7 %copy-start.5 = (f32[1,8,128,128]{3,2,1,0:T(8,128)S(1)}, f32[1,8,128,128]{3,2,1,0:T(8,128)}, u32[]{:S(2)}) copy-start(f32[1,8,128,128]{3,2,1,0:T(8,128)} %param.19) | copy-start | bytes 1572868
  0.6 5.1 %collective-permute-start.3 = (f32[8,128,128]{2,1,0:T(8,128)}, f32[8,128,128]{2,1,0:T(8,128)S(1)}, u32[]{:S(2)}, u32[]{:S(2)}) collective-permute-start(f32[8,128,128]{2,1,0:T(8,128)} %bitcast.27), channel_id=1, source_target_pairs={{0,4},{4,0},{8,12},{12,8},{16,20},{20,16},{24,28},{28,24},{32,36},... | collective-permute-start | bytes 1572872 | tf_op jit(solution)/shard_map/ppermute | solution.py:513
  4.0 1.8 %collective-permute-start.4 = (f32[8,128]{1,0:T(8,128)}, f32[8,128]{1,0:T(8,128)S(1)}, u32[]{:S(2)}, u32[]{:S(2)}) collective-permute-start(f32[8,128]{1,0:T(8,128)} %bitcast.31), channel_id=1, source_target_pairs={{0,4},{4,0},{8,12},{12,8},{16,20},{20,16},{24,28},{28,24},{32,36},... | collective-permute-start | bytes 12296 | tf_op jit(solution)/shard_map/ppermute | solution.py:514
  7.5 41.9 %copy-start.10 = (s32[32]{0:T(128)S(1)}, s32[32]{0:T(128)}, u32[]{:S(2)}) copy-start(s32[32]{0:T(128)} %slot_sector.7) | copy-start | bytes 388
  7.5 41.9 %copy-start.11 = (s32[1,32]{1,0:T(1,128)S(1)}, s32[1,32]{1,0:T(1,128)}, u32[]{:S(2)}) copy-start(s32[1,32]{1,0:T(1,128)} %sizes.5) | copy-start | bytes 388
  8.6 21.1 %all-to-all-start = ((bf16[32,48,128]{2,1,0:T(8,128)(2,1)}), bf16[32,48,128]{2,1,0:T(8,128)(2,1)S(1)}, u32[]{:S(2)}, u32[]{:S(2)}) async-start(bf16[32,48,128]{2,1,0:T(8,128)(2,1)} %chip_maps.1), calls=%async_computation | async-start | bytes 786432 | tf_op jit(solution)/shard_map/all_to_all | solution.py:521
  20.0 19.2 %collective-permute-start.2 = (bf16[2048,128]{1,0:T(8,128)(2,1)S(1)}, bf16[2048,128]{1,0:T(8,128)(2,1)S(1)}, u32[]{:S(2)}, u32[]{:S(2)}) collective-permute-start(bf16[2048,128]{1,0:T(8,128)(2,1)S(1)} %start_message.1.own_ref), channel_id=1, source_target_pairs={{0,3},{1,0},{2,1},{3,2},{4,7},{5,4},{6,5},{7,6},{8,11},{9,8},{10,9... | collective-permute-start | bytes 1572872 | tf_op jit(solution)/shard_map/ppermute | solution.py:480
  22.8 16.4 %collective-permute-start.1 = (bf16[2048,128]{1,0:T(8,128)(2,1)S(1)}, bf16[2048,128]{1,0:T(8,128)(2,1)S(1)}, u32[]{:S(2)}, u32[]{:S(2)}) collective-permute-start(bf16[2048,128]{1,0:T(8,128)(2,1)S(1)} %start_message.1.own_ref), channel_id=1, source_target_pairs={{0,2},{1,3},{2,0},{3,1},{4,6},{5,7},{6,4},{7,5},{8,10},{9,11},{10,... | collective-permute-start | bytes 1572872 | tf_op jit(solution)/shard_map/ppermute | solution.py:480
  23.1 26.2 %collective-permute-start = (bf16[2048,128]{1,0:T(8,128)(2,1)S(1)}, bf16[2048,128]{1,0:T(8,128)(2,1)S(1)}, u32[]{:S(2)}, u32[]{:S(2)}) collective-permute-start(bf16[2048,128]{1,0:T(8,128)(2,1)S(1)} %start_message.1.own_ref), channel_id=1, source_target_pairs={{0,1},{1,2},{2,3},{3,0},{4,5},{5,6},{6,7},{7,4},{8,9},{9,10},{10,1... | collective-permute-start | bytes 1572872 | tf_op jit(solution)/shard_map/ppermute | solution.py:480
  30.7 18.6 %all-to-all-start.1 = ((bf16[32,32,128]{2,1,0:T(8,128)(2,1)}), bf16[32,32,128]{2,1,0:T(8,128)(2,1)S(1)}, u32[]{:S(2)}, u32[]{:S(2)}) async-start(bf16[32,32,128]{2,1,0:T(8,128)(2,1)} %copy-done.6), calls=%async_computation.1 | async-start | bytes 524288 | tf_op jit(solution)/shard_map/all_to_all | solution.py:523
  53.8 22.1 %copy-start.1 = (bf16[1,8,16,128,128]{4,3,2,1,0:T(8,128)(2,1)S(1)}, bf16[1,8,16,128,128]{4,3,2,1,0:T(8,128)(2,1)}, u32[]{:S(2)}) copy-start(bf16[1,8,16,128,128]{4,3,2,1,0:T(8,128)(2,1)} %param.15) | copy-start | bytes 12582916
  53.8 22.1 %copy-start.3 = (bf16[1,8,16,128,128]{4,3,2,1,0:T(8,128)(2,1)S(1)}, bf16[1,8,16,128,128]{4,3,2,1,0:T(8,128)(2,1)}, u32[]{:S(2)}) copy-start(bf16[1,8,16,128,128]{4,3,2,1,0:T(8,128)(2,1)} %param.16) | copy-start | bytes 12582916
  60.6 5.7 %collective-permute-start.7 = (bf16[1040,128]{1,0:T(8,128)(2,1)S(1)}, bf16[1040,128]{1,0:T(8,128)(2,1)S(1)}, u32[]{:S(2)}, u32[]{:S(2)}) collective-permute-start(bf16[1040,128]{1,0:T(8,128)(2,1)S(1)} %get-tuple-element.16.tile_0), channel_id=1, source_target_pairs={{0,3},{1,0},{2,1},{3,2},{4,7},{5,4},{6,5},{7,6},{8,11},{9,8},{10,9... | collective-permute-start | bytes 798728 | tf_op jit(solution)/shard_map/ppermute | solution.py:480
  62.0 6.9 %collective-permute-start.6 = (bf16[1040,128]{1,0:T(8,128)(2,1)S(1)}, bf16[1040,128]{1,0:T(8,128)(2,1)S(1)}, u32[]{:S(2)}, u32[]{:S(2)}) collective-permute-start(bf16[1040,128]{1,0:T(8,128)(2,1)S(1)} %get-tuple-element.16.tile_0), channel_id=1, source_target_pairs={{0,2},{1,3},{2,0},{3,1},{4,6},{5,7},{6,4},{7,5},{8,10},{9,11},{10,... | collective-permute-start | bytes 798728 | tf_op jit(solution)/shard_map/ppermute | solution.py:480
  62.4 13.5 %collective-permute-start.5 = (bf16[1040,128]{1,0:T(8,128)(2,1)S(1)}, bf16[1040,128]{1,0:T(8,128)(2,1)S(1)}, u32[]{:S(2)}, u32[]{:S(2)}) collective-permute-start(bf16[1040,128]{1,0:T(8,128)(2,1)S(1)} %get-tuple-element.16.tile_0), channel_id=1, source_target_pairs={{0,1},{1,2},{2,3},{3,0},{4,5},{5,6},{6,7},{7,4},{8,9},{9,10},{10,1... | collective-permute-start | bytes 798728 | tf_op jit(solution)/shard_map/ppermute | solution.py:480
  82.5 5.8 %collective-permute-start.10 = (bf16[1040,128]{1,0:T(8,128)(2,1)S(1)}, bf16[1040,128]{1,0:T(8,128)(2,1)S(1)}, u32[]{:S(2)}, u32[]{:S(2)}) collective-permute-start(bf16[1040,128]{1,0:T(8,128)(2,1)S(1)} %get-tuple-element.20.tile_0), channel_id=1, source_target_pairs={{0,3},{1,0},{2,1},{3,2},{4,7},{5,4},{6,5},{7,6},{8,11},{9,8},{10,9... | collective-permute-start | bytes 798728 | tf_op jit(solution)/shard_map/ppermute | solution.py:480
  82.6 7.0 %collective-permute-start.9 = (bf16[1040,128]{1,0:T(8,128)(2,1)S(1)}, bf16[1040,128]{1,0:T(8,128)(2,1)S(1)}, u32[]{:S(2)}, u32[]{:S(2)}) collective-permute-start(bf16[1040,128]{1,0:T(8,128)(2,1)S(1)} %get-tuple-element.20.tile_0), channel_id=1, source_target_pairs={{0,2},{1,3},{2,0},{3,1},{4,6},{5,7},{6,4},{7,5},{8,10},{9,11},{10,... | collective-permute-start | bytes 798728 | tf_op jit(solution)/shard_map/ppermute | solution.py:480
  82.7 14.9 %collective-permute-start.8 = (bf16[1040,128]{1,0:T(8,128)(2,1)S(1)}, bf16[1040,128]{1,0:T(8,128)(2,1)S(1)}, u32[]{:S(2)}, u32[]{:S(2)}) collective-permute-start(bf16[1040,128]{1,0:T(8,128)(2,1)S(1)} %get-tuple-element.20.tile_0), channel_id=1, source_target_pairs={{0,1},{1,2},{2,3},{3,0},{4,5},{5,6},{6,7},{7,4},{8,9},{9,10},{10,1... | collective-permute-start | bytes 798728 | tf_op jit(solution)/shard_map/ppermute | solution.py:480
  97.6 24.4 %copy-start.13 = (f32[1,8,128]{2,1,0:T(8,128)S(1)}, f32[1,8,128]{2,1,0:T(8,128)}, u32[]{:S(2)}) copy-start(f32[1,8,128]{2,1,0:T(8,128)} %param.20) | copy-start | bytes 12292
  97.6 24.4 %copy-start.14 = (s32[1,32]{1,0:T(1,128)S(1)}, s32[1,32]{1,0:T(1,128)}, u32[]{:S(2)}) copy-start(s32[1,32]{1,0:T(1,128)} %ranks.1) | copy-start | bytes 388
  104.3 2.5 %collective-permute-start.13 = (bf16[16,128]{1,0:T(8,128)(2,1)S(1)}, bf16[16,128]{1,0:T(8,128)(2,1)S(1)}, u32[]{:S(2)}, u32[]{:S(2)}) collective-permute-start(bf16[16,128]{1,0:T(8,128)(2,1)S(1)} %get-tuple-element.22.tile_0), channel_id=1, source_target_pairs={{0,3},{1,0},{2,1},{3,2},{4,7},{5,4},{6,5},{7,6},{8,11},{9,8},{10,9... | collective-permute-start | bytes 12296 | tf_op jit(solution)/shard_map/ppermute | solution.py:480
  104.4 4.0 %collective-permute-start.12 = (bf16[16,128]{1,0:T(8,128)(2,1)S(1)}, bf16[16,128]{1,0:T(8,128)(2,1)S(1)}, u32[]{:S(2)}, u32[]{:S(2)}) collective-permute-start(bf16[16,128]{1,0:T(8,128)(2,1)S(1)} %get-tuple-element.22.tile_0), channel_id=1, source_target_pairs={{0,2},{1,3},{2,0},{3,1},{4,6},{5,7},{6,4},{7,5},{8,10},{9,11},{10,... | collective-permute-start | bytes 12296 | tf_op jit(solution)/shard_map/ppermute | solution.py:480
  104.5 4.7 %collective-permute-start.11 = (bf16[16,128]{1,0:T(8,128)(2,1)S(1)}, bf16[16,128]{1,0:T(8,128)(2,1)S(1)}, u32[]{:S(2)}, u32[]{:S(2)}) collective-permute-start(bf16[16,128]{1,0:T(8,128)(2,1)S(1)} %get-tuple-element.22.tile_0), channel_id=1, source_target_pairs={{0,1},{1,2},{2,3},{3,0},{4,5},{5,6},{6,7},{7,4},{8,9},{9,10},{10,1... | collective-permute-start | bytes 12296 | tf_op jit(solution)/shard_map/ppermute | solution.py:480
  110.1 11.9 %collective-permute-start.14 = (bf16[8,128,128]{2,1,0:T(8,128)(2,1)}, bf16[8,128,128]{2,1,0:T(8,128)(2,1)S(1)}, u32[]{:S(2)}, u32[]{:S(2)}) collective-permute-start(bf16[8,128,128]{2,1,0:T(8,128)(2,1)} %get-tuple-element.25.ground_ref), channel_id=1, source_target_pairs={{4,0},{8,4},{12,8},{16,12},{20,16},{24,20},{28,24},{32,28},{36,32}... | collective-permute-start | bytes 786440 | tf_op jit(solution)/shard_map/ppermute | solution.py:549
  (8 other events, 9.8 us)

commit v2 on v1

v2 whole, which is shorter than its diff:
```python
import functools

import jax
import jax.numpy as jnp
from jax import lax
from jax.experimental import pallas as pl
from jax.experimental.pallas import tpu as pltpu
from jax.sharding import PartitionSpec as P

STEPS = 3
DAMPING = 0.5
F32 = jnp.float32
BF16 = jnp.bfloat16
VMEM = pltpu.VMEM
SMEM = pltpu.SMEM
HBM = pltpu.HBM
LIMIT = 20 * 1024 * 1024
SIZES, RANKS, CORE, SOURCES = 0, 64, 96, 128


def params(**more):
    return pltpu.CompilerParams(vmem_limit_bytes=LIMIT, **more)


def whole(space=VMEM):
    return pl.BlockSpec(memory_space=space)


def in_hbm(value):
    return pltpu.with_memory_space_constraint(value, HBM)


def cost(flops, bytes_accessed):
    return pl.CostEstimate(flops=flops, bytes_accessed=bytes_accessed, transcendentals=0)


def start_kernel(
    slot_hbm,
    pair_hbm,
    sizes_hbm,
    ranks_hbm,
    psi_hbm,
    plan,
    out_ref,
    slot_sector,
    pair_table,
    sizes,
    ranks,
    slot_of,
    psi_ref,
    sem,
):
    terms, sectors = pair_table.shape
    slots, cap, _ = out_ref.shape
    me = lax.axis_index("blk")
    moves = (
        (slot_hbm, slot_sector),
        (pair_hbm, pair_table),
        (sizes_hbm, sizes),
        (ranks_hbm, ranks),
        (psi_hbm, psi_ref),
    )
    fetches = [pltpu.make_async_copy(a, b, sem.at[k]) for k, (a, b) in enumerate(moves)]
    for fetch in fetches:
        fetch.start()
    for fetch in fetches:
        fetch.wait()
    plan[CORE] = lax.axis_index("sect") & 1
    for j in range(slots):
        sector = slot_sector[me * slots + j]
        size = sizes[0, sector]
        plan[SIZES + j] = size
        plan[RANKS + j] = ranks[0, sector]
        block = jnp.where(support_of(size, cap), psi_ref[j].astype(F32), 0.0)
        out_ref[j] = block.astype(BF16)
    for slot in range(sectors):
        slot_of[slot_sector[slot]] = slot

    def tables(j, carry):
        sector = slot_sector[me * slots + j]
        for w in range(terms):
            source = slot_of[pair_table[w, sector]]
            plan[SOURCES + j * terms + w] = ((me * slots - (source & -slots)) & (3 * slots)) | (
                source & (slots - 1)
            )
        return carry

    lax.fori_loop(0, slots, tables, 0)


def start(slot_sector, pair_table, sizes, ranks, psi):
    pairs = pair_table.T
    terms = pairs.shape[0]
    slots = psi.shape[0]
    tables = (slot_sector, pairs, sizes, ranks)
    return pl.pallas_call(
        start_kernel,
        out_shape=[
            jax.ShapeDtypeStruct((SOURCES + slots * terms,), jnp.int32),
            jax.ShapeDtypeStruct(psi.shape, BF16),
        ],
        in_specs=[whole(HBM)] * 5,
        out_specs=[whole(SMEM), whole()],
        scratch_shapes=[pltpu.SMEM(t.shape, jnp.int32) for t in tables]
        + [
            pltpu.SMEM(slot_sector.shape, jnp.int32),
            pltpu.VMEM(psi.shape, BF16),
            pltpu.SemaphoreType.DMA((5,)),
        ],
        compiler_params=params(),
        cost_estimate=cost(4 * psi.size, 4 * psi.size),
        name="start",
    )(*[in_hbm(t) for t in tables], in_hbm(psi))


def half_kernel(precond_hbm, out_ref, half_ref, precond_ref, sem):
    slots = precond_ref.shape[0]
    fetches = [
        pltpu.make_async_copy(precond_hbm.at[j], precond_ref.at[j], sem.at[j]) for j in range(slots)
    ]
    for fetch in fetches:
        fetch.start()
    for j in range(slots):
        fetches[j].wait()
        half = DAMPING / precond_ref[j]
        half_ref[j] = half
        out_ref[j] = half.astype(BF16)


def half_message(precond):
    slots, cap, _ = precond.shape
    return pl.pallas_call(
        half_kernel,
        out_shape=[
            jax.ShapeDtypeStruct((slots, cap, cap), BF16),
            jax.ShapeDtypeStruct((slots, cap, cap), F32),
        ],
        in_specs=[whole(HBM)],
        out_specs=[whole(), whole()],
        scratch_shapes=[pltpu.VMEM(precond.shape, F32), pltpu.SemaphoreType.DMA((slots,))],
        compiler_params=params(),
        cost_estimate=cost(2 * slots * cap * cap, 100 * slots * cap * cap),
        name="half_message",
    )(in_hbm(precond))


def chip_kernel(plan, own_hbm, other_h, own_d_hbm, other_d, out_ref, late_t, own_h, own_d, h_sem, d_sem):
    slots, cap = own_d.shape
    mine = slots // 2
    chips, rows, _ = out_ref.shape
    chunk = rows - 8
    cuts = cap // chunk
    core_here = plan[CORE]
    first = core_here * mine
    fetch_d = pltpu.make_async_copy(own_d_hbm, own_d, d_sem)
    fetch_d.start()
    fetches = [
        pltpu.make_async_copy(own_hbm.at[first + j], own_h.at[j], h_sem.at[j]) for j in range(mine)
    ]
    for fetch in fetches:
        fetch.start()
    fetch_d.wait()
    row = lax.broadcasted_iota(jnp.int32, (8, cap), 0)

    def emit(core):
        early_d, late_d = (own_d, other_d) if core == 0 else (other_d, own_d)
        late_t[...] = jnp.transpose(late_d[...])
        whole_d = early_d[...] * late_d[...]
        high = whole_d.astype(BF16).astype(F32)
        low = whole_d - high
        for j in range(mine):
            k = core * mine + j
            tail = jnp.where(
                row == 0, high[k : k + 1, :], jnp.where(row == 1, low[k : k + 1, :], 0.0)
            )
            fetches[j].wait()
            early_h, late_h = (own_h[j], other_h[k]) if core == 0 else (other_h[k], own_h[j])
            both = late_t[:, k : k + 1] * early_h * late_d[k : k + 1, :] + late_h
            for cut in range(cuts):
                part = jnp.concatenate([both[cut * chunk : (cut + 1) * chunk], tail], axis=0)
                out_ref[j * cuts + cut] = part.astype(BF16)

    @pl.when(core_here == 0)
    def _():
        emit(0)

    @pl.when(core_here != 0)
    def _():
        emit(1)


def chip_maps(plan, own_h, other_h, own_d, other_d, chips):
    slots, cap = own_d.shape
    chunk = slots // 2 * cap // chips
    return pl.pallas_call(
        chip_kernel,
        out_shape=jax.ShapeDtypeStruct((chips, chunk + 8, cap), BF16),
        in_specs=[whole(SMEM), whole(HBM), whole(), whole(HBM), whole()],
        out_specs=whole(),
        scratch_shapes=[
            pltpu.VMEM((cap, slots), F32),
            pltpu.VMEM((slots // 2, cap, cap), F32),
            pltpu.VMEM((slots, cap), F32),
            pltpu.SemaphoreType.DMA((slots // 2,)),
            pltpu.SemaphoreType.DMA,
        ],
        compiler_params=params(),
        cost_estimate=cost(2 * slots * cap * cap, 6 * slots * cap * cap),
        name="chip_maps",
    )(plan, in_hbm(own_h), other_h, in_hbm(own_d), other_d)


def scan_kernel(maps_ref, out_ref, factor, factor_t):
    chips, chunk, cap = out_ref.shape
    cuts = cap // chunk
    for z in range(chips):
        tail = maps_ref[z].astype(F32)[chunk : chunk + 8]
        factor[z : z + 1, :] = tail[0:1, :] + tail[1:2, :]
    factor_t[...] = jnp.transpose(factor[...])
    first = pl.multiple_of(lax.rem(lax.axis_index("sect") // 2, cuts) * chunk, chunk)
    columns = factor_t[pl.ds(first, chunk), :]
    state = jnp.zeros((chunk, cap), F32)
    for z in range(chips):
        out_ref[z] = state.astype(BF16)
        source = maps_ref[z].astype(F32)[0:chunk]
        state = columns[:, z : z + 1] * state * factor[z : z + 1, :] + source


def scan_maps(maps):
    chips, rows, cap = maps.shape
    chunk = rows - 8
    return pl.pallas_call(
        scan_kernel,
        out_shape=jax.ShapeDtypeStruct((chips, chunk, cap), BF16),
        in_specs=[whole()],
        out_specs=whole(),
        scratch_shapes=[pltpu.VMEM((chips, cap), F32), pltpu.VMEM((cap, chips), F32)],
        compiler_params=params(),
        cost_estimate=cost(4 * chips * chunk * cap, 200 * chips * chunk * cap),
        name="scan_maps",
    )(maps)


def pack_sums(values, cap):
    row = lax.broadcasted_iota(jnp.int32, (16, cap), 0)
    tile = jnp.zeros((16, cap), F32)
    for k, value in enumerate(values):
        rest = jnp.broadcast_to(value, (16, cap))
        for piece in range(3):
            part = rest.astype(BF16).astype(F32)
            tile = jnp.where(row == 3 * k + piece, part, tile)
            rest = rest - part
    return tile.astype(BF16)


def unpack_sums(tile):
    tile = tile.astype(F32)
    return [
        tile[3 * k : 3 * k + 1] + tile[3 * k + 1 : 3 * k + 2] + tile[3 * k + 2 : 3 * k + 3]
        for k in range(5)
    ]


def local_quotient(numerator, overlap):
    return jnp.where(overlap > 0.0, numerator / jnp.where(overlap > 0.0, overlap, 1.0), 0.0)


def paired(values):
    return (values[0] + values[2]) + (values[1] + values[3])


def resolve(tiles, entries):
    sums = [unpack_sums(tile) for tile in tiles]
    rayleigh = paired([s[0] for s in sums]) / paired([s[1] for s in sums])
    deltas = [rayleigh - local_quotient(s[0], s[1]) for s in sums]
    squares = paired(
        [s[2] + delta * (2.0 * s[3] + delta * s[4]) for s, delta in zip(sums, deltas)]
    )
    scale = lax.rsqrt(squares / entries + 1e-06)
    return rayleigh, deltas, scale


def total(x):
    return jnp.sum(jnp.sum(x, axis=0, keepdims=True), axis=1, keepdims=True)


AHEAD = 3


def fetch_ops(j, left_hbm, right_hbm, left_ref, right_ref, ops_sem):
    pltpu.make_async_copy(left_hbm.at[j], left_ref.at[j], ops_sem.at[0, j]).start()
    pltpu.make_async_copy(right_hbm.at[j], right_ref.at[j], ops_sem.at[1, j]).start()


def fetch_first_ops(*refs):
    for j in range(AHEAD):
        fetch_ops(j, *refs)


def ops_scratch(left, *more):
    return [
        pltpu.VMEM(left.shape, BF16),
        pltpu.VMEM(left.shape, BF16),
        *more,
        pltpu.SemaphoreType.DMA((2, left.shape[0])),
    ]


def products(
    j, plan, left_hbm, right_hbm, left_ref, right_ref, ops_sem, psi_ref, inner
):
    pltpu.make_async_copy(left_hbm.at[j], left_ref.at[j], ops_sem.at[0, j]).wait()
    pltpu.make_async_copy(right_hbm.at[j], right_ref.at[j], ops_sem.at[1, j]).wait()

    @pl.when(j + AHEAD < left_ref.shape[0])
    def _():
        fetch_ops(j + AHEAD, left_hbm, right_hbm, left_ref, right_ref, ops_sem)

    terms, cap = left_ref.shape[1], left_ref.shape[2]
    for w in range(terms):
        inner[:, w * cap : (w + 1) * cap] = jnp.dot(
            left_ref[j, w], psi_ref[plan[SOURCES + j * terms + w]], preferred_element_type=F32
        ).astype(BF16)
    result = jnp.zeros((cap, cap), F32)
    for w in range(0, terms, 2):
        pair = jnp.concatenate([right_ref[j, w], right_ref[j, w + 1]], axis=1)
        result = result + lax.dot_general(
            inner[:, w * cap : (w + 2) * cap],
            pair,
            (((1,), (1,)), ((), ())),
            preferred_element_type=F32,
        )
    return result


def support_of(size, cap):
    row = lax.broadcasted_iota(jnp.int32, (cap, cap), 0)
    column = lax.broadcasted_iota(jnp.int32, (cap, cap), 1)
    return (row < size) & (column < size)


def close_step(slots, psi_ref, half_ref, applied, a_ref, message_ref):
    cap = applied.shape[1]
    zero = jnp.zeros((cap, cap), F32)
    numerator, overlap = zero, zero
    for j in range(slots):
        current = psi_ref[j].astype(F32)
        numerator = numerator + current * applied[j]
        overlap = overlap + current * current
    numerator, overlap = total(numerator), total(overlap)
    quotient = local_quotient(numerator, overlap)
    aa, ab, bb = zero, zero, zero
    for j in range(slots):
        current = psi_ref[j].astype(F32)
        half = half_ref[j]
        a = current - half * (applied[j] - quotient * current)
        b = half * current
        a_ref[j] = a
        if message_ref.shape[0] > 16:
            message_ref[j * cap : (j + 1) * cap, :] = a.astype(BF16)
        aa = aa + a * a
        ab = ab + a * b
        bb = bb + b * b
    sums = [numerator, overlap, total(aa), total(ab), total(bb)]
    rows = message_ref.shape[0]
    message_ref[rows - 16 : rows, :] = pack_sums(sums, cap)


def first_kernel(
    plan,
    psi_0,
    psi_1,
    psi_2,
    psi_3,
    left_hbm,
    right_hbm,
    psi_ref,
    ops_ref,
    inner,
    left_ref,
    right_ref,
    psi_sem,
    ops_sem,
):
    slots, cap = ops_ref.shape[0], ops_ref.shape[1]
    fetches = []
    for k, part in enumerate((psi_0, psi_1, psi_2, psi_3)):
        target = psi_ref.at[pl.ds(k * slots, slots)]
        fetches.append(pltpu.make_async_copy(part, target, psi_sem.at[k]))
    for fetch in fetches:
        fetch.start()
    for fetch in fetches:
        fetch.wait()
    fetch_first_ops(left_hbm, right_hbm, left_ref, right_ref, ops_sem)

    def one(j, carry):
        ops_ref[j] = products(
            j,
            plan,
            left_hbm,
            right_hbm,
            left_ref,
            right_ref,
            ops_sem,
            psi_ref,
            inner,
        )
        return carry

    lax.fori_loop(0, slots, one, 0)


def close_kernel(
    plan,
    psi_ref,
    ops_ref,
    env_own,
    env_got,
    other_h,
    other_d,
    half_ref,
    env_low,
    a_ref,
    message_ref,
    applied,
    other_t,
):
    slots, cap = ops_ref.shape[0], ops_ref.shape[1]
    core = plan[CORE]
    other_t[...] = jnp.transpose(other_d[...])
    for j in range(slots):
        mine = slots // 2
        own, got = env_own[j % mine], env_got[j % mine]
        env = jnp.where(core == j // mine, own.astype(F32), got.astype(F32))
        further = other_t[:, j : j + 1] * env * other_d[j : j + 1, :] + other_h[j]
        env = jnp.where(core == 0, env, further).astype(BF16)
        env_low[j] = env
        result = ops_ref[j] + jnp.dot(env, psi_ref[j], preferred_element_type=F32)
        applied[j] = jnp.where(support_of(plan[SIZES + j], cap), result, 0.0)
    close_step(slots, psi_ref, half_ref, applied, a_ref, message_ref)


def later_kernel(
    entries,
    plan,
    a_own,
    msg_0,
    msg_1,
    msg_2,
    msg_3,
    half_1,
    half_2,
    half_3,
    before,
    env_low,
    half_ref,
    left_hbm,
    right_hbm,
    psi_ref,
    a_ref,
    message_ref,
    applied,
    inner,
    left_ref,
    right_ref,
    ops_sem,
):
    slots, cap = applied.shape[0], applied.shape[1]
    fetch_first_ops(left_hbm, right_hbm, left_ref, right_ref, ops_sem)
    rows = msg_1.shape[0]
    tiles = [m[rows - 16 : rows, :] for m in (msg_0, msg_1, msg_2, msg_3)]
    _, deltas, scale = resolve(tiles, entries)
    for i in range(slots):
        b = half_ref[i] * before[i].astype(F32)
        psi_ref[i] = (scale * (a_own[i] + deltas[0] * b)).astype(BF16)
    for k, (message, half) in enumerate(((msg_1, half_1), (msg_2, half_2), (msg_3, half_3)), 1):
        for i in range(slots):
            a = message[i * cap : (i + 1) * cap, :].astype(F32)
            b = half[i].astype(F32) * before[k * slots + i].astype(F32)
            psi_ref[k * slots + i] = (scale * (a + deltas[k] * b)).astype(BF16)

    def one(j, carry):
        result = products(
            j,
            plan,
            left_hbm,
            right_hbm,
            left_ref,
            right_ref,
            ops_sem,
            psi_ref,
            inner,
        )
        result = result + jnp.dot(env_low[j], psi_ref[j], preferred_element_type=F32)
        applied[j] = jnp.where(support_of(plan[SIZES + j], cap), result, 0.0)
        return carry

    lax.fori_loop(0, slots, one, 0)
    close_step(slots, psi_ref, half_ref, applied, a_ref, message_ref)


def step_cost(left):
    slots, terms, cap, _ = left.shape
    return cost(4 * slots * terms * cap**3, 12 * slots * terms * cap * cap)


def first_products(plan, psi, left, right):
    slots, terms, cap, _ = left.shape
    return pl.pallas_call(
        first_kernel,
        out_shape=[
            jax.ShapeDtypeStruct((4 * slots, cap, cap), BF16),
            jax.ShapeDtypeStruct((slots, cap, cap), F32),
        ],
        in_specs=[whole(SMEM)] + [whole(HBM)] * 6,
        out_specs=[whole()] * 2,
        scratch_shapes=[
            pltpu.VMEM((cap, terms * cap), BF16),
            *ops_scratch(left, pltpu.SemaphoreType.DMA((4,))),
        ],
        compiler_params=params(),
        cost_estimate=cost(cap**3, slots * cap * cap),
        name="first_products",
    )(plan, *[in_hbm(p) for p in psi], in_hbm(left), in_hbm(right))


def first_close(plan, psi, ops, env_own, env_got, other_h, other_d, half):
    slots, cap, _ = ops.shape
    return pl.pallas_call(
        close_kernel,
        out_shape=[
            jax.ShapeDtypeStruct((slots, cap, cap), BF16),
            jax.ShapeDtypeStruct((slots, cap, cap), F32),
            jax.ShapeDtypeStruct((slots * cap + 16, cap), BF16),
        ],
        in_specs=[whole(SMEM)] + [whole()] * 7,
        out_specs=[whole()] * 3,
        scratch_shapes=[
            pltpu.VMEM((slots, cap, cap), F32),
            pltpu.VMEM((cap, slots), F32),
        ],
        compiler_params=params(),
        cost_estimate=cost(2 * slots * cap**3, 20 * slots * cap * cap),
        name="first_close",
    )(plan, psi, ops, env_own, env_got, other_h, other_d, half)


def later_step(
    plan, entries, a_own, message, got, halves, before, env, half, left, right, last
):
    slots, terms, cap, _ = left.shape
    out_rows = 16 if last else slots * cap + 16
    return pl.pallas_call(
        functools.partial(later_kernel, entries),
        out_shape=[
            jax.ShapeDtypeStruct((4 * slots, cap, cap), BF16),
            jax.ShapeDtypeStruct((slots, cap, cap), F32),
            jax.ShapeDtypeStruct((out_rows, cap), BF16),
        ],
        in_specs=[whole(SMEM)] + [whole()] * 11 + [whole(HBM)] * 2,
        out_specs=[whole()] * 3,
        scratch_shapes=[
            pltpu.VMEM((slots, cap, cap), F32),
            pltpu.VMEM((cap, terms * cap), BF16),
            *ops_scratch(left),
        ],
        compiler_params=params(),
        cost_estimate=step_cost(left),
        name="last_step" if last else "later_step",
    )(plan, a_own, message, *got, *halves, before, env, half, in_hbm(left), in_hbm(right))


def ground_kernel(
    entries,
    plan,
    tile_0,
    tile_1,
    tile_2,
    tile_3,
    a_ref,
    psi_ref,
    half_ref,
    inv_sv,
    ground_ref,
    scaled_ref,
    energy_ref,
):
    slots, cap = a_ref.shape[0], a_ref.shape[1]
    lane = lax.broadcasted_iota(jnp.int32, (1, cap), 1)
    tiles = [t[...] for t in (tile_0, tile_1, tile_2, tile_3)]
    rayleigh, deltas, scale = resolve(tiles, entries)
    energy_ref[0] = rayleigh[0, 0]
    for j in range(slots):
        b = half_ref[j] * psi_ref[j].astype(F32)
        ground = (scale * (a_ref[j] + deltas[0] * b)).astype(BF16)
        ground_ref[j] = ground
        weight = jnp.where(lane < plan[RANKS + j], inv_sv[j : j + 1, :] / cap, 0.0)
        scaled_ref[j] = (ground.astype(F32) * weight).astype(BF16)


def ground_state(plan, tiles, a_own, psi, half, inv_sv, entries):
    slots, cap, _ = a_own.shape
    return pl.pallas_call(
        functools.partial(ground_kernel, entries),
        out_shape=[
            jax.ShapeDtypeStruct((slots, cap, cap), BF16),
            jax.ShapeDtypeStruct((slots, cap, cap), BF16),
            jax.ShapeDtypeStruct((1,), F32),
        ],
        in_specs=[whole(SMEM)] + [whole()] * 8,
        out_specs=[whole(), whole(), whole(SMEM)],
        compiler_params=params(),
        cost_estimate=cost(4 * slots * cap * cap, 12 * slots * cap * cap),
        name="ground_state",
    )(plan, *tiles, a_own, psi, half, inv_sv)


def merge_kernel(scaled_ref, next_ref, out_ref):
    live = lax.axis_index("sect") < lax.axis_size("sect") - 1
    for j in range(scaled_ref.shape[0]):
        merged = jnp.dot(scaled_ref[j], next_ref[j], preferred_element_type=F32)
        out_ref[j] = jnp.where(live, merged, 0.0).astype(BF16)


def merge(scaled, following):
    slots, cap, _ = scaled.shape
    return pl.pallas_call(
        merge_kernel,
        out_shape=jax.ShapeDtypeStruct((slots, cap, cap), BF16),
        in_specs=[whole()] * 2,
        out_specs=whole(),
        compiler_params=params(),
        cost_estimate=cost(2 * slots * cap**3, 6 * slots * cap * cap),
        name="merge",
    )(scaled, following)


def around(value, shift):
    count = lax.axis_size("blk")
    return lax.ppermute(value, "blk", [(i, (i + shift) % count) for i in range(count)])


def three(value):
    return [around(value, shift) for shift in (1, 2, 3)]


def shards(
    psi_guess,
    sector_sizes,
    slot_sector,
    pair_table,
    left_ops,
    right_ops,
    decay,
    source_h,
    precond,
    inv_sv,
    ranks,
):
    sections = lax.axis_size("sect")
    chips = sections // 2
    slots, cap = psi_guess.shape[1], psi_guess.shape[2]
    entries = float(slot_sector.shape[0] * cap * cap)
    left, right = left_ops[0], right_ops[0]

    swap = [(i, i ^ 1) for i in range(sections)]
    other_h = lax.ppermute(source_h[0], "sect", swap)
    other_d = lax.ppermute(decay[0], "sect", swap)
    plan, own_psi = start(slot_sector, pair_table, sector_sizes, ranks, psi_guess[0])
    maps = chip_maps(plan, source_h[0], other_h, decay[0], other_d, chips)
    groups = [[2 * q + c for q in range(chips)] for c in range(2)]
    got_maps = lax.all_to_all(maps, "sect", 0, 0, tiled=True, axis_index_groups=groups)
    own_psi, late_precond, _ = lax.optimization_barrier((own_psi, precond[0], maps))
    got_psi = three(own_psi)
    own_half, half = half_message(late_precond)
    halves = three(own_half)
    got_maps, own_half = lax.optimization_barrier((got_maps, own_half))
    env = scan_maps(got_maps)
    got_env = lax.all_to_all(env, "sect", 0, 0, tiled=True, axis_index_groups=groups)
    env_own = got_env.reshape(slots // 2, cap, cap)
    psi, ops = first_products(plan, [own_psi] + got_psi, left, right)
    env_own, ops, halves[1:] = lax.optimization_barrier((env_own, ops, halves[1:]))
    env_got = lax.ppermute(env_own, "sect", swap)
    env_low, a_own, message = first_close(
        plan, psi, ops, env_own, env_got, other_h, other_d, half
    )
    message, halves[0] = lax.optimization_barrier((message, halves[0]))
    for step in range(1, STEPS):
        psi, a_own, message = later_step(
            plan,
            entries,
            a_own,
            message,
            three(message),
            halves,
            psi,
            env_low,
            half,
            left,
            right,
            step == STEPS - 1,
        )
    tiles = [message] + three(message)
    ground, scaled, energies = ground_state(
        plan, tiles, a_own, psi, half, inv_sv[0], entries
    )
    following = lax.ppermute(ground, "sect", [(i + 1, i) for i in range(sections - 1)])
    merged = merge(scaled, following)
    return (ground[None], energies, merged[None])


def solution(mesh):
    in_specs = (
        P("sect", "blk", None, None),
        P("sect", None),
        P(),
        P(),
        P("sect", "blk", None, None, None),
        P("sect", "blk", None, None, None),
        P("sect", "blk", None),
        P("sect", "blk", None, None),
        P("sect", "blk", None, None),
        P("sect", "blk", None),
        P("sect", None),
    )
    out_specs = (P("sect", "blk", None, None), P("sect"), P("sect", "blk", None, None))
    return jax.shard_map(shards, mesh=mesh, in_specs=in_specs, out_specs=out_specs, check_vma=False)
```

time: 125 us -> 115 us (0.920)
  waiting for transfers between devices: 54.8 us -> 38.3 us
  local copies, waits for them, and re-layouts: 10.5 us -> 0.76 us
  starting transfers between devices: 34.1 us -> 43.4 us
  Pallas kernels: 24.1 us -> 31.5 us
    unnamed x31 -> x8, local copies, waits for them, and re-layouts: 10.5 us -> 0.76 us
    ppermute x12 -> x15, waiting for transfers between devices: 39.9 us -> 30.7 us  [around(): lax.ppermute(value, 'blk', [(i, (i + shift) % count) for i in range(count)])]
    pallas_call x5 -> x7, Pallas kernels: 21.1 us -> 27.1 us  [the longest x2 13.1 us: later_step(): pl.pallas_call(functools.partial(later_kernel, entries), out_shape=[jax.S...]
    all_to_all x1, waiting for transfers between devices: 5.8 us -> 0.23 us  [shards(): lax.all_to_all(maps, 'sect', 0, 0, tiled=True, axis_index_groups=groups)]
    ppermute x12 -> x15, starting transfers between devices: 9.4 us -> 13.7 us  [around(): lax.ppermute(value, 'blk', [(i, (i + shift) % count) for i in range(count)])]
    ppermute x0 -> x1, starting transfers between devices: none -> 3.82 us  [shards(): env_got = lax.ppermute(env_own, 'sect', swap)]
    ppermute x1, waiting for transfers between devices: 7.47 us -> 5.26 us  [shards(): lax.ppermute(ground, 'sect', [(i + 1, i) for i in range(sections - 1)])]
    ppermute x1, waiting for transfers between devices: 1.65 us -> 0.01 us  [shards(): other_d = lax.ppermute(decay[0], 'sect', swap)]
  transfers between devices with their start and end apart: 17 -> 21, of which waited for: 13 -> 13; matrix products, arithmetic and copies ran while one was open for 1% -> 0% of each run, Pallas kernels for 0% -> 12%
where the time goes in v2:
time: 115 us
  starting transfers between devices  43.4 us (38%)
  waiting for transfers between devices  38.3 us (33%)
  Pallas kernels  31.5 us (27%)
    ppermute x15, waiting for transfers between devices, around(): lax.ppermute(value, 'blk', [(i, (i + shift) % count) for i in range(count)])  30.7 us
    ppermute x15, starting transfers between devices, around(): lax.ppermute(value, 'blk', [(i, (i + shift) % count) for i in range(count)])  13.7 us
    pallas_call x2, Pallas kernels, later_step(): pl.pallas_call(functools.partial(later_kernel, entries), out_shape=[jax.S...  13.1 us
    all_to_all x1, starting transfers between devices, shards(): lax.all_to_all(maps, 'sect', 0, 0, tiled=True, axis_index_groups=groups)  9.31 us
    all_to_all x1, starting transfers between devices, shards(): lax.all_to_all(env, 'sect', 0, 0, tiled=True, axis_index_groups=groups)  9 us
    pallas_call x1, Pallas kernels, first_products(): pl.pallas_call(first_kernel, out_shape=[jax.ShapeDtypeStruct((4 * slots,...  7.14 us
    ppermute x1, waiting for transfers between devices, shards(): lax.ppermute(ground, 'sect', [(i + 1, i) for i in range(sections - 1)])  5.26 us
    ppermute x1, starting transfers between devices, shards(): lax.ppermute(ground, 'sect', [(i + 1, i) for i in range(sections - 1)])  4.17 us
  transfers between devices with their start and end apart: 21, of which 13 were waited for; matrix products, arithmetic and copies ran while one was open for 0% of the time, Pallas kernels for 12%

profile of v2, /device:TPU:1, one launch (start us, length us, event | category | flops | bytes accessed | tf_op | source)
XLA Modules:
  0.0 114.8 jit_solution(16272228411785013142)
XLA Ops:
  0.6 3.3 %collective-permute-start = (f32[8,128,128]{2,1,0:T(8,128)}, f32[8,128,128]{2,1,0:T(8,128)S(1)}, u32[]{:S(2)}, u32[]{:S(2)}) collective-permute-start(f32[8,128,128]{2,1,0:T(8,128)} %bitcast.20), channel_id=1, source_target_pairs={{0,4},{4,0},{8,12},{12,8},{16,20},{20,16},{24,28},{28,24},{32,36},... | collective-permute-start | bytes 1572872 | tf_op jit(solution)/shard_map/ppermute | solution.py:667
  4.1 2.1 %start.1 = (s32[256]{0:T(256)S(1)}, bf16[8,128,128]{2,1,0:T(8,128)(2,1)S(1)}) custom-call(s32[32]{0:T(128)} %slot_hbm.1, s32[16,32]{1,0:T(8,128)} %bitcast.25, s32[1,32]{1,0:T(1,128)} %sizes_hbm.1, s32[1,32]{1,0:T(1,128)} %ranks_hbm.1, bf16[8,128,128]{2,1,0:T(8,128)(2,1)} %bitcast.24), custom_call_target="tpu_custom_call" | custom-call | flops 524288 | bytes 524288 | tf_op jit(solution)/shard_map/start/pallas_call | solution.py:96
  6.2 2.5 %chip_maps.1 = bf16[32,24,128]{2,1,0:T(8,128)(2,1)} custom-call(s32[256]{0:T(256)S(1)} %get-tuple-element.30.plan, f32[8,128,128]{2,1,0:T(8,128)} %bitcast.21, f32[8,128,128]{2,1,0:T(8,128)S(1)} %collective-permute-done.other_h, f32[8,128]{1,0:T(8,128)} %bitcast.27, f32[8,128]{1,0:T(8,128)S(1)} %collective-permute-done.1.other_d), custom_call_target="tpu_custom_call" | custom-call | flops 262144 | bytes 786432 | tf_op jit(solution)/shard_map/chip_maps/pallas_call | solution.py:195
  8.7 9.3 %all-to-all-start = ((bf16[32,24,128]{2,1,0:T(8,128)(2,1)}), bf16[32,24,128]{2,1,0:T(8,128)(2,1)S(1)}, u32[]{:S(2)}, u32[]{:S(2)}) async-start(bf16[32,24,128]{2,1,0:T(8,128)(2,1)} %chip_maps.1), calls=%async_computation | async-start | bytes 393216 | tf_op jit(solution)/shard_map/all_to_all | solution.py:672
  18.1 2.8 %collective-permute-start.4 = (bf16[8,128,128]{2,1,0:T(8,128)(2,1)S(1)}, bf16[8,128,128]{2,1,0:T(8,128)(2,1)}, u32[]{:S(2)}, u32[]{:S(2)}) collective-permute-start(bf16[8,128,128]{2,1,0:T(8,128)(2,1)S(1)} %get-tuple-element.32.psi_0), channel_id=1, source_target_pairs={{0,3},{1,0},{2,1},{3,2},{4,7},{5,4},{6,5},{7,6},{8,11},{9,8},{10,9... | collective-permute-start | bytes 786440 | tf_op jit(solution)/shard_map/ppermute | solution.py:640
  21.9 1.8 %half_message.1 = (bf16[8,128,128]{2,1,0:T(8,128)(2,1)}, f32[8,128,128]{2,1,0:T(8,128)S(1)}) custom-call(f32[8,128,128]{2,1,0:T(8,128)} %bitcast.22), custom_call_target="tpu_custom_call" | custom-call | flops 262144 | bytes 13107200 | tf_op jit(solution)/shard_map/half_message/pallas_call | solution.py:132
  23.7 2.1 %collective-permute-start.6 = (bf16[8,128,128]{2,1,0:T(8,128)(2,1)}, bf16[8,128,128]{2,1,0:T(8,128)(2,1)S(1)}, u32[]{:S(2)}, u32[]{:S(2)}) collective-permute-start(bf16[8,128,128]{2,1,0:T(8,128)(2,1)} %get-tuple-element.35), channel_id=1, source_target_pairs={{0,3},{1,0},{2,1},{3,2},{4,7},{5,4},{6,5},{7,6},{8,11},{9,8},{10,9... | collective-permute-start | bytes 786440 | tf_op jit(solution)/shard_map/ppermute | solution.py:640
  25.8 1.4 %collective-permute-start.5 = (bf16[8,128,128]{2,1,0:T(8,128)(2,1)}, bf16[8,128,128]{2,1,0:T(8,128)(2,1)S(1)}, u32[]{:S(2)}, u32[]{:S(2)}) collective-permute-start(bf16[8,128,128]{2,1,0:T(8,128)(2,1)} %get-tuple-element.35), channel_id=1, source_target_pairs={{0,2},{1,3},{2,0},{3,1},{4,6},{5,7},{6,4},{7,5},{8,10},{9,11},{10,... | collective-permute-start | bytes 786440 | tf_op jit(solution)/shard_map/ppermute | solution.py:640
  28.4 9.0 %all-to-all-start.1 = ((bf16[32,16,128]{2,1,0:T(8,128)(2,1)}), bf16[32,16,128]{2,1,0:T(8,128)(2,1)S(1)}, u32[]{:S(2)}, u32[]{:S(2)}) async-start(bf16[32,16,128]{2,1,0:T(8,128)(2,1)} %scan_maps.1), calls=%async_computation.1 | async-start | bytes 262144 | tf_op jit(solution)/shard_map/all_to_all | solution.py:679
  38.3 7.1 %first_products.1 = (bf16[32,128,128]{2,1,0:T(8,128)(2,1)S(1)}, f32[8,128,128]{2,1,0:T(8,128)S(1)}) custom-call(s32[256]{0:T(256)S(1)} %get-tuple-element.30.plan, bf16[8,128,128]{2,1,0:T(8,128)(2,1)} %copy-done, bf16[8,128,128]{2,1,0:T(8,128)(2,1)} %copy-done.3, bf16[8,128,128]{2,1,0:T(8,128)(2,1)} %copy-done.2, ...), custom_call_target="tpu_custom_call" | custom-call | flops 2097152 | bytes 131072 | tf_op jit(solution)/shard_map/first_products/pallas_call | solution.py:509
  45.5 1.2 %all-to-all-done.1 = bf16[32,16,128]{2,1,0:T(8,128)(2,1)S(1)} async-done(((bf16[32,16,128]{2,1,0:T(8,128)(2,1)}), bf16[32,16,128]{2,1,0:T(8,128)(2,1)S(1)}, u32[]{:S(2)}, u32[]{:S(2)}) %all-to-all-start.1) | async-done | bytes 131104 | tf_op jit(solution)/shard_map/all_to_all | solution.py:679
  46.7 3.8 %collective-permute-start.7 = (bf16[4,128,128]{2,1,0:T(8,128)(2,1)S(1)}, bf16[4,128,128]{2,1,0:T(8,128)(2,1)S(1)}, u32[]{:S(2)}, u32[]{:S(2)}) collective-permute-start(bf16[4,128,128]{2,1,0:T(8,128)(2,1)S(1)} %bitcast.11), channel_id=1, source_target_pairs={{0,4},{4,0},{8,12},{12,8},{16,20},{20,16},{24,28},{28,24},{32,36},... | collective-permute-start | bytes 393224 | tf_op jit(solution)/shard_map/ppermute | solution.py:683
  51.5 1.5 %first_close.1 = (bf16[8,128,128]{2,1,0:T(8,128)(2,1)S(1)}, f32[8,128,128]{2,1,0:T(8,128)S(1)}, bf16[1040,128]{1,0:T(8,128)(2,1)S(1)}) custom-call(s32[256]{0:T(256)S(1)} %get-tuple-element.30.plan, bf16[32,128,128]{2,1,0:T(8,128)(2,1)S(1)} %get-tuple-element.33.psi_ref.before, f32[8,128,128]{2,1,0:T(8,128)S(1)} %get-tuple-element.38.ops_ref, ...), custom_call_target="tpu_custom_call" | custom-call | flops 33554432 | bytes 2621440 | tf_op jit(solution)/shard_map/first_close/pallas_call | solution.py:529
  55.5 5.2 %collective-permute-done.11.msg_3 = bf16[1040,128]{1,0:T(8,128)(2,1)S(1)} collective-permute-done((bf16[1040,128]{1,0:T(8,128)(2,1)S(1)}, bf16[1040,128]{1,0:T(8,128)(2,1)S(1)}, u32[]{:S(2)}, u32[]{:S(2)}) %collective-permute-start.11) | collective-permute-done | bytes 266272 | tf_op jit(solution)/shard_map/ppermute | solution.py:640
  60.7 1.9 %collective-permute-done.10.msg_2 = bf16[1040,128]{1,0:T(8,128)(2,1)S(1)} collective-permute-done((bf16[1040,128]{1,0:T(8,128)(2,1)S(1)}, bf16[1040,128]{1,0:T(8,128)(2,1)S(1)}, u32[]{:S(2)}, u32[]{:S(2)}) %collective-permute-start.10) | collective-permute-done | bytes 266272 | tf_op jit(solution)/shard_map/ppermute | solution.py:640
  62.6 6.7 %collective-permute-done.9.msg_1 = bf16[1040,128]{1,0:T(8,128)(2,1)S(1)} collective-permute-done((bf16[1040,128]{1,0:T(8,128)(2,1)S(1)}, bf16[1040,128]{1,0:T(8,128)(2,1)S(1)}, u32[]{:S(2)}, u32[]{:S(2)}) %collective-permute-start.9) | collective-permute-done | bytes 266272 | tf_op jit(solution)/shard_map/ppermute | solution.py:640
  69.3 6.5 %later_step.1 = (bf16[32,128,128]{2,1,0:T(8,128)(2,1)S(1)}, f32[8,128,128]{2,1,0:T(8,128)S(1)}, bf16[1040,128]{1,0:T(8,128)(2,1)S(1)}) custom-call(s32[256]{0:T(256)S(1)} %get-tuple-element.30.plan, f32[8,128,128]{2,1,0:T(8,128)S(1)} %get-tuple-element.41.a_own, bf16[1040,128]{1,0:T(8,128)(2,1)S(1)} %get-tuple-element.43.msg_0, ...), custom_call_target="tpu_custom_call" | custom-call | flops 1073741824 | bytes 25165824 | tf_op jit(solution)/shard_map/later_step/pallas_call | solution.py:553
  77.7 5.6 %collective-permute-done.14.msg_3 = bf16[1040,128]{1,0:T(8,128)(2,1)S(1)} collective-permute-done((bf16[1040,128]{1,0:T(8,128)(2,1)S(1)}, bf16[1040,128]{1,0:T(8,128)(2,1)S(1)}, u32[]{:S(2)}, u32[]{:S(2)}) %collective-permute-start.14) | collective-permute-done | bytes 266272 | tf_op jit(solution)/shard_map/ppermute | solution.py:640
  84.4 7.1 %collective-permute-done.12.msg_1 = bf16[1040,128]{1,0:T(8,128)(2,1)S(1)} collective-permute-done((bf16[1040,128]{1,0:T(8,128)(2,1)S(1)}, bf16[1040,128]{1,0:T(8,128)(2,1)S(1)}, u32[]{:S(2)}, u32[]{:S(2)}) %collective-permute-start.12) | collective-permute-done | bytes 266272 | tf_op jit(solution)/shard_map/ppermute | solution.py:640
  91.5 6.6 %last_step.1 = (bf16[32,128,128]{2,1,0:T(8,128)(2,1)S(1)}, f32[8,128,128]{2,1,0:T(8,128)S(1)}, bf16[16,128]{1,0:T(8,128)(2,1)S(1)}) custom-call(s32[256]{0:T(256)S(1)} %get-tuple-element.30.plan, f32[8,128,128]{2,1,0:T(8,128)S(1)} %get-tuple-element.48.a_own, bf16[1040,128]{1,0:T(8,128)(2,1)S(1)} %get-tuple-element.49.msg_0, ...), custom_call_target="tpu_custom_call" | custom-call | flops 1073741824 | bytes 25165824 | tf_op jit(solution)/shard_map/last_step/pallas_call | solution.py:553
  100.6 1.6 %collective-permute-done.16.tile_2 = bf16[16,128]{1,0:T(8,128)(2,1)S(1)} collective-permute-done((bf16[16,128]{1,0:T(8,128)(2,1)S(1)}, bf16[16,128]{1,0:T(8,128)(2,1)S(1)}, u32[]{:S(2)}, u32[]{:S(2)}) %collective-permute-start.16) | collective-permute-done | bytes 4128 | tf_op jit(solution)/shard_map/ppermute | solution.py:640
  103.0 1.4 %ground_state.1 = (bf16[8,128,128]{2,1,0:T(8,128)(2,1)}, bf16[8,128,128]{2,1,0:T(8,128)(2,1)S(1)}, f32[1]{0:T(128)}) custom-call(s32[256]{0:T(256)S(1)} %get-tuple-element.30.plan, bf16[16,128]{1,0:T(8,128)(2,1)S(1)} %get-tuple-element.51.tile_0, bf16[16,128]{1,0:T(8,128)(2,1)S(1)} %collective-permute-done.15.tile_1, ...), custom_call_target="tpu_custom_call" | custom-call | flops 524288 | bytes 1572864 | tf_op jit(solution)/shard_map/ground_state/pallas_call | solution.py:603
  104.5 4.2 %collective-permute-start.18 = (bf16[8,128,128]{2,1,0:T(8,128)(2,1)}, bf16[8,128,128]{2,1,0:T(8,128)(2,1)S(1)}, u32[]{:S(2)}, u32[]{:S(2)}) collective-permute-start(bf16[8,128,128]{2,1,0:T(8,128)(2,1)} %get-tuple-element.54), channel_id=1, source_target_pairs={{4,0},{8,4},{12,8},{16,12},{20,16},{24,20},{28,24},{32,28},{36,32}... | collective-permute-start | bytes 786440 | tf_op jit(solution)/shard_map/ppermute | solution.py:707
  108.6 5.3 %collective-permute-done.18.next_ref = bf16[8,128,128]{2,1,0:T(8,128)(2,1)S(1)} collective-permute-done((bf16[8,128,128]{2,1,0:T(8,128)(2,1)}, bf16[8,128,128]{2,1,0:T(8,128)(2,1)S(1)}, u32[]{:S(2)}, u32[]{:S(2)}) %collective-permute-start.18) | collective-permute-done | bytes 262176 | tf_op jit(solution)/shard_map/ppermute | solution.py:707
  (36 shorter events, 13.9 us)
Async XLA Ops:
  0.6 5.6 %collective-permute-start = (f32[8,128,128]{2,1,0:T(8,128)}, f32[8,128,128]{2,1,0:T(8,128)S(1)}, u32[]{:S(2)}, u32[]{:S(2)}) collective-permute-start(f32[8,128,128]{2,1,0:T(8,128)} %bitcast.20), channel_id=1, source_target_pairs={{0,4},{4,0},{8,12},{12,8},{16,20},{20,16},{24,28},{28,24},{32,36},... | collective-permute-start | bytes 1572872 | tf_op jit(solution)/shard_map/ppermute | solution.py:667
  4.0 2.3 %collective-permute-start.1 = (f32[8,128]{1,0:T(8,128)}, f32[8,128]{1,0:T(8,128)S(1)}, u32[]{:S(2)}, u32[]{:S(2)}) collective-permute-start(f32[8,128]{1,0:T(8,128)} %bitcast.26), channel_id=1, source_target_pairs={{0,4},{4,0},{8,12},{12,8},{16,20},{20,16},{24,28},{28,24},{32,36},... | collective-permute-start | bytes 12296 | tf_op jit(solution)/shard_map/ppermute | solution.py:668
  6.2 31.4 %copy-start = (bf16[8,128,128]{2,1,0:T(8,128)(2,1)}, bf16[8,128,128]{2,1,0:T(8,128)(2,1)S(1)}, u32[]{:S(2)}) copy-start(bf16[8,128,128]{2,1,0:T(8,128)(2,1)S(1)} %get-tuple-element.32.psi_0) | copy-start | bytes 786436
  8.7 18.7 %all-to-all-start = ((bf16[32,24,128]{2,1,0:T(8,128)(2,1)}), bf16[32,24,128]{2,1,0:T(8,128)(2,1)S(1)}, u32[]{:S(2)}, u32[]{:S(2)}) async-start(bf16[32,24,128]{2,1,0:T(8,128)(2,1)} %chip_maps.1), calls=%async_computation | async-start | bytes 393216 | tf_op jit(solution)/shard_map/all_to_all | solution.py:672
  18.1 19.4 %collective-permute-start.4 = (bf16[8,128,128]{2,1,0:T(8,128)(2,1)S(1)}, bf16[8,128,128]{2,1,0:T(8,128)(2,1)}, u32[]{:S(2)}, u32[]{:S(2)}) collective-permute-start(bf16[8,128,128]{2,1,0:T(8,128)(2,1)S(1)} %get-tuple-element.32.psi_0), channel_id=1, source_target_pairs={{0,3},{1,0},{2,1},{3,2},{4,7},{5,4},{6,5},{7,6},{8,11},{9,8},{10,9... | collective-permute-start | bytes 786440 | tf_op jit(solution)/shard_map/ppermute | solution.py:640
  20.9 16.7 %collective-permute-start.3 = (bf16[8,128,128]{2,1,0:T(8,128)(2,1)S(1)}, bf16[8,128,128]{2,1,0:T(8,128)(2,1)S(1)}, u32[]{:S(2)}, u32[]{:S(2)}) collective-permute-start(bf16[8,128,128]{2,1,0:T(8,128)(2,1)S(1)} %get-tuple-element.32.psi_0), channel_id=1, source_target_pairs={{0,2},{1,3},{2,0},{3,1},{4,6},{5,7},{6,4},{7,5},{8,10},{9,11},{10,... | collective-permute-start | bytes 786440 | tf_op jit(solution)/shard_map/ppermute | solution.py:640
  21.2 16.3 %collective-permute-start.2 = (bf16[8,128,128]{2,1,0:T(8,128)(2,1)S(1)}, bf16[8,128,128]{2,1,0:T(8,128)(2,1)S(1)}, u32[]{:S(2)}, u32[]{:S(2)}) collective-permute-start(bf16[8,128,128]{2,1,0:T(8,128)(2,1)S(1)} %get-tuple-element.32.psi_0), channel_id=1, source_target_pairs={{0,1},{1,2},{2,3},{3,0},{4,5},{5,6},{6,7},{7,4},{8,9},{9,10},{10,1... | collective-permute-start | bytes 786440 | tf_op jit(solution)/shard_map/ppermute | solution.py:640
  23.7 21.7 %collective-permute-start.6 = (bf16[8,128,128]{2,1,0:T(8,128)(2,1)}, bf16[8,128,128]{2,1,0:T(8,128)(2,1)S(1)}, u32[]{:S(2)}, u32[]{:S(2)}) collective-permute-start(bf16[8,128,128]{2,1,0:T(8,128)(2,1)} %get-tuple-element.35), channel_id=1, source_target_pairs={{0,3},{1,0},{2,1},{3,2},{4,7},{5,4},{6,5},{7,6},{8,11},{9,8},{10,9... | collective-permute-start | bytes 786440 | tf_op jit(solution)/shard_map/ppermute | solution.py:640
  25.8 19.7 %collective-permute-start.5 = (bf16[8,128,128]{2,1,0:T(8,128)(2,1)}, bf16[8,128,128]{2,1,0:T(8,128)(2,1)S(1)}, u32[]{:S(2)}, u32[]{:S(2)}) collective-permute-start(bf16[8,128,128]{2,1,0:T(8,128)(2,1)} %get-tuple-element.35), channel_id=1, source_target_pairs={{0,2},{1,3},{2,0},{3,1},{4,6},{5,7},{6,4},{7,5},{8,10},{9,11},{10,... | collective-permute-start | bytes 786440 | tf_op jit(solution)/shard_map/ppermute | solution.py:640
  28.4 18.3 %all-to-all-start.1 = ((bf16[32,16,128]{2,1,0:T(8,128)(2,1)}), bf16[32,16,128]{2,1,0:T(8,128)(2,1)S(1)}, u32[]{:S(2)}, u32[]{:S(2)}) async-start(bf16[32,16,128]{2,1,0:T(8,128)(2,1)} %scan_maps.1), calls=%async_computation.1 | async-start | bytes 262144 | tf_op jit(solution)/shard_map/all_to_all | solution.py:679
  37.4 15.6 %collective-permute-start.8 = (bf16[8,128,128]{2,1,0:T(8,128)(2,1)}, bf16[8,128,128]{2,1,0:T(8,128)(2,1)S(1)}, u32[]{:S(2)}, u32[]{:S(2)}) collective-permute-start(bf16[8,128,128]{2,1,0:T(8,128)(2,1)} %get-tuple-element.35), channel_id=1, source_target_pairs={{0,1},{1,2},{2,3},{3,0},{4,5},{5,6},{6,7},{7,4},{8,9},{9,10},{10,1... | collective-permute-start | bytes 786440 | tf_op jit(solution)/shard_map/ppermute | solution.py:640
  37.6 0.8 copy-start.3
  46.7 4.8 %collective-permute-start.7 = (bf16[4,128,128]{2,1,0:T(8,128)(2,1)S(1)}, bf16[4,128,128]{2,1,0:T(8,128)(2,1)S(1)}, u32[]{:S(2)}, u32[]{:S(2)}) collective-permute-start(bf16[4,128,128]{2,1,0:T(8,128)(2,1)S(1)} %bitcast.11), channel_id=1, source_target_pairs={{0,4},{4,0},{8,12},{12,8},{16,20},{20,16},{24,28},{28,24},{32,36},... | collective-permute-start | bytes 393224 | tf_op jit(solution)/shard_map/ppermute | solution.py:683
  53.0 7.7 %collective-permute-start.11 = (bf16[1040,128]{1,0:T(8,128)(2,1)S(1)}, bf16[1040,128]{1,0:T(8,128)(2,1)S(1)}, u32[]{:S(2)}, u32[]{:S(2)}) collective-permute-start(bf16[1040,128]{1,0:T(8,128)(2,1)S(1)} %get-tuple-element.43.msg_0), channel_id=1, source_target_pairs={{0,3},{1,0},{2,1},{3,2},{4,7},{5,4},{6,5},{7,6},{8,11},{9,8},{10,9... | collective-permute-start | bytes 798728 | tf_op jit(solution)/shard_map/ppermute | solution.py:640
  53.7 8.8 %collective-permute-start.10 = (bf16[1040,128]{1,0:T(8,128)(2,1)S(1)}, bf16[1040,128]{1,0:T(8,128)(2,1)S(1)}, u32[]{:S(2)}, u32[]{:S(2)}) collective-permute-start(bf16[1040,128]{1,0:T(8,128)(2,1)S(1)} %get-tuple-element.43.msg_0), channel_id=1, source_target_pairs={{0,2},{1,3},{2,0},{3,1},{4,6},{5,7},{6,4},{7,5},{8,10},{9,11},{10,... | collective-permute-start | bytes 798728 | tf_op jit(solution)/shard_map/ppermute | solution.py:640
  54.7 14.5 %collective-permute-start.9 = (bf16[1040,128]{1,0:T(8,128)(2,1)S(1)}, bf16[1040,128]{1,0:T(8,128)(2,1)S(1)}, u32[]{:S(2)}, u32[]{:S(2)}) collective-permute-start(bf16[1040,128]{1,0:T(8,128)(2,1)S(1)} %get-tuple-element.43.msg_0), channel_id=1, source_target_pairs={{0,1},{1,2},{2,3},{3,0},{4,5},{5,6},{6,7},{7,4},{8,9},{9,10},{10,1... | collective-permute-start | bytes 798728 | tf_op jit(solution)/shard_map/ppermute | solution.py:640
  75.8 7.5 %collective-permute-start.14 = (bf16[1040,128]{1,0:T(8,128)(2,1)S(1)}, bf16[1040,128]{1,0:T(8,128)(2,1)S(1)}, u32[]{:S(2)}, u32[]{:S(2)}) collective-permute-start(bf16[1040,128]{1,0:T(8,128)(2,1)S(1)} %get-tuple-element.49.msg_0), channel_id=1, source_target_pairs={{0,3},{1,0},{2,1},{3,2},{4,7},{5,4},{6,5},{7,6},{8,11},{9,8},{10,9... | collective-permute-start | bytes 798728 | tf_op jit(solution)/shard_map/ppermute | solution.py:640
  75.9 8.5 %collective-permute-start.13 = (bf16[1040,128]{1,0:T(8,128)(2,1)S(1)}, bf16[1040,128]{1,0:T(8,128)(2,1)S(1)}, u32[]{:S(2)}, u32[]{:S(2)}) collective-permute-start(bf16[1040,128]{1,0:T(8,128)(2,1)S(1)} %get-tuple-element.49.msg_0), channel_id=1, source_target_pairs={{0,2},{1,3},{2,0},{3,1},{4,6},{5,7},{6,4},{7,5},{8,10},{9,11},{10,... | collective-permute-start | bytes 798728 | tf_op jit(solution)/shard_map/ppermute | solution.py:640
  77.0 14.5 %collective-permute-start.12 = (bf16[1040,128]{1,0:T(8,128)(2,1)S(1)}, bf16[1040,128]{1,0:T(8,128)(2,1)S(1)}, u32[]{:S(2)}, u32[]{:S(2)}) collective-permute-start(bf16[1040,128]{1,0:T(8,128)(2,1)S(1)} %get-tuple-element.49.msg_0), channel_id=1, source_target_pairs={{0,1},{1,2},{2,3},{3,0},{4,5},{5,6},{6,7},{7,4},{8,9},{9,10},{10,1... | collective-permute-start | bytes 798728 | tf_op jit(solution)/shard_map/ppermute | solution.py:640
  91.5 11.5 %copy-start.1 = (f32[1,8,128]{2,1,0:T(8,128)S(1)}, f32[1,8,128]{2,1,0:T(8,128)}, u32[]{:S(2)}) copy-start(f32[1,8,128]{2,1,0:T(8,128)} %param.20) | copy-start | bytes 12292
  98.1 2.5 %collective-permute-start.17 = (bf16[16,128]{1,0:T(8,128)(2,1)S(1)}, bf16[16,128]{1,0:T(8,128)(2,1)S(1)}, u32[]{:S(2)}, u32[]{:S(2)}) collective-permute-start(bf16[16,128]{1,0:T(8,128)(2,1)S(1)} %get-tuple-element.51.tile_0), channel_id=1, source_target_pairs={{0,3},{1,0},{2,1},{3,2},{4,7},{5,4},{6,5},{7,6},{8,11},{9,8},{10,9... | collective-permute-start | bytes 12296 | tf_op jit(solution)/shard_map/ppermute | solution.py:640
  98.2 4.0 %collective-permute-start.16 = (bf16[16,128]{1,0:T(8,128)(2,1)S(1)}, bf16[16,128]{1,0:T(8,128)(2,1)S(1)}, u32[]{:S(2)}, u32[]{:S(2)}) collective-permute-start(bf16[16,128]{1,0:T(8,128)(2,1)S(1)} %get-tuple-element.51.tile_0), channel_id=1, source_target_pairs={{0,2},{1,3},{2,0},{3,1},{4,6},{5,7},{6,4},{7,5},{8,10},{9,11},{10,... | collective-permute-start | bytes 12296 | tf_op jit(solution)/shard_map/ppermute | solution.py:640
  99.2 3.8 %collective-permute-start.15 = (bf16[16,128]{1,0:T(8,128)(2,1)S(1)}, bf16[16,128]{1,0:T(8,128)(2,1)S(1)}, u32[]{:S(2)}, u32[]{:S(2)}) collective-permute-start(bf16[16,128]{1,0:T(8,128)(2,1)S(1)} %get-tuple-element.51.tile_0), channel_id=1, source_target_pairs={{0,1},{1,2},{2,3},{3,0},{4,5},{5,6},{6,7},{7,4},{8,9},{9,10},{10,1... | collective-permute-start | bytes 12296 | tf_op jit(solution)/shard_map/ppermute | solution.py:640
  104.5 9.4 %collective-permute-start.18 = (bf16[8,128,128]{2,1,0:T(8,128)(2,1)}, bf16[8,128,128]{2,1,0:T(8,128)(2,1)S(1)}, u32[]{:S(2)}, u32[]{:S(2)}) collective-permute-start(bf16[8,128,128]{2,1,0:T(8,128)(2,1)} %get-tuple-element.54), channel_id=1, source_target_pairs={{4,0},{8,4},{12,8},{16,12},{20,16},{24,20},{28,24},{32,28},{36,32}... | collective-permute-start | bytes 786440 | tf_op jit(solution)/shard_map/ppermute | solution.py:707
  (1 other events, 0.7 us)

commit v3 on v2

--- a/solution.py
+++ b/solution.py
@@ -40,8 +40,12 @@
     sizes_hbm,
     ranks_hbm,
     psi_hbm,
+    h_hbm,
+    d_hbm,
     plan,
     out_ref,
+    h_ref,
+    d_ref,
     slot_sector,
     pair_table,
     sizes,
@@ -53,19 +57,22 @@
     terms, sectors = pair_table.shape
     slots, cap, _ = out_ref.shape
     me = lax.axis_index("blk")
+    core = lax.axis_index("sect") & 1
     moves = (
         (slot_hbm, slot_sector),
         (pair_hbm, pair_table),
         (sizes_hbm, sizes),
         (ranks_hbm, ranks),
         (psi_hbm, psi_ref),
+        (d_hbm, d_ref),
+        (h_hbm.at[pl.ds(core * (slots // 2), slots // 2)], h_ref),
     )
     fetches = [pltpu.make_async_copy(a, b, sem.at[k]) for k, (a, b) in enumerate(moves)]
     for fetch in fetches:
         fetch.start()
-    for fetch in fetches:
+    for fetch in fetches[:5]:
         fetch.wait()
-    plan[CORE] = lax.axis_index("sect") & 1
+    plan[CORE] = core
     for j in range(slots):
         sector = slot_sector[me * slots + j]
         size = sizes[0, sector]
@@ -86,9 +93,11 @@
         return carry
 
     lax.fori_loop(0, slots, tables, 0)
-
-
-def start(slot_sector, pair_table, sizes, ranks, psi):
+    for fetch in fetches[5:]:
+        fetch.wait()
+
+
+def start(slot_sector, pair_table, sizes, ranks, psi, own_h, own_d):
     pairs = pair_table.T
     terms = pairs.shape[0]
     slots = psi.shape[0]
@@ -98,19 +107,21 @@
         out_shape=[
             jax.ShapeDtypeStruct((SOURCES + slots * terms,), jnp.int32),
             jax.ShapeDtypeStruct(psi.shape, BF16),
-        ],
-        in_specs=[whole(HBM)] * 5,
-        out_specs=[whole(SMEM), whole()],
+            jax.ShapeDtypeStruct((slots // 2, *psi.shape[1:]), F32),
+            jax.ShapeDtypeStruct(own_d.shape, F32),
+        ],
+        in_specs=[whole(HBM)] * 7,
+        out_specs=[whole(SMEM), whole(), whole(), whole()],
         scratch_shapes=[pltpu.SMEM(t.shape, jnp.int32) for t in tables]
         + [
             pltpu.SMEM(slot_sector.shape, jnp.int32),
             pltpu.VMEM(psi.shape, BF16),
-            pltpu.SemaphoreType.DMA((5,)),
+            pltpu.SemaphoreType.DMA((7,)),
         ],
         compiler_params=params(),
         cost_estimate=cost(4 * psi.size, 4 * psi.size),
         name="start",
-    )(*[in_hbm(t) for t in tables], in_hbm(psi))
+    )(*[in_hbm(t) for t in (*tables, psi, own_h, own_d)])
 
 
 def half_kernel(precond_hbm, out_ref, half_ref, precond_ref, sem):
@@ -144,22 +155,13 @@
     )(in_hbm(precond))
 
 
-def chip_kernel(plan, own_hbm, other_h, own_d_hbm, other_d, out_ref, late_t, own_h, own_d, h_sem, d_sem):
+def chip_kernel(own_h, other_h, own_d, other_d, out_ref, late_t):
     slots, cap = own_d.shape
     mine = slots // 2
     chips, rows, _ = out_ref.shape
     chunk = rows - 8
     cuts = cap // chunk
-    core_here = plan[CORE]
-    first = core_here * mine
-    fetch_d = pltpu.make_async_copy(own_d_hbm, own_d, d_sem)
-    fetch_d.start()
-    fetches = [
-        pltpu.make_async_copy(own_hbm.at[first + j], own_h.at[j], h_sem.at[j]) for j in range(mine)
-    ]
-    for fetch in fetches:
-        fetch.start()
-    fetch_d.wait()
+    core_here = lax.axis_index("sect") & 1
     row = lax.broadcasted_iota(jnp.int32, (8, cap), 0)
 
     def emit(core):
@@ -173,7 +175,6 @@
             tail = jnp.where(
                 row == 0, high[k : k + 1, :], jnp.where(row == 1, low[k : k + 1, :], 0.0)
             )
-            fetches[j].wait()
             early_h, late_h = (own_h[j], other_h[k]) if core == 0 else (other_h[k], own_h[j])
             both = late_t[:, k : k + 1] * early_h * late_d[k : k + 1, :] + late_h
             for cut in range(cuts):
@@ -189,25 +190,19 @@
         emit(1)
 
 
-def chip_maps(plan, own_h, other_h, own_d, other_d, chips):
+def chip_maps(own_h, other_h, own_d, other_d, chips):
     slots, cap = own_d.shape
     chunk = slots // 2 * cap // chips
     return pl.pallas_call(
         chip_kernel,
         out_shape=jax.ShapeDtypeStruct((chips, chunk + 8, cap), BF16),
-        in_specs=[whole(SMEM), whole(HBM), whole(), whole(HBM), whole()],
+        in_specs=[whole()] * 4,
         out_specs=whole(),
-        scratch_shapes=[
-            pltpu.VMEM((cap, slots), F32),
-            pltpu.VMEM((slots // 2, cap, cap), F32),
-            pltpu.VMEM((slots, cap), F32),
-            pltpu.SemaphoreType.DMA((slots // 2,)),
-            pltpu.SemaphoreType.DMA,
-        ],
+        scratch_shapes=[pltpu.VMEM((cap, slots), F32)],
         compiler_params=params(),
         cost_estimate=cost(2 * slots * cap * cap, 6 * slots * cap * cap),
         name="chip_maps",
-    )(plan, in_hbm(own_h), other_h, in_hbm(own_d), other_d)
+    )(own_h, other_h, own_d, other_d)
 
 
 def scan_kernel(maps_ref, out_ref, factor, factor_t):
@@ -241,7 +236,7 @@
     )(maps)
 
 
-def pack_sums(values, cap):
+def pack_rows(values, cap):
     row = lax.broadcasted_iota(jnp.int32, (16, cap), 0)
     tile = jnp.zeros((16, cap), F32)
     for k, value in enumerate(values):
@@ -253,11 +248,11 @@
     return tile.astype(BF16)
 
 
-def unpack_sums(tile):
+def unpack_rows(tile, count):
     tile = tile.astype(F32)
     return [
         tile[3 * k : 3 * k + 1] + tile[3 * k + 1 : 3 * k + 2] + tile[3 * k + 2 : 3 * k + 3]
-        for k in range(5)
+        for k in range(count)
     ]
 
 
@@ -270,7 +265,7 @@
 
 
 def resolve(tiles, entries):
-    sums = [unpack_sums(tile) for tile in tiles]
+    sums = [unpack_rows(tile, 5) for tile in tiles]
     rayleigh = paired([s[0] for s in sums]) / paired([s[1] for s in sums])
     deltas = [rayleigh - local_quotient(s[0], s[1]) for s in sums]
     squares = paired(
@@ -287,35 +282,7 @@
 AHEAD = 3
 
 
-def fetch_ops(j, left_hbm, right_hbm, left_ref, right_ref, ops_sem):
-    pltpu.make_async_copy(left_hbm.at[j], left_ref.at[j], ops_sem.at[0, j]).start()
-    pltpu.make_async_copy(right_hbm.at[j], right_ref.at[j], ops_sem.at[1, j]).start()
-
-
-def fetch_first_ops(*refs):
-    for j in range(AHEAD):
-        fetch_ops(j, *refs)
-
-
-def ops_scratch(left, *more):
-    return [
-        pltpu.VMEM(left.shape, BF16),
-        pltpu.VMEM(left.shape, BF16),
-        *more,
-        pltpu.SemaphoreType.DMA((2, left.shape[0])),
-    ]
-
-
-def products(
-    j, plan, left_hbm, right_hbm, left_ref, right_ref, ops_sem, psi_ref, inner
-):
-    pltpu.make_async_copy(left_hbm.at[j], left_ref.at[j], ops_sem.at[0, j]).wait()
-    pltpu.make_async_copy(right_hbm.at[j], right_ref.at[j], ops_sem.at[1, j]).wait()
-
-    @pl.when(j + AHEAD < left_ref.shape[0])
-    def _():
-        fetch_ops(j + AHEAD, left_hbm, right_hbm, left_ref, right_ref, ops_sem)
-
+def products(j, plan, left_ref, right_ref, psi_ref, inner):
     terms, cap = left_ref.shape[1], left_ref.shape[2]
     for w in range(terms):
         inner[:, w * cap : (w + 1) * cap] = jnp.dot(
@@ -339,8 +306,8 @@
     return (row < size) & (column < size)
 
 
-def close_step(slots, psi_ref, half_ref, applied, a_ref, message_ref):
-    cap = applied.shape[1]
+def close_step(psi_ref, half_ref, applied, a_ref, upper_ref, lower_ref):
+    slots, cap, _ = applied.shape
     zero = jnp.zeros((cap, cap), F32)
     numerator, overlap = zero, zero
     for j in range(slots):
@@ -356,14 +323,19 @@
         a = current - half * (applied[j] - quotient * current)
         b = half * current
         a_ref[j] = a
-        if message_ref.shape[0] > 16:
-            message_ref[j * cap : (j + 1) * cap, :] = a.astype(BF16)
+        if upper_ref is None:
+            pass
+        elif j < slots // 2:
+            upper_ref[j * cap : (j + 1) * cap, :] = a.astype(BF16)
+        else:
+            i = j - slots // 2
+            lower_ref[i * cap : (i + 1) * cap, :] = a.astype(BF16)
         aa = aa + a * a
         ab = ab + a * b
         bb = bb + b * b
     sums = [numerator, overlap, total(aa), total(ab), total(bb)]
-    rows = message_ref.shape[0]
-    message_ref[rows - 16 : rows, :] = pack_sums(sums, cap)
+    rows = lower_ref.shape[0]
+    lower_ref[rows - 16 : rows, :] = pack_rows(sums, cap)
 
 
 def first_kernel(
@@ -382,29 +354,39 @@
     psi_sem,
     ops_sem,
 ):
-    slots, cap = ops_ref.shape[0], ops_ref.shape[1]
+    slots = psi_0.shape[0]
     fetches = []
     for k, part in enumerate((psi_0, psi_1, psi_2, psi_3)):
         target = psi_ref.at[pl.ds(k * slots, slots)]
         fetches.append(pltpu.make_async_copy(part, target, psi_sem.at[k]))
+
+    def fetch_ops(j):
+        return (
+            pltpu.make_async_copy(left_hbm.at[j], left_ref.at[j], ops_sem.at[0, j]),
+            pltpu.make_async_copy(right_hbm.at[j], right_ref.at[j], ops_sem.at[1, j]),
+        )
+
+    def begin(j):
+        for copy in fetch_ops(j):
+            copy.start()
+
     for fetch in fetches:
         fetch.start()
+    begin(0)
     for fetch in fetches:
         fetch.wait()
-    fetch_first_ops(left_hbm, right_hbm, left_ref, right_ref, ops_sem)
+    for j in range(1, AHEAD):
+        begin(j)
 
     def one(j, carry):
-        ops_ref[j] = products(
-            j,
-            plan,
-            left_hbm,
-            right_hbm,
-            left_ref,
-            right_ref,
-            ops_sem,
-            psi_ref,
-            inner,
-        )
+        for copy in fetch_ops(j):
+            copy.wait()
+
+        @pl.when(j + AHEAD < slots)
+        def _():
+            begin(j + AHEAD)
+
+        ops_ref[j] = products(j, plan, left_ref, right_ref, psi_ref, inner)
         return carry
 
     lax.fori_loop(0, slots, one, 0)
@@ -421,11 +403,12 @@
     half_ref,
     env_low,
     a_ref,
-    message_ref,
+    upper_ref,
+    lower_ref,
     applied,
     other_t,
 ):
-    slots, cap = ops_ref.shape[0], ops_ref.shape[1]
+    slots, cap = applied.shape[0], applied.shape[1]
     core = plan[CORE]
     other_t[...] = jnp.transpose(other_d[...])
     for j in range(slots):
@@ -437,66 +420,56 @@
         env_low[j] = env
         result = ops_ref[j] + jnp.dot(env, psi_ref[j], preferred_element_type=F32)
         applied[j] = jnp.where(support_of(plan[SIZES + j], cap), result, 0.0)
-    close_step(slots, psi_ref, half_ref, applied, a_ref, message_ref)
+    close_step(psi_ref, half_ref, applied, a_ref, upper_ref, lower_ref)
 
 
 def later_kernel(
+    last,
     entries,
     plan,
     a_own,
-    msg_0,
-    msg_1,
-    msg_2,
-    msg_3,
-    half_1,
-    half_2,
-    half_3,
+    lower_0,
+    upper_1,
+    lower_1,
+    upper_2,
+    lower_2,
+    upper_3,
+    lower_3,
+    far_b,
     before,
     env_low,
     half_ref,
-    left_hbm,
-    right_hbm,
+    left_ref,
+    right_ref,
     psi_ref,
     a_ref,
-    message_ref,
-    applied,
-    inner,
-    left_ref,
-    right_ref,
-    ops_sem,
+    *more,
 ):
+    upper_ref = None if last else more[0]
+    lower_ref, applied, inner = more[-3:]
     slots, cap = applied.shape[0], applied.shape[1]
-    fetch_first_ops(left_hbm, right_hbm, left_ref, right_ref, ops_sem)
-    rows = msg_1.shape[0]
-    tiles = [m[rows - 16 : rows, :] for m in (msg_0, msg_1, msg_2, msg_3)]
+    rows = lower_1.shape[0]
+    tiles = [m[rows - 16 : rows, :] for m in (lower_0, lower_1, lower_2, lower_3)]
     _, deltas, scale = resolve(tiles, entries)
     for i in range(slots):
         b = half_ref[i] * before[i].astype(F32)
         psi_ref[i] = (scale * (a_own[i] + deltas[0] * b)).astype(BF16)
-    for k, (message, half) in enumerate(((msg_1, half_1), (msg_2, half_2), (msg_3, half_3)), 1):
+    received = ((upper_1, lower_1), (upper_2, lower_2), (upper_3, lower_3))
+    for k, (upper, lower) in enumerate(received, 1):
         for i in range(slots):
-            a = message[i * cap : (i + 1) * cap, :].astype(F32)
-            b = half[i].astype(F32) * before[k * slots + i].astype(F32)
+            message, at = (upper, i) if i < slots // 2 else (lower, i - slots // 2)
+            a = message[at * cap : (at + 1) * cap, :].astype(F32)
+            b = far_b[(k - 1) * slots + i].astype(F32)
             psi_ref[k * slots + i] = (scale * (a + deltas[k] * b)).astype(BF16)
 
     def one(j, carry):
-        result = products(
-            j,
-            plan,
-            left_hbm,
-            right_hbm,
-            left_ref,
-            right_ref,
-            ops_sem,
-            psi_ref,
-            inner,
-        )
+        result = products(j, plan, left_ref, right_ref, psi_ref, inner)
         result = result + jnp.dot(env_low[j], psi_ref[j], preferred_element_type=F32)
         applied[j] = jnp.where(support_of(plan[SIZES + j], cap), result, 0.0)
         return carry
 
     lax.fori_loop(0, slots, one, 0)
-    close_step(slots, psi_ref, half_ref, applied, a_ref, message_ref)
+    close_step(psi_ref, half_ref, applied, a_ref, upper_ref, lower_ref)
 
 
 def step_cost(left):
@@ -516,7 +489,10 @@
         out_specs=[whole()] * 2,
         scratch_shapes=[
             pltpu.VMEM((cap, terms * cap), BF16),
-            *ops_scratch(left, pltpu.SemaphoreType.DMA((4,))),
+            pltpu.VMEM(left.shape, BF16),
+            pltpu.VMEM(right.shape, BF16),
+            pltpu.SemaphoreType.DMA((4,)),
+            pltpu.SemaphoreType.DMA((2, slots)),
         ],
         compiler_params=params(),
         cost_estimate=cost(cap**3, slots * cap * cap),
@@ -524,17 +500,65 @@
     )(plan, *[in_hbm(p) for p in psi], in_hbm(left), in_hbm(right))
 
 
+def ready_kernel(half_1, half_2, half_3, before, left_hbm, b_ref, left_ref, sem):
+    slots = half_1.shape[0]
+    left_copy = pltpu.make_async_copy(left_hbm, left_ref, sem)
+    left_copy.start()
+    for k, half in enumerate((half_1, half_2, half_3)):
+        for i in range(slots):
+            place = (k + 1) * slots + i
+            b_ref[k * slots + i] = (half[i].astype(F32) * before[place].astype(F32)).astype(BF16)
+    left_copy.wait()
+
+
+def ready_left(halves, before, left):
+    slots, _, cap, _ = left.shape
+    return pl.pallas_call(
+        ready_kernel,
+        out_shape=[
+            jax.ShapeDtypeStruct((3 * slots, cap, cap), BF16),
+            pltpu.VMEM(left.shape, BF16),
+        ],
+        in_specs=[whole()] * 4 + [whole(HBM)],
+        out_specs=[whole()] * 2,
+        scratch_shapes=[pltpu.SemaphoreType.DMA],
+        compiler_params=params(),
+        cost_estimate=cost(3 * slots * cap * cap, 2 * left.size),
+        name="ready_left",
+    )(*halves, before, in_hbm(left))
+
+
+def copy_kernel(right_hbm, right_ref, sem):
+    right_copy = pltpu.make_async_copy(right_hbm, right_ref, sem)
+    right_copy.start()
+    right_copy.wait()
+
+
+def ready_right(right):
+    return pl.pallas_call(
+        copy_kernel,
+        out_shape=pltpu.VMEM(right.shape, BF16),
+        in_specs=[whole(HBM)],
+        out_specs=whole(),
+        scratch_shapes=[pltpu.SemaphoreType.DMA],
+        compiler_params=params(),
+        cost_estimate=cost(right.size, 2 * right.size),
+        name="ready_right",
+    )(in_hbm(right))
+
+
 def first_close(plan, psi, ops, env_own, env_got, other_h, other_d, half):
-    slots, cap, _ = ops.shape
+    slots, cap, _ = half.shape
     return pl.pallas_call(
         close_kernel,
         out_shape=[
             jax.ShapeDtypeStruct((slots, cap, cap), BF16),
             jax.ShapeDtypeStruct((slots, cap, cap), F32),
-            jax.ShapeDtypeStruct((slots * cap + 16, cap), BF16),
+            jax.ShapeDtypeStruct((slots // 2 * cap, cap), BF16),
+            jax.ShapeDtypeStruct((slots // 2 * cap + 16, cap), BF16),
         ],
         in_specs=[whole(SMEM)] + [whole()] * 7,
-        out_specs=[whole()] * 3,
+        out_specs=[whole()] * 4,
         scratch_shapes=[
             pltpu.VMEM((slots, cap, cap), F32),
             pltpu.VMEM((cap, slots), F32),
@@ -545,94 +569,115 @@
     )(plan, psi, ops, env_own, env_got, other_h, other_d, half)
 
 
-def later_step(
-    plan, entries, a_own, message, got, halves, before, env, half, left, right, last
-):
+def later_step(plan, entries, a_own, lower, got, far_b, before, env, half, left, right, last):
     slots, terms, cap, _ = left.shape
-    out_rows = 16 if last else slots * cap + 16
-    return pl.pallas_call(
-        functools.partial(later_kernel, entries),
+    rows = slots // 2 * cap
+    sent = [jax.ShapeDtypeStruct((16 if last else rows + 16, cap), BF16)]
+    if not last:
+        sent = [jax.ShapeDtypeStruct((rows, cap), BF16)] + sent
+    return pl.pallas_call(
+        functools.partial(later_kernel, last, entries),
         out_shape=[
             jax.ShapeDtypeStruct((4 * slots, cap, cap), BF16),
             jax.ShapeDtypeStruct((slots, cap, cap), F32),
-            jax.ShapeDtypeStruct((out_rows, cap), BF16),
-        ],
-        in_specs=[whole(SMEM)] + [whole()] * 11 + [whole(HBM)] * 2,
-        out_specs=[whole()] * 3,
+            *sent,
+        ],
+        in_specs=[whole(SMEM)] + [whole()] * 14,
+        out_specs=[whole()] * (2 + len(sent)),
         scratch_shapes=[
             pltpu.VMEM((slots, cap, cap), F32),
             pltpu.VMEM((cap, terms * cap), BF16),
-            *ops_scratch(left),
         ],
         compiler_params=params(),
         cost_estimate=step_cost(left),
         name="last_step" if last else "later_step",
-    )(plan, a_own, message, *got, *halves, before, env, half, in_hbm(left), in_hbm(right))
-
-
-def ground_kernel(
-    entries,
-    plan,
-    tile_0,
-    tile_1,
-    tile_2,
-    tile_3,
-    a_ref,
-    psi_ref,
-    half_ref,
-    inv_sv,
-    ground_ref,
-    scaled_ref,
-    energy_ref,
-):
-    slots, cap = a_ref.shape[0], a_ref.shape[1]
-    lane = lax.broadcasted_iota(jnp.int32, (1, cap), 1)
+    )(plan, a_own, lower, *got, far_b, before, env, half, left, right)
+
+
+def near_kernel(a_ref, psi_ref, half_ref, near_ref):
+    for j in range(a_ref.shape[0]):
+        near_ref[0, j] = a_ref[j].astype(BF16)
+        near_ref[1, j] = (half_ref[j] * psi_ref[j].astype(F32)).astype(BF16)
+
+
+def near_message(a_own, psi, half):
+    slots, cap, _ = a_own.shape
+    return pl.pallas_call(
+        near_kernel,
+        out_shape=jax.ShapeDtypeStruct((2, slots, cap, cap), BF16),
+        in_specs=[whole()] * 3,
+        out_specs=whole(),
+        compiler_params=params(),
+        cost_estimate=cost(2 * slots * cap * cap, 12 * slots * cap * cap),
+        name="near_message",
+    )(a_own, psi, half)
+
+
+def settle_kernel(entries, tile_0, tile_1, tile_2, tile_3, factors_ref, energy_ref):
     tiles = [t[...] for t in (tile_0, tile_1, tile_2, tile_3)]
     rayleigh, deltas, scale = resolve(tiles, entries)
     energy_ref[0] = rayleigh[0, 0]
+    factors_ref[...] = pack_rows([scale, deltas[0]], factors_ref.shape[1])
+
+
+def settle(tiles, entries):
+    cap = tiles[0].shape[1]
+    return pl.pallas_call(
+        functools.partial(settle_kernel, entries),
+        out_shape=[jax.ShapeDtypeStruct((16, cap), BF16), jax.ShapeDtypeStruct((1,), F32)],
+        in_specs=[whole()] * 4,
+        out_specs=[whole(), whole(SMEM)],
+        compiler_params=params(),
+        cost_estimate=cost(16 * cap, 128 * cap),
+        name="settle",
+    )(*tiles)
+
+
+def ground_kernel(plan, factors_ref, a_ref, psi_ref, half_ref, inv_sv, ground_ref, scaled_ref):
+    slots, cap = a_ref.shape[0], a_ref.shape[1]
+    scale, delta = unpack_rows(factors_ref[...], 2)
+    lane = lax.broadcasted_iota(jnp.int32, (1, cap), 1)
     for j in range(slots):
         b = half_ref[j] * psi_ref[j].astype(F32)
-        ground = (scale * (a_ref[j] + deltas[0] * b)).astype(BF16)
+        ground = (scale * (a_ref[j] + delta * b)).astype(BF16)
         ground_ref[j] = ground
         weight = jnp.where(lane < plan[RANKS + j], inv_sv[j : j + 1, :] / cap, 0.0)
         scaled_ref[j] = (ground.astype(F32) * weight).astype(BF16)
 
 
-def ground_state(plan, tiles, a_own, psi, half, inv_sv, entries):
+def ground_state(plan, factors, a_own, psi, half, inv_sv):
     slots, cap, _ = a_own.shape
     return pl.pallas_call(
-        functools.partial(ground_kernel, entries),
-        out_shape=[
-            jax.ShapeDtypeStruct((slots, cap, cap), BF16),
-            jax.ShapeDtypeStruct((slots, cap, cap), BF16),
-            jax.ShapeDtypeStruct((1,), F32),
-        ],
-        in_specs=[whole(SMEM)] + [whole()] * 8,
-        out_specs=[whole(), whole(), whole(SMEM)],
+        ground_kernel,
+        out_shape=[jax.ShapeDtypeStruct((slots, cap, cap), BF16)] * 2,
+        in_specs=[whole(SMEM)] + [whole()] * 5,
+        out_specs=[whole(), whole()],
         compiler_params=params(),
         cost_estimate=cost(4 * slots * cap * cap, 12 * slots * cap * cap),
         name="ground_state",
-    )(plan, *tiles, a_own, psi, half, inv_sv)
-
-
-def merge_kernel(scaled_ref, next_ref, out_ref):
+    )(plan, factors, a_own, psi, half, inv_sv)
+
+
+def merge_kernel(factors_ref, scaled_ref, near_ref, out_ref):
     live = lax.axis_index("sect") < lax.axis_size("sect") - 1
+    scale, delta = unpack_rows(factors_ref[...], 2)
     for j in range(scaled_ref.shape[0]):
-        merged = jnp.dot(scaled_ref[j], next_ref[j], preferred_element_type=F32)
+        following = scale * (near_ref[0, j].astype(F32) + delta * near_ref[1, j].astype(F32))
+        merged = jnp.dot(scaled_ref[j], following.astype(BF16), preferred_element_type=F32)
         out_ref[j] = jnp.where(live, merged, 0.0).astype(BF16)
 
 
-def merge(scaled, following):
+def merge(factors, scaled, near):
     slots, cap, _ = scaled.shape
     return pl.pallas_call(
         merge_kernel,
         out_shape=jax.ShapeDtypeStruct((slots, cap, cap), BF16),
-        in_specs=[whole()] * 2,
+        in_specs=[whole()] * 3,
         out_specs=whole(),
         compiler_params=params(),
         cost_estimate=cost(2 * slots * cap**3, 6 * slots * cap * cap),
         name="merge",
-    )(scaled, following)
+    )(factors, scaled, near)
 
 
 def around(value, shift):
@@ -642,6 +687,16 @@
 
 def three(value):
     return [around(value, shift) for shift in (1, 2, 3)]
+
+
+def pass_on(upper, lower):
+    upper_1 = around(upper, 1)
+    lower_3 = around(lower, 3)
+    lower_1 = around(lower, 1)
+    upper_3 = around(upper, 3)
+    upper_2 = around(upper_1, 1)
+    lower_2 = around(lower_3, 3)
+    return [upper_1, lower_1, upper_2, lower_2, upper_3, lower_3]
 
 
 def shards(
@@ -666,8 +721,10 @@
     swap = [(i, i ^ 1) for i in range(sections)]
     other_h = lax.ppermute(source_h[0], "sect", swap)
     other_d = lax.ppermute(decay[0], "sect", swap)
-    plan, own_psi = start(slot_sector, pair_table, sector_sizes, ranks, psi_guess[0])
-    maps = chip_maps(plan, source_h[0], other_h, decay[0], other_d, chips)
+    plan, own_psi, own_h, own_d = start(
+        slot_sector, pair_table, sector_sizes, ranks, psi_guess[0], source_h[0], decay[0]
+    )
+    maps = chip_maps(own_h, other_h, own_d, other_d, chips)
     groups = [[2 * q + c for q in range(chips)] for c in range(2)]
     got_maps = lax.all_to_all(maps, "sect", 0, 0, tiled=True, axis_index_groups=groups)
     own_psi, late_precond, _ = lax.optimization_barrier((own_psi, precond[0], maps))
@@ -681,31 +738,28 @@
     psi, ops = first_products(plan, [own_psi] + got_psi, left, right)
     env_own, ops, halves[1:] = lax.optimization_barrier((env_own, ops, halves[1:]))
     env_got = lax.ppermute(env_own, "sect", swap)
-    env_low, a_own, message = first_close(
+    env_low, a_own, upper, lower = first_close(
         plan, psi, ops, env_own, env_got, other_h, other_d, half
     )
-    message, halves[0] = lax.optimization_barrier((message, halves[0]))
+    lower, halves[0] = lax.optimization_barrier((lower, halves[0]))
     for step in range(1, STEPS):
-        psi, a_own, message = later_step(
-            plan,
-            entries,
-            a_own,
-            message,
-            three(message),
-            halves,
-            psi,
-            env_low,
-            half,
-            left,
-            right,
-            step == STEPS - 1,
+        last = step == STEPS - 1
+        got = pass_on(upper, lower)
+        later_left, later_right, _ = lax.optimization_barrier((left, right, lower))
+        far_b, later_left = ready_left(halves, psi, later_left)
+        later_right = ready_right(later_right)
+        psi, a_own, *sent = later_step(
+            plan, entries, a_own, lower, got, far_b, psi, env_low, half, later_left, later_right, last
         )
-    tiles = [message] + three(message)
-    ground, scaled, energies = ground_state(
-        plan, tiles, a_own, psi, half, inv_sv[0], entries
-    )
-    following = lax.ppermute(ground, "sect", [(i + 1, i) for i in range(sections - 1)])
-    merged = merge(scaled, following)
+        upper, lower = sent[0], sent[-1]
+    tile = lower
+    near = near_message(a_own, psi, half)
+    behind = [(i + 1, i) for i in range(sections - 1)]
+    near = lax.ppermute(near, "sect", behind)
+    factors, energies = settle([tile] + three(tile), entries)
+    near_factors = lax.ppermute(factors, "sect", behind)
+    ground, scaled = ground_state(plan, factors, a_own, psi, half, inv_sv[0])
+    merged = merge(near_factors, scaled, near)
     return (ground[None], energies, merged[None])
 
 

time: 115 us -> 108 us (0.939)
  waiting for transfers between devices: 38.3 us -> 13.5 us
  starting transfers between devices: 43.4 us -> 55.4 us
  Pallas kernels: 31.5 us -> 37.1 us
    ppermute x15 -> x21, waiting for transfers between devices: 30.7 us -> 9 us  [around(): lax.ppermute(value, 'blk', [(i, (i + shift) % count) for i in range(count)])]
    pallas_call x3 -> x9, Pallas kernels: 14.5 us -> 21.9 us  [the longest x2 11.1 us: later_step(): pl.pallas_call(functools.partial(later_kernel, last, entries), out_shape=...]
    ppermute x15 -> x21, starting transfers between devices: 13.7 us -> 20.8 us  [around(): lax.ppermute(value, 'blk', [(i, (i + shift) % count) for i in range(count)])]
    ppermute x1 -> x2, starting transfers between devices: 4.17 us -> 8.99 us  [the longest x1 5.99 us: shards(): near = lax.ppermute(near, 'sect', behind)]
    ppermute x1 -> x2, waiting for transfers between devices: 5.26 us -> 1.85 us  [the longest x1 1.85 us: shards(): near_factors = lax.ppermute(factors, 'sect', behind)]
    pallas_call x1, Pallas kernels: 2.48 us -> 0.97 us  [chip_maps(): pl.pallas_call(chip_kernel, out_shape=jax.ShapeDtypeStruct((chips, chunk...]
  transfers between devices with their start and end apart: 21 -> 28, of which waited for: 13 -> 9; matrix products, arithmetic and copies ran while one was open for 0% -> 0% of each run, Pallas kernels for 12% -> 22%
where the time goes in v3:
time: 108 us
  starting transfers between devices  55.4 us (51%)
  Pallas kernels  37.1 us (34%)
  waiting for transfers between devices  13.5 us (12%)
    ppermute x21, starting transfers between devices, around(): lax.ppermute(value, 'blk', [(i, (i + shift) % count) for i in range(count)])  20.8 us
    pallas_call x2, Pallas kernels, later_step(): pl.pallas_call(functools.partial(later_kernel, last, entries), out_shape=...  11.1 us
    all_to_all x1, starting transfers between devices, shards(): lax.all_to_all(maps, 'sect', 0, 0, tiled=True, axis_index_groups=groups)  9.3 us
    all_to_all x1, starting transfers between devices, shards(): lax.all_to_all(env, 'sect', 0, 0, tiled=True, axis_index_groups=groups)  9.02 us
    ppermute x21, waiting for transfers between devices, around(): lax.ppermute(value, 'blk', [(i, (i + shift) % count) for i in range(count)])  9 us
    pallas_call x1, Pallas kernels, first_products(): pl.pallas_call(first_kernel, out_shape=[jax.ShapeDtypeStruct((4 * slots,...  6.83 us
    ppermute x1, starting transfers between devices, shards(): near = lax.ppermute(near, 'sect', behind)  5.99 us
    pallas_call x2, Pallas kernels, ready_right(): pl.pallas_call(copy_kernel, out_shape=pltpu.VMEM(right.shape, BF16), in_s...  4.4 us
  transfers between devices with their start and end apart: 28, of which 9 were waited for; matrix products, arithmetic and copies ran while one was open for 0% of the time, Pallas kernels for 22%

profile of v3, /device:TPU:1, one launch (start us, length us, event | category | flops | bytes accessed | tf_op | source)
XLA Modules:
  0.0 107.8 jit_solution(12014077658191696685)
XLA Ops:
  0.6 3.3 %collective-permute-start = (f32[8,128,128]{2,1,0:T(8,128)}, f32[8,128,128]{2,1,0:T(8,128)S(1)}, u32[]{:S(2)}, u32[]{:S(2)}) collective-permute-start(f32[8,128,128]{2,1,0:T(8,128)} %bitcast.20), channel_id=1, source_target_pairs={{0,4},{4,0},{8,12},{12,8},{16,20},{20,16},{24,28},{28,24},{32,36},... | collective-permute-start | bytes 1572872 | tf_op jit(solution)/shard_map/ppermute | solution.py:722
  4.1 2.2 %start.1 = (s32[256]{0:T(256)S(1)}, bf16[8,128,128]{2,1,0:T(8,128)(2,1)S(1)}, f32[4,128,128]{2,1,0:T(8,128)S(1)}, f32[8,128]{1,0:T(8,128)S(1)}) custom-call(s32[32]{0:T(128)} %slot_hbm.1, s32[16,32]{1,0:T(8,128)} %bitcast.25, s32[1,32]{1,0:T(1,128)} %sizes_hbm.1, s32[1,32]{1,0:T(1,128)} %ranks_hbm.1, bf16[8,128,128]{2,1,0:T(8,128)(2,1)} %bitcast.23, ...), custom_call_target="tpu_custom_call" | custom-call | flops 524288 | bytes 524288 | tf_op jit(solution)/shard_map/start/pallas_call | solution.py:105
  7.2 9.3 %all-to-all-start = ((bf16[32,24,128]{2,1,0:T(8,128)(2,1)}), bf16[32,24,128]{2,1,0:T(8,128)(2,1)S(1)}, u32[]{:S(2)}, u32[]{:S(2)}) async-start(bf16[32,24,128]{2,1,0:T(8,128)(2,1)} %chip_maps.1), calls=%async_computation | async-start | bytes 393216 | tf_op jit(solution)/shard_map/all_to_all | solution.py:729
  16.5 2.8 %collective-permute-start.4 = (bf16[8,128,128]{2,1,0:T(8,128)(2,1)S(1)}, bf16[8,128,128]{2,1,0:T(8,128)(2,1)}, u32[]{:S(2)}, u32[]{:S(2)}) collective-permute-start(bf16[8,128,128]{2,1,0:T(8,128)(2,1)S(1)} %get-tuple-element.47.psi_0), channel_id=1, source_target_pairs={{0,3},{1,0},{2,1},{3,2},{4,7},{5,4},{6,5},{7,6},{8,11},{9,8},{10,9... | collective-permute-start | bytes 786440 | tf_op jit(solution)/shard_map/ppermute | solution.py:685
  20.4 1.8 %half_message.1 = (bf16[8,128,128]{2,1,0:T(8,128)(2,1)}, f32[8,128,128]{2,1,0:T(8,128)S(1)}) custom-call(f32[8,128,128]{2,1,0:T(8,128)} %bitcast.22), custom_call_target="tpu_custom_call" | custom-call | flops 262144 | bytes 13107200 | tf_op jit(solution)/shard_map/half_message/pallas_call | solution.py:143
  22.2 2.1 %collective-permute-start.6 = (bf16[8,128,128]{2,1,0:T(8,128)(2,1)}, bf16[8,128,128]{2,1,0:T(8,128)(2,1)S(1)}, u32[]{:S(2)}, u32[]{:S(2)}) collective-permute-start(bf16[8,128,128]{2,1,0:T(8,128)(2,1)} %get-tuple-element.50), channel_id=1, source_target_pairs={{0,3},{1,0},{2,1},{3,2},{4,7},{5,4},{6,5},{7,6},{8,11},{9,8},{10,9... | collective-permute-start | bytes 786440 | tf_op jit(solution)/shard_map/ppermute | solution.py:685
  26.9 9.0 %all-to-all-start.1 = ((bf16[32,16,128]{2,1,0:T(8,128)(2,1)}), bf16[32,16,128]{2,1,0:T(8,128)(2,1)S(1)}, u32[]{:S(2)}, u32[]{:S(2)}) async-start(bf16[32,16,128]{2,1,0:T(8,128)(2,1)} %scan_maps.1), calls=%async_computation.1 | async-start | bytes 262144 | tf_op jit(solution)/shard_map/all_to_all | solution.py:736
  36.8 6.8 %first_products.1 = (bf16[32,128,128]{2,1,0:T(8,128)(2,1)S(1)}, f32[8,128,128]{2,1,0:T(8,128)S(1)}) custom-call(s32[256]{0:T(256)S(1)} %get-tuple-element.43.plan, bf16[8,128,128]{2,1,0:T(8,128)(2,1)} %copy-done, bf16[8,128,128]{2,1,0:T(8,128)(2,1)} %copy-done.3, bf16[8,128,128]{2,1,0:T(8,128)(2,1)} %copy-done.2, ...), custom_call_target="tpu_custom_call" | custom-call | flops 2097152 | bytes 131072 | tf_op jit(solution)/shard_map/first_products/pallas_call | solution.py:482
  45.2 3.8 %collective-permute-start.7 = (bf16[4,128,128]{2,1,0:T(8,128)(2,1)S(1)}, bf16[4,128,128]{2,1,0:T(8,128)(2,1)S(1)}, u32[]{:S(2)}, u32[]{:S(2)}) collective-permute-start(bf16[4,128,128]{2,1,0:T(8,128)(2,1)S(1)} %bitcast.11), channel_id=1, source_target_pairs={{0,4},{4,0},{8,12},{12,8},{16,20},{20,16},{24,28},{28,24},{32,36},... | collective-permute-start | bytes 393224 | tf_op jit(solution)/shard_map/ppermute | solution.py:740
  53.1 3.3 %collective-permute-done.12.lower_3 = bf16[528,128]{1,0:T(8,128)(2,1)S(1)} collective-permute-done((bf16[528,128]{1,0:T(8,128)(2,1)S(1)}, bf16[528,128]{1,0:T(8,128)(2,1)S(1)}, u32[]{:S(2)}, u32[]{:S(2)}) %collective-permute-start.12) | collective-permute-done | bytes 135200 | tf_op jit(solution)/shard_map/ppermute | solution.py:685
  56.4 1.6 %collective-permute-start.13 = (bf16[528,128]{1,0:T(8,128)(2,1)S(1)}, bf16[528,128]{1,0:T(8,128)(2,1)S(1)}, u32[]{:S(2)}, u32[]{:S(2)}) collective-permute-start(bf16[528,128]{1,0:T(8,128)(2,1)S(1)} %collective-permute-done.12.lower_3), channel_id=1, source_target_pairs={{0,3},{1,0},{2,1},{3,2},{4,7},{5,4},{6,5},{7,6},{8,11},{9,8},{10,9... | collective-permute-start | bytes 405512 | tf_op jit(solution)/shard_map/ppermute | solution.py:685
  59.5 2.2 %ready_left.2 = (bf16[24,128,128]{2,1,0:T(8,128)(2,1)S(1)}, bf16[8,16,128,128]{3,2,1,0:T(8,128)(2,1)S(1)}) custom-call(bf16[8,128,128]{2,1,0:T(8,128)(2,1)S(1)} %collective-permute-done.8.half_1, bf16[8,128,128]{2,1,0:T(8,128)(2,1)S(1)} %collective-permute-done.5.half_2, bf16[8,128,128]{2,1,0:T(8,128)(2,1)S(1)} %collective-permute-done.6.half_3, ...), custom_call_target="tpu_custom_call" | custom-call | flops 393216 | bytes 4194304 | tf_op jit(solution)/shard_map/ready_left/pallas_call | solution.py:516
  61.7 2.2 %ready_right.2.right_ref = bf16[8,16,128,128]{3,2,1,0:T(8,128)(2,1)S(1)} custom-call(bf16[8,16,128,128]{3,2,1,0:T(8,128)(2,1)} %bitcast.18), custom_call_target="tpu_custom_call" | custom-call | flops 2097152 | bytes 4194304 | tf_op jit(solution)/shard_map/ready_right/pallas_call | solution.py:538
  63.9 5.5 %later_step.1 = (bf16[32,128,128]{2,1,0:T(8,128)(2,1)S(1)}, f32[8,128,128]{2,1,0:T(8,128)S(1)}, bf16[512,128]{1,0:T(8,128)(2,1)S(1)}, bf16[528,128]{1,0:T(8,128)(2,1)S(1)}) custom-call(s32[256]{0:T(256)S(1)} %get-tuple-element.43.plan, f32[8,128,128]{2,1,0:T(8,128)S(1)} %get-tuple-element.56.a_own, bf16[528,128]{1,0:T(8,128)(2,1)S(1)} %get-tuple-element.58.lower_0, ...), custom_call_target="tpu_custom_call" | custom-call | flops 1073741824 | bytes 25165824 | tf_op jit(solution)/shard_map/later_step/pallas_call | solution.py:578
  69.5 2.1 %collective-permute-start.18 = (bf16[528,128]{1,0:T(8,128)(2,1)S(1)}, bf16[528,128]{1,0:T(8,128)(2,1)S(1)}, u32[]{:S(2)}, u32[]{:S(2)}) collective-permute-start(bf16[528,128]{1,0:T(8,128)(2,1)S(1)} %get-tuple-element.69.lower_0), channel_id=1, source_target_pairs={{0,3},{1,0},{2,1},{3,2},{4,7},{5,4},{6,5},{7,6},{8,11},{9,8},{10,9... | collective-permute-start | bytes 405512 | tf_op jit(solution)/shard_map/ppermute | solution.py:685
  71.6 2.0 %collective-permute-done.18.lower_3 = bf16[528,128]{1,0:T(8,128)(2,1)S(1)} collective-permute-done((bf16[528,128]{1,0:T(8,128)(2,1)S(1)}, bf16[528,128]{1,0:T(8,128)(2,1)S(1)}, u32[]{:S(2)}, u32[]{:S(2)}) %collective-permute-start.18) | collective-permute-done | bytes 135200 | tf_op jit(solution)/shard_map/ppermute | solution.py:685
  73.5 3.1 %collective-permute-start.19 = (bf16[528,128]{1,0:T(8,128)(2,1)S(1)}, bf16[528,128]{1,0:T(8,128)(2,1)S(1)}, u32[]{:S(2)}, u32[]{:S(2)}) collective-permute-start(bf16[528,128]{1,0:T(8,128)(2,1)S(1)} %collective-permute-done.18.lower_3), channel_id=1, source_target_pairs={{0,3},{1,0},{2,1},{3,2},{4,7},{5,4},{6,5},{7,6},{8,11},{9,8},{10,9... | collective-permute-start | bytes 405512 | tf_op jit(solution)/shard_map/ppermute | solution.py:685
  78.1 2.2 %ready_left.3 = (bf16[24,128,128]{2,1,0:T(8,128)(2,1)S(1)}, bf16[8,16,128,128]{3,2,1,0:T(8,128)(2,1)S(1)}) custom-call(bf16[8,128,128]{2,1,0:T(8,128)(2,1)S(1)} %collective-permute-done.8.half_1, bf16[8,128,128]{2,1,0:T(8,128)(2,1)S(1)} %collective-permute-done.5.half_2, bf16[8,128,128]{2,1,0:T(8,128)(2,1)S(1)} %collective-permute-done.6.half_3, ...), custom_call_target="tpu_custom_call" | custom-call | flops 393216 | bytes 4194304 | tf_op jit(solution)/shard_map/ready_left/pallas_call | solution.py:516
  80.3 2.2 %ready_right.3.right_ref = bf16[8,16,128,128]{3,2,1,0:T(8,128)(2,1)S(1)} custom-call(bf16[8,16,128,128]{3,2,1,0:T(8,128)(2,1)} %bitcast.19), custom_call_target="tpu_custom_call" | custom-call | flops 2097152 | bytes 4194304 | tf_op jit(solution)/shard_map/ready_right/pallas_call | solution.py:538
  82.6 5.6 %last_step.1 = (bf16[32,128,128]{2,1,0:T(8,128)(2,1)S(1)}, f32[8,128,128]{2,1,0:T(8,128)S(1)}, bf16[16,128]{1,0:T(8,128)(2,1)S(1)}) custom-call(s32[256]{0:T(256)S(1)} %get-tuple-element.43.plan, f32[8,128,128]{2,1,0:T(8,128)S(1)} %get-tuple-element.68.a_own, bf16[528,128]{1,0:T(8,128)(2,1)S(1)} %get-tuple-element.69.lower_0, ...), custom_call_target="tpu_custom_call" | custom-call | flops 1073741824 | bytes 25165824 | tf_op jit(solution)/shard_map/last_step/pallas_call | solution.py:578
  88.2 6.0 %collective-permute-start.25 = (bf16[2,8,128,128]{3,2,1,0:T(8,128)(2,1)S(1)}, bf16[2,8,128,128]{3,2,1,0:T(8,128)(2,1)S(1)}, u32[]{:S(2)}, u32[]{:S(2)}) collective-permute-start(bf16[2,8,128,128]{3,2,1,0:T(8,128)(2,1)S(1)} %near_message.1), channel_id=1, source_target_pairs={{4,0},{8,4},{12,8},{16,12},{20,16},{24,20},{28,24},{32,28},{36,32}... | collective-permute-start | bytes 1572872 | tf_op jit(solution)/shard_map/ppermute | solution.py:758
  96.9 2.3 %collective-permute-done.22.tile_2 = bf16[16,128]{1,0:T(8,128)(2,1)S(1)} collective-permute-done((bf16[16,128]{1,0:T(8,128)(2,1)S(1)}, bf16[16,128]{1,0:T(8,128)(2,1)S(1)}, u32[]{:S(2)}, u32[]{:S(2)}) %collective-permute-start.22) | collective-permute-done | bytes 4128 | tf_op jit(solution)/shard_map/ppermute | solution.py:685
  100.6 3.0 %collective-permute-start.24 = (bf16[16,128]{1,0:T(8,128)(2,1)S(1)}, bf16[16,128]{1,0:T(8,128)(2,1)S(1)}, u32[]{:S(2)}, u32[]{:S(2)}) collective-permute-start(bf16[16,128]{1,0:T(8,128)(2,1)S(1)} %get-tuple-element.77.factors_ref), channel_id=1, source_target_pairs={{4,0},{8,4},{12,8},{16,12},{20,16},{24,20},{28,24},{32,28},{36,32}... | collective-permute-start | bytes 12296 | tf_op jit(solution)/shard_map/ppermute | solution.py:760
  105.0 1.8 %collective-permute-done.24.factors_ref = bf16[16,128]{1,0:T(8,128)(2,1)S(1)} collective-permute-done((bf16[16,128]{1,0:T(8,128)(2,1)S(1)}, bf16[16,128]{1,0:T(8,128)(2,1)S(1)}, u32[]{:S(2)}, u32[]{:S(2)}) %collective-permute-start.24) | collective-permute-done | bytes 4128 | tf_op jit(solution)/shard_map/ppermute | solution.py:760
  (56 shorter events, 20.5 us)
Async XLA Ops:
  0.6 5.6 %collective-permute-start = (f32[8,128,128]{2,1,0:T(8,128)}, f32[8,128,128]{2,1,0:T(8,128)S(1)}, u32[]{:S(2)}, u32[]{:S(2)}) collective-permute-start(f32[8,128,128]{2,1,0:T(8,128)} %bitcast.20), channel_id=1, source_target_pairs={{0,4},{4,0},{8,12},{12,8},{16,20},{20,16},{24,28},{28,24},{32,36},... | collective-permute-start | bytes 1572872 | tf_op jit(solution)/shard_map/ppermute | solution.py:722
  7.2 18.7 %all-to-all-start = ((bf16[32,24,128]{2,1,0:T(8,128)(2,1)}), bf16[32,24,128]{2,1,0:T(8,128)(2,1)S(1)}, u32[]{:S(2)}, u32[]{:S(2)}) async-start(bf16[32,24,128]{2,1,0:T(8,128)(2,1)} %chip_maps.1), calls=%async_computation | async-start | bytes 393216 | tf_op jit(solution)/shard_map/all_to_all | solution.py:729
  16.5 19.4 %collective-permute-start.4 = (bf16[8,128,128]{2,1,0:T(8,128)(2,1)S(1)}, bf16[8,128,128]{2,1,0:T(8,128)(2,1)}, u32[]{:S(2)}, u32[]{:S(2)}) collective-permute-start(bf16[8,128,128]{2,1,0:T(8,128)(2,1)S(1)} %get-tuple-element.47.psi_0), channel_id=1, source_target_pairs={{0,3},{1,0},{2,1},{3,2},{4,7},{5,4},{6,5},{7,6},{8,11},{9,8},{10,9... | collective-permute-start | bytes 786440 | tf_op jit(solution)/shard_map/ppermute | solution.py:685
  19.3 16.7 %collective-permute-start.3 = (bf16[8,128,128]{2,1,0:T(8,128)(2,1)S(1)}, bf16[8,128,128]{2,1,0:T(8,128)(2,1)S(1)}, u32[]{:S(2)}, u32[]{:S(2)}) collective-permute-start(bf16[8,128,128]{2,1,0:T(8,128)(2,1)S(1)} %get-tuple-element.47.psi_0), channel_id=1, source_target_pairs={{0,2},{1,3},{2,0},{3,1},{4,6},{5,7},{6,4},{7,5},{8,10},{9,11},{10,... | collective-permute-start | bytes 786440 | tf_op jit(solution)/shard_map/ppermute | solution.py:685
  19.7 16.3 %collective-permute-start.2 = (bf16[8,128,128]{2,1,0:T(8,128)(2,1)S(1)}, bf16[8,128,128]{2,1,0:T(8,128)(2,1)S(1)}, u32[]{:S(2)}, u32[]{:S(2)}) collective-permute-start(bf16[8,128,128]{2,1,0:T(8,128)(2,1)S(1)} %get-tuple-element.47.psi_0), channel_id=1, source_target_pairs={{0,1},{1,2},{2,3},{3,0},{4,5},{5,6},{6,7},{7,4},{8,9},{9,10},{10,1... | collective-permute-start | bytes 786440 | tf_op jit(solution)/shard_map/ppermute | solution.py:685
  22.2 21.4 %collective-permute-start.6 = (bf16[8,128,128]{2,1,0:T(8,128)(2,1)}, bf16[8,128,128]{2,1,0:T(8,128)(2,1)S(1)}, u32[]{:S(2)}, u32[]{:S(2)}) collective-permute-start(bf16[8,128,128]{2,1,0:T(8,128)(2,1)} %get-tuple-element.50), channel_id=1, source_target_pairs={{0,3},{1,0},{2,1},{3,2},{4,7},{5,4},{6,5},{7,6},{8,11},{9,8},{10,9... | collective-permute-start | bytes 786440 | tf_op jit(solution)/shard_map/ppermute | solution.py:685
  24.3 19.4 %collective-permute-start.5 = (bf16[8,128,128]{2,1,0:T(8,128)(2,1)}, bf16[8,128,128]{2,1,0:T(8,128)(2,1)S(1)}, u32[]{:S(2)}, u32[]{:S(2)}) collective-permute-start(bf16[8,128,128]{2,1,0:T(8,128)(2,1)} %get-tuple-element.50), channel_id=1, source_target_pairs={{0,2},{1,3},{2,0},{3,1},{4,6},{5,7},{6,4},{7,5},{8,10},{9,11},{10,... | collective-permute-start | bytes 786440 | tf_op jit(solution)/shard_map/ppermute | solution.py:685
  26.9 18.3 %all-to-all-start.1 = ((bf16[32,16,128]{2,1,0:T(8,128)(2,1)}), bf16[32,16,128]{2,1,0:T(8,128)(2,1)S(1)}, u32[]{:S(2)}, u32[]{:S(2)}) async-start(bf16[32,16,128]{2,1,0:T(8,128)(2,1)} %scan_maps.1), calls=%async_computation.1 | async-start | bytes 262144 | tf_op jit(solution)/shard_map/all_to_all | solution.py:736
  35.9 15.6 %collective-permute-start.8 = (bf16[8,128,128]{2,1,0:T(8,128)(2,1)}, bf16[8,128,128]{2,1,0:T(8,128)(2,1)S(1)}, u32[]{:S(2)}, u32[]{:S(2)}) collective-permute-start(bf16[8,128,128]{2,1,0:T(8,128)(2,1)} %get-tuple-element.50), channel_id=1, source_target_pairs={{0,1},{1,2},{2,3},{3,0},{4,5},{5,6},{6,7},{7,4},{8,9},{9,10},{10,1... | collective-permute-start | bytes 786440 | tf_op jit(solution)/shard_map/ppermute | solution.py:685
  45.2 4.8 %collective-permute-start.7 = (bf16[4,128,128]{2,1,0:T(8,128)(2,1)S(1)}, bf16[4,128,128]{2,1,0:T(8,128)(2,1)S(1)}, u32[]{:S(2)}, u32[]{:S(2)}) collective-permute-start(bf16[4,128,128]{2,1,0:T(8,128)(2,1)S(1)} %bitcast.11), channel_id=1, source_target_pairs={{0,4},{4,0},{8,12},{12,8},{16,20},{20,16},{24,28},{28,24},{32,36},... | collective-permute-start | bytes 393224 | tf_op jit(solution)/shard_map/ppermute | solution.py:740
  51.5 4.9 %collective-permute-start.12 = (bf16[528,128]{1,0:T(8,128)(2,1)S(1)}, bf16[528,128]{1,0:T(8,128)(2,1)S(1)}, u32[]{:S(2)}, u32[]{:S(2)}) collective-permute-start(bf16[528,128]{1,0:T(8,128)(2,1)S(1)} %get-tuple-element.58.lower_0), channel_id=1, source_target_pairs={{0,3},{1,0},{2,1},{3,2},{4,7},{5,4},{6,5},{7,6},{8,11},{9,8},{10,9... | collective-permute-start | bytes 405512 | tf_op jit(solution)/shard_map/ppermute | solution.py:685
  52.0 6.2 %collective-permute-start.9 = (bf16[512,128]{1,0:T(8,128)(2,1)S(1)}, bf16[512,128]{1,0:T(8,128)(2,1)S(1)}, u32[]{:S(2)}, u32[]{:S(2)}) collective-permute-start(bf16[512,128]{1,0:T(8,128)(2,1)S(1)} %get-tuple-element.59), channel_id=1, source_target_pairs={{0,1},{1,2},{2,3},{3,0},{4,5},{5,6},{6,7},{7,4},{8,9},{9,10},{10,1... | collective-permute-start | bytes 393224 | tf_op jit(solution)/shard_map/ppermute | solution.py:685
  53.0 10.9 %collective-permute-start.10 = (bf16[528,128]{1,0:T(8,128)(2,1)S(1)}, bf16[528,128]{1,0:T(8,128)(2,1)S(1)}, u32[]{:S(2)}, u32[]{:S(2)}) collective-permute-start(bf16[528,128]{1,0:T(8,128)(2,1)S(1)} %get-tuple-element.58.lower_0), channel_id=1, source_target_pairs={{0,1},{1,2},{2,3},{3,0},{4,5},{5,6},{6,7},{7,4},{8,9},{9,10},{10,1... | collective-permute-start | bytes 405512 | tf_op jit(solution)/shard_map/ppermute | solution.py:685
  56.4 7.6 %collective-permute-start.13 = (bf16[528,128]{1,0:T(8,128)(2,1)S(1)}, bf16[528,128]{1,0:T(8,128)(2,1)S(1)}, u32[]{:S(2)}, u32[]{:S(2)}) collective-permute-start(bf16[528,128]{1,0:T(8,128)(2,1)S(1)} %collective-permute-done.12.lower_3), channel_id=1, source_target_pairs={{0,3},{1,0},{2,1},{3,2},{4,7},{5,4},{6,5},{7,6},{8,11},{9,8},{10,9... | collective-permute-start | bytes 405512 | tf_op jit(solution)/shard_map/ppermute | solution.py:685
  58.0 5.9 %collective-permute-start.14 = (bf16[512,128]{1,0:T(8,128)(2,1)S(1)}, bf16[512,128]{1,0:T(8,128)(2,1)S(1)}, u32[]{:S(2)}, u32[]{:S(2)}) collective-permute-start(bf16[512,128]{1,0:T(8,128)(2,1)S(1)} %get-tuple-element.59), channel_id=1, source_target_pairs={{0,3},{1,0},{2,1},{3,2},{4,7},{5,4},{6,5},{7,6},{8,11},{9,8},{10,9... | collective-permute-start | bytes 393224 | tf_op jit(solution)/shard_map/ppermute | solution.py:685
  58.2 5.7 %collective-permute-start.11 = (bf16[512,128]{1,0:T(8,128)(2,1)S(1)}, bf16[512,128]{1,0:T(8,128)(2,1)S(1)}, u32[]{:S(2)}, u32[]{:S(2)}) collective-permute-start(bf16[512,128]{1,0:T(8,128)(2,1)S(1)} %collective-permute-done.9.upper_1), channel_id=1, source_target_pairs={{0,1},{1,2},{2,3},{3,0},{4,5},{5,6},{6,7},{7,4},{8,9},{9,10},{10,1... | collective-permute-start | bytes 393224 | tf_op jit(solution)/shard_map/ppermute | solution.py:685
  69.5 4.1 %collective-permute-start.18 = (bf16[528,128]{1,0:T(8,128)(2,1)S(1)}, bf16[528,128]{1,0:T(8,128)(2,1)S(1)}, u32[]{:S(2)}, u32[]{:S(2)}) collective-permute-start(bf16[528,128]{1,0:T(8,128)(2,1)S(1)} %get-tuple-element.69.lower_0), channel_id=1, source_target_pairs={{0,3},{1,0},{2,1},{3,2},{4,7},{5,4},{6,5},{7,6},{8,11},{9,8},{10,9... | collective-permute-start | bytes 405512 | tf_op jit(solution)/shard_map/ppermute | solution.py:685
  71.6 5.1 %collective-permute-start.15 = (bf16[512,128]{1,0:T(8,128)(2,1)S(1)}, bf16[512,128]{1,0:T(8,128)(2,1)S(1)}, u32[]{:S(2)}, u32[]{:S(2)}) collective-permute-start(bf16[512,128]{1,0:T(8,128)(2,1)S(1)} %get-tuple-element.70), channel_id=1, source_target_pairs={{0,1},{1,2},{2,3},{3,0},{4,5},{5,6},{6,7},{7,4},{8,9},{9,10},{10,1... | collective-permute-start | bytes 393224 | tf_op jit(solution)/shard_map/ppermute | solution.py:685
  71.6 11.0 %collective-permute-start.16 = (bf16[528,128]{1,0:T(8,128)(2,1)S(1)}, bf16[528,128]{1,0:T(8,128)(2,1)S(1)}, u32[]{:S(2)}, u32[]{:S(2)}) collective-permute-start(bf16[528,128]{1,0:T(8,128)(2,1)S(1)} %get-tuple-element.69.lower_0), channel_id=1, source_target_pairs={{0,1},{1,2},{2,3},{3,0},{4,5},{5,6},{6,7},{7,4},{8,9},{9,10},{10,1... | collective-permute-start | bytes 405512 | tf_op jit(solution)/shard_map/ppermute | solution.py:685
  73.5 9.0 %collective-permute-start.19 = (bf16[528,128]{1,0:T(8,128)(2,1)S(1)}, bf16[528,128]{1,0:T(8,128)(2,1)S(1)}, u32[]{:S(2)}, u32[]{:S(2)}) collective-permute-start(bf16[528,128]{1,0:T(8,128)(2,1)S(1)} %collective-permute-done.18.lower_3), channel_id=1, source_target_pairs={{0,3},{1,0},{2,1},{3,2},{4,7},{5,4},{6,5},{7,6},{8,11},{9,8},{10,9... | collective-permute-start | bytes 405512 | tf_op jit(solution)/shard_map/ppermute | solution.py:685
  76.6 5.9 %collective-permute-start.20 = (bf16[512,128]{1,0:T(8,128)(2,1)S(1)}, bf16[512,128]{1,0:T(8,128)(2,1)S(1)}, u32[]{:S(2)}, u32[]{:S(2)}) collective-permute-start(bf16[512,128]{1,0:T(8,128)(2,1)S(1)} %get-tuple-element.70), channel_id=1, source_target_pairs={{0,3},{1,0},{2,1},{3,2},{4,7},{5,4},{6,5},{7,6},{8,11},{9,8},{10,9... | collective-permute-start | bytes 393224 | tf_op jit(solution)/shard_map/ppermute | solution.py:685
  76.7 5.9 %collective-permute-start.17 = (bf16[512,128]{1,0:T(8,128)(2,1)S(1)}, bf16[512,128]{1,0:T(8,128)(2,1)S(1)}, u32[]{:S(2)}, u32[]{:S(2)}) collective-permute-start(bf16[512,128]{1,0:T(8,128)(2,1)S(1)} %collective-permute-done.15.upper_1), channel_id=1, source_target_pairs={{0,1},{1,2},{2,3},{3,0},{4,5},{5,6},{6,7},{7,4},{8,9},{9,10},{10,1... | collective-permute-start | bytes 393224 | tf_op jit(solution)/shard_map/ppermute | solution.py:685
  88.2 18.6 %collective-permute-start.25 = (bf16[2,8,128,128]{3,2,1,0:T(8,128)(2,1)S(1)}, bf16[2,8,128,128]{3,2,1,0:T(8,128)(2,1)S(1)}, u32[]{:S(2)}, u32[]{:S(2)}) collective-permute-start(bf16[2,8,128,128]{3,2,1,0:T(8,128)(2,1)S(1)} %near_message.1), channel_id=1, source_target_pairs={{4,0},{8,4},{12,8},{16,12},{20,16},{24,20},{28,24},{32,28},{36,32}... | collective-permute-start | bytes 1572872 | tf_op jit(solution)/shard_map/ppermute | solution.py:758
  100.6 6.2 %collective-permute-start.24 = (bf16[16,128]{1,0:T(8,128)(2,1)S(1)}, bf16[16,128]{1,0:T(8,128)(2,1)S(1)}, u32[]{:S(2)}, u32[]{:S(2)}) collective-permute-start(bf16[16,128]{1,0:T(8,128)(2,1)S(1)} %get-tuple-element.77.factors_ref), channel_id=1, source_target_pairs={{4,0},{8,4},{12,8},{16,12},{20,16},{24,20},{28,24},{32,28},{36,32}... | collective-permute-start | bytes 12296 | tf_op jit(solution)/shard_map/ppermute | solution.py:760
  (8 other events, 64.9 us)

commit v4 on v3

--- a/solution.py
+++ b/solution.py
@@ -42,10 +42,12 @@
     psi_hbm,
     h_hbm,
     d_hbm,
+    precond_hbm,
     plan,
     out_ref,
     h_ref,
     d_ref,
+    precond_ref,
     slot_sector,
     pair_table,
     sizes,
@@ -66,6 +68,7 @@
         (psi_hbm, psi_ref),
         (d_hbm, d_ref),
         (h_hbm.at[pl.ds(core * (slots // 2), slots // 2)], h_ref),
+        (precond_hbm, precond_ref),
     )
     fetches = [pltpu.make_async_copy(a, b, sem.at[k]) for k, (a, b) in enumerate(moves)]
     for fetch in fetches:
@@ -97,7 +100,7 @@
         fetch.wait()
 
 
-def start(slot_sector, pair_table, sizes, ranks, psi, own_h, own_d):
+def start(slot_sector, pair_table, sizes, ranks, psi, own_h, own_d, precond):
     pairs = pair_table.T
     terms = pairs.shape[0]
     slots = psi.shape[0]
@@ -109,30 +112,24 @@
             jax.ShapeDtypeStruct(psi.shape, BF16),
             jax.ShapeDtypeStruct((slots // 2, *psi.shape[1:]), F32),
             jax.ShapeDtypeStruct(own_d.shape, F32),
-        ],
-        in_specs=[whole(HBM)] * 7,
-        out_specs=[whole(SMEM), whole(), whole(), whole()],
+            pltpu.VMEM(precond.shape, F32),
+        ],
+        in_specs=[whole(HBM)] * 8,
+        out_specs=[whole(SMEM), whole(), whole(), whole(), whole()],
         scratch_shapes=[pltpu.SMEM(t.shape, jnp.int32) for t in tables]
         + [
             pltpu.SMEM(slot_sector.shape, jnp.int32),
             pltpu.VMEM(psi.shape, BF16),
-            pltpu.SemaphoreType.DMA((7,)),
+            pltpu.SemaphoreType.DMA((8,)),
         ],
         compiler_params=params(),
         cost_estimate=cost(4 * psi.size, 4 * psi.size),
         name="start",
-    )(*[in_hbm(t) for t in (*tables, psi, own_h, own_d)])
-
-
-def half_kernel(precond_hbm, out_ref, half_ref, precond_ref, sem):
-    slots = precond_ref.shape[0]
-    fetches = [
-        pltpu.make_async_copy(precond_hbm.at[j], precond_ref.at[j], sem.at[j]) for j in range(slots)
-    ]
-    for fetch in fetches:
-        fetch.start()
-    for j in range(slots):
-        fetches[j].wait()
+    )(*[in_hbm(t) for t in (*tables, psi, own_h, own_d, precond)])
+
+
+def half_kernel(precond_ref, out_ref, half_ref):
+    for j in range(precond_ref.shape[0]):
         half = DAMPING / precond_ref[j]
         half_ref[j] = half
         out_ref[j] = half.astype(BF16)
@@ -146,13 +143,12 @@
             jax.ShapeDtypeStruct((slots, cap, cap), BF16),
             jax.ShapeDtypeStruct((slots, cap, cap), F32),
         ],
-        in_specs=[whole(HBM)],
+        in_specs=[whole()],
         out_specs=[whole(), whole()],
-        scratch_shapes=[pltpu.VMEM(precond.shape, F32), pltpu.SemaphoreType.DMA((slots,))],
         compiler_params=params(),
         cost_estimate=cost(2 * slots * cap * cap, 100 * slots * cap * cap),
         name="half_message",
-    )(in_hbm(precond))
+    )(precond)
 
 
 def chip_kernel(own_h, other_h, own_d, other_d, out_ref, late_t):
@@ -689,14 +685,17 @@
     return [around(value, shift) for shift in (1, 2, 3)]
 
 
-def pass_on(upper, lower):
+def pass_on(upper, lower, beside):
     upper_1 = around(upper, 1)
     lower_3 = around(lower, 3)
     lower_1 = around(lower, 1)
     upper_3 = around(upper, 3)
+    done = list(beside())
+    lower_3, done[0] = lax.optimization_barrier((lower_3, done[0]))
+    upper_1, upper_3 = lax.optimization_barrier((upper_1, upper_3))
     upper_2 = around(upper_1, 1)
     lower_2 = around(lower_3, 3)
-    return [upper_1, lower_1, upper_2, lower_2, upper_3, lower_3]
+    return [upper_1, lower_1, upper_2, lower_2, upper_3, lower_3], done
 
 
 def shards(
@@ -721,13 +720,13 @@
     swap = [(i, i ^ 1) for i in range(sections)]
     other_h = lax.ppermute(source_h[0], "sect", swap)
     other_d = lax.ppermute(decay[0], "sect", swap)
-    plan, own_psi, own_h, own_d = start(
-        slot_sector, pair_table, sector_sizes, ranks, psi_guess[0], source_h[0], decay[0]
+    plan, own_psi, own_h, own_d, near_precond = start(
+        slot_sector, pair_table, sector_sizes, ranks, psi_guess[0], source_h[0], decay[0], precond[0]
     )
     maps = chip_maps(own_h, other_h, own_d, other_d, chips)
     groups = [[2 * q + c for q in range(chips)] for c in range(2)]
     got_maps = lax.all_to_all(maps, "sect", 0, 0, tiled=True, axis_index_groups=groups)
-    own_psi, late_precond, _ = lax.optimization_barrier((own_psi, precond[0], maps))
+    own_psi, late_precond, _ = lax.optimization_barrier((own_psi, near_precond, maps))
     got_psi = three(own_psi)
     own_half, half = half_message(late_precond)
     halves = three(own_half)
@@ -744,9 +743,10 @@
     lower, halves[0] = lax.optimization_barrier((lower, halves[0]))
     for step in range(1, STEPS):
         last = step == STEPS - 1
-        got = pass_on(upper, lower)
         later_left, later_right, _ = lax.optimization_barrier((left, right, lower))
-        far_b, later_left = ready_left(halves, psi, later_left)
+        got, (far_b, later_left) = pass_on(
+            upper, lower, functools.partial(ready_left, halves, psi, later_left)
+        )
         later_right = ready_right(later_right)
         psi, a_own, *sent = later_step(
             plan, entries, a_own, lower, got, far_b, psi, env_low, half, later_left, later_right, last

time: 108 us -> 106 us (0.981)
  starting transfers between devices: 55.4 us -> 52.7 us
  waiting for transfers between devices: 13.5 us -> 15.5 us
    ppermute x21, waiting for transfers between devices: 9 us -> 11.6 us  [around(): lax.ppermute(value, 'blk', [(i, (i + shift) % count) for i in range(count)])]
    ppermute x21, starting transfers between devices: 20.8 us -> 18.7 us  [around(): lax.ppermute(value, 'blk', [(i, (i + shift) % count) for i in range(count)])]
    all_to_all x1, starting transfers between devices: 9.02 us -> 7.86 us  [shards(): lax.all_to_all(env, 'sect', 0, 0, tiled=True, axis_index_groups=groups)]
    all_to_all x1, waiting for transfers between devices: 0.21 us -> 1.36 us  [shards(): lax.all_to_all(maps, 'sect', 0, 0, tiled=True, axis_index_groups=groups)]
    all_to_all x1, waiting for transfers between devices: 1.49 us -> 0.41 us  [shards(): lax.all_to_all(env, 'sect', 0, 0, tiled=True, axis_index_groups=groups)]
  transfers between devices with their start and end apart: 28 -> 28, of which waited for: 9 -> 12; matrix products, arithmetic and copies ran while one was open for 0% -> 0% of each run, Pallas kernels for 22% -> 22%
where the time goes in v4:
time: 106 us
  starting transfers between devices  52.7 us (50%)
  Pallas kernels  36.1 us (34%)
  waiting for transfers between devices  15.5 us (15%)
    ppermute x21, starting transfers between devices, around(): lax.ppermute(value, 'blk', [(i, (i + shift) % count) for i in range(count)])  18.7 us
    ppermute x21, waiting for transfers between devices, around(): lax.ppermute(value, 'blk', [(i, (i + shift) % count) for i in range(count)])  11.6 us
    pallas_call x2, Pallas kernels, later_step(): pl.pallas_call(functools.partial(later_kernel, last, entries), out_shape=...  11.1 us
    all_to_all x1, starting transfers between devices, shards(): lax.all_to_all(maps, 'sect', 0, 0, tiled=True, axis_index_groups=groups)  9.3 us
    all_to_all x1, starting transfers between devices, shards(): lax.all_to_all(env, 'sect', 0, 0, tiled=True, axis_index_groups=groups)  7.86 us
    ppermute x1, starting transfers between devices, shards(): near = lax.ppermute(near, 'sect', behind)  6.9 us
    pallas_call x1, Pallas kernels, first_products(): pl.pallas_call(first_kernel, out_shape=[jax.ShapeDtypeStruct((4 * slots,...  6.84 us
    pallas_call x2, Pallas kernels, ready_right(): pl.pallas_call(copy_kernel, out_shape=pltpu.VMEM(right.shape, BF16), in_s...  4.39 us
  transfers between devices with their start and end apart: 28, of which 12 were waited for; matrix products, arithmetic and copies ran while one was open for 0% of the time, Pallas kernels for 22%

profile of v4, /device:TPU:1, one launch (start us, length us, event | category | flops | bytes accessed | tf_op | source)
XLA Modules:
  0.0 105.9 jit_solution(1675296327692094777)
XLA Ops:
  0.6 3.3 %collective-permute-start = (f32[8,128,128]{2,1,0:T(8,128)}, f32[8,128,128]{2,1,0:T(8,128)S(1)}, u32[]{:S(2)}, u32[]{:S(2)}) collective-permute-start(f32[8,128,128]{2,1,0:T(8,128)} %bitcast.21), channel_id=1, source_target_pairs={{0,4},{4,0},{8,12},{12,8},{16,20},{20,16},{24,28},{28,24},{32,36},... | collective-permute-start | bytes 1572872 | tf_op jit(solution)/shard_map/ppermute | solution.py:721
  4.1 2.2 %start.1 = (s32[256]{0:T(256)S(1)}, bf16[8,128,128]{2,1,0:T(8,128)(2,1)S(1)}, f32[4,128,128]{2,1,0:T(8,128)S(1)}, f32[8,128]{1,0:T(8,128)S(1)}, f32[8,128,128]{2,1,0:T(8,128)S(1)}) custom-call(s32[32]{0:T(128)} %slot_hbm.1, s32[16,32]{1,0:T(8,128)} %bitcast.25, s32[1,32]{1,0:T(1,128)} %sizes_hbm.1, s32[1,32]{1,0:T(1,128)} %ranks_hbm.1, ...), custom_call_target="tpu_custom_call" | custom-call | flops 524288 | bytes 524288 | tf_op jit(solution)/shard_map/start/pallas_call | solution.py:108
  7.2 9.3 %all-to-all-start = ((bf16[32,24,128]{2,1,0:T(8,128)(2,1)}), bf16[32,24,128]{2,1,0:T(8,128)(2,1)S(1)}, u32[]{:S(2)}, u32[]{:S(2)}) async-start(bf16[32,24,128]{2,1,0:T(8,128)(2,1)} %chip_maps.1), calls=%async_computation | async-start | bytes 393216 | tf_op jit(solution)/shard_map/all_to_all | solution.py:728
  16.5 2.8 %collective-permute-start.4 = (bf16[8,128,128]{2,1,0:T(8,128)(2,1)S(1)}, bf16[8,128,128]{2,1,0:T(8,128)(2,1)}, u32[]{:S(2)}, u32[]{:S(2)}) collective-permute-start(bf16[8,128,128]{2,1,0:T(8,128)(2,1)S(1)} %get-tuple-element.57.psi_0), channel_id=1, source_target_pairs={{0,3},{1,0},{2,1},{3,2},{4,7},{5,4},{6,5},{7,6},{8,11},{9,8},{10,9... | collective-permute-start | bytes 786440 | tf_op jit(solution)/shard_map/ppermute | solution.py:681
  21.2 2.0 %collective-permute-start.6 = (bf16[8,128,128]{2,1,0:T(8,128)(2,1)}, bf16[8,128,128]{2,1,0:T(8,128)(2,1)S(1)}, u32[]{:S(2)}, u32[]{:S(2)}) collective-permute-start(bf16[8,128,128]{2,1,0:T(8,128)(2,1)} %get-tuple-element.60), channel_id=1, source_target_pairs={{0,3},{1,0},{2,1},{3,2},{4,7},{5,4},{6,5},{7,6},{8,11},{9,8},{10,9... | collective-permute-start | bytes 786440 | tf_op jit(solution)/shard_map/ppermute | solution.py:681
  23.2 1.4 %collective-permute-start.5 = (bf16[8,128,128]{2,1,0:T(8,128)(2,1)}, bf16[8,128,128]{2,1,0:T(8,128)(2,1)S(1)}, u32[]{:S(2)}, u32[]{:S(2)}) collective-permute-start(bf16[8,128,128]{2,1,0:T(8,128)(2,1)} %get-tuple-element.60), channel_id=1, source_target_pairs={{0,2},{1,3},{2,0},{3,1},{4,6},{5,7},{6,4},{7,5},{8,10},{9,11},{10,... | collective-permute-start | bytes 786440 | tf_op jit(solution)/shard_map/ppermute | solution.py:681
  26.9 7.9 %all-to-all-start.1 = ((bf16[32,16,128]{2,1,0:T(8,128)(2,1)}), bf16[32,16,128]{2,1,0:T(8,128)(2,1)S(1)}, u32[]{:S(2)}, u32[]{:S(2)}) async-start(bf16[32,16,128]{2,1,0:T(8,128)(2,1)} %scan_maps.1), calls=%async_computation.1 | async-start | bytes 262144 | tf_op jit(solution)/shard_map/all_to_all | solution.py:735
  36.7 6.8 %first_products.1 = (bf16[32,128,128]{2,1,0:T(8,128)(2,1)S(1)}, f32[8,128,128]{2,1,0:T(8,128)S(1)}) custom-call(s32[256]{0:T(256)S(1)} %get-tuple-element.52.plan, bf16[8,128,128]{2,1,0:T(8,128)(2,1)} %copy-done, bf16[8,128,128]{2,1,0:T(8,128)(2,1)} %copy-done.3, bf16[8,128,128]{2,1,0:T(8,128)(2,1)} %copy-done.2, ...), custom_call_target="tpu_custom_call" | custom-call | flops 2097152 | bytes 131072 | tf_op jit(solution)/shard_map/first_products/pallas_call | solution.py:478
  44.0 3.8 %collective-permute-start.7 = (bf16[4,128,128]{2,1,0:T(8,128)(2,1)S(1)}, bf16[4,128,128]{2,1,0:T(8,128)(2,1)S(1)}, u32[]{:S(2)}, u32[]{:S(2)}) collective-permute-start(bf16[4,128,128]{2,1,0:T(8,128)(2,1)S(1)} %bitcast.11), channel_id=1, source_target_pairs={{0,4},{4,0},{8,12},{12,8},{16,20},{20,16},{24,28},{28,24},{32,36},... | collective-permute-start | bytes 393224 | tf_op jit(solution)/shard_map/ppermute | solution.py:739
  48.8 1.5 %first_close.1 = (bf16[8,128,128]{2,1,0:T(8,128)(2,1)S(1)}, f32[8,128,128]{2,1,0:T(8,128)S(1)}, bf16[512,128]{1,0:T(8,128)(2,1)S(1)}, bf16[528,128]{1,0:T(8,128)(2,1)S(1)}) custom-call(s32[256]{0:T(256)S(1)} %get-tuple-element.52.plan, bf16[32,128,128]{2,1,0:T(8,128)(2,1)S(1)} %get-tuple-element.58.psi_ref.before, ...), custom_call_target="tpu_custom_call" | custom-call | flops 33554432 | bytes 2621440 | tf_op jit(solution)/shard_map/first_close/pallas_call | solution.py:548
  50.9 1.4 %collective-permute-start.10 = (bf16[512,128]{1,0:T(8,128)(2,1)S(1)}, bf16[512,128]{1,0:T(8,128)(2,1)S(1)}, u32[]{:S(2)}, u32[]{:S(2)}) collective-permute-start(bf16[512,128]{1,0:T(8,128)(2,1)S(1)} %get-tuple-element.69), channel_id=1, source_target_pairs={{0,3},{1,0},{2,1},{3,2},{4,7},{5,4},{6,5},{7,6},{8,11},{9,8},{10,9... | collective-permute-start | bytes 393224 | tf_op jit(solution)/shard_map/ppermute | solution.py:681
  53.4 2.2 %ready_left.2 = (bf16[24,128,128]{2,1,0:T(8,128)(2,1)S(1)}, bf16[8,16,128,128]{3,2,1,0:T(8,128)(2,1)S(1)}) custom-call(bf16[8,128,128]{2,1,0:T(8,128)(2,1)S(1)} %collective-permute-done.8.half_1, bf16[8,128,128]{2,1,0:T(8,128)(2,1)S(1)} %collective-permute-done.5.half_2, bf16[8,128,128]{2,1,0:T(8,128)(2,1)S(1)} %collective-permute-done.6.half_3, ...), custom_call_target="tpu_custom_call" | custom-call | flops 393216 | bytes 4194304 | tf_op jit(solution)/shard_map/ready_left/pallas_call | solution.py:512
  55.6 1.7 %collective-permute-start.14 = (bf16[528,128]{1,0:T(8,128)(2,1)S(1)}, bf16[528,128]{1,0:T(8,128)(2,1)S(1)}, u32[]{:S(2)}, u32[]{:S(2)}) collective-permute-start(bf16[528,128]{1,0:T(8,128)(2,1)S(1)} %collective-permute-done.13.lower_3), channel_id=1, source_target_pairs={{0,3},{1,0},{2,1},{3,2},{4,7},{5,4},{6,5},{7,6},{8,11},{9,8},{10,9... | collective-permute-start | bytes 405512 | tf_op jit(solution)/shard_map/ppermute | solution.py:681
  58.1 2.2 %ready_right.2.right_ref = bf16[8,16,128,128]{3,2,1,0:T(8,128)(2,1)S(1)} custom-call(bf16[8,16,128,128]{3,2,1,0:T(8,128)(2,1)} %bitcast.18), custom_call_target="tpu_custom_call" | custom-call | flops 2097152 | bytes 4194304 | tf_op jit(solution)/shard_map/ready_right/pallas_call | solution.py:534
  60.5 2.6 %collective-permute-done.12.upper_2 = bf16[512,128]{1,0:T(8,128)(2,1)S(1)} collective-permute-done((bf16[512,128]{1,0:T(8,128)(2,1)S(1)}, bf16[512,128]{1,0:T(8,128)(2,1)S(1)}, u32[]{:S(2)}, u32[]{:S(2)}) %collective-permute-start.12) | collective-permute-done | bytes 131104 | tf_op jit(solution)/shard_map/ppermute | solution.py:681
  63.1 5.5 %later_step.1 = (bf16[32,128,128]{2,1,0:T(8,128)(2,1)S(1)}, f32[8,128,128]{2,1,0:T(8,128)S(1)}, bf16[512,128]{1,0:T(8,128)(2,1)S(1)}, bf16[528,128]{1,0:T(8,128)(2,1)S(1)}) custom-call(s32[256]{0:T(256)S(1)} %get-tuple-element.52.plan, f32[8,128,128]{2,1,0:T(8,128)S(1)} %get-tuple-element.66.a_own, bf16[528,128]{1,0:T(8,128)(2,1)S(1)} %get-tuple-element.68.lower_0, ...), custom_call_target="tpu_custom_call" | custom-call | flops 1073741824 | bytes 25165824 | tf_op jit(solution)/shard_map/later_step/pallas_call | solution.py:574
  71.6 2.2 %ready_left.3 = (bf16[24,128,128]{2,1,0:T(8,128)(2,1)S(1)}, bf16[8,16,128,128]{3,2,1,0:T(8,128)(2,1)S(1)}) custom-call(bf16[8,128,128]{2,1,0:T(8,128)(2,1)S(1)} %collective-permute-done.8.half_1, bf16[8,128,128]{2,1,0:T(8,128)(2,1)S(1)} %collective-permute-done.5.half_2, bf16[8,128,128]{2,1,0:T(8,128)(2,1)S(1)} %collective-permute-done.6.half_3, ...), custom_call_target="tpu_custom_call" | custom-call | flops 393216 | bytes 4194304 | tf_op jit(solution)/shard_map/ready_left/pallas_call | solution.py:512
  73.8 2.0 %collective-permute-start.20 = (bf16[528,128]{1,0:T(8,128)(2,1)S(1)}, bf16[528,128]{1,0:T(8,128)(2,1)S(1)}, u32[]{:S(2)}, u32[]{:S(2)}) collective-permute-start(bf16[528,128]{1,0:T(8,128)(2,1)S(1)} %collective-permute-done.19.lower_3), channel_id=1, source_target_pairs={{0,3},{1,0},{2,1},{3,2},{4,7},{5,4},{6,5},{7,6},{8,11},{9,8},{10,9... | collective-permute-start | bytes 405512 | tf_op jit(solution)/shard_map/ppermute | solution.py:681
  75.9 2.2 %ready_right.3.right_ref = bf16[8,16,128,128]{3,2,1,0:T(8,128)(2,1)S(1)} custom-call(bf16[8,16,128,128]{3,2,1,0:T(8,128)(2,1)} %bitcast.19), custom_call_target="tpu_custom_call" | custom-call | flops 2097152 | bytes 4194304 | tf_op jit(solution)/shard_map/ready_right/pallas_call | solution.py:534
  78.1 3.6 %collective-permute-done.18.upper_2 = bf16[512,128]{1,0:T(8,128)(2,1)S(1)} collective-permute-done((bf16[512,128]{1,0:T(8,128)(2,1)S(1)}, bf16[512,128]{1,0:T(8,128)(2,1)S(1)}, u32[]{:S(2)}, u32[]{:S(2)}) %collective-permute-start.18) | collective-permute-done | bytes 131104 | tf_op jit(solution)/shard_map/ppermute | solution.py:681
  81.7 5.6 %last_step.1 = (bf16[32,128,128]{2,1,0:T(8,128)(2,1)S(1)}, f32[8,128,128]{2,1,0:T(8,128)S(1)}, bf16[16,128]{1,0:T(8,128)(2,1)S(1)}) custom-call(s32[256]{0:T(256)S(1)} %get-tuple-element.52.plan, f32[8,128,128]{2,1,0:T(8,128)S(1)} %get-tuple-element.82.a_own, bf16[528,128]{1,0:T(8,128)(2,1)S(1)} %get-tuple-element.83.lower_0, ...), custom_call_target="tpu_custom_call" | custom-call | flops 1073741824 | bytes 25165824 | tf_op jit(solution)/shard_map/last_step/pallas_call | solution.py:574
  87.3 6.9 %collective-permute-start.25 = (bf16[2,8,128,128]{3,2,1,0:T(8,128)(2,1)S(1)}, bf16[2,8,128,128]{3,2,1,0:T(8,128)(2,1)S(1)}, u32[]{:S(2)}, u32[]{:S(2)}) collective-permute-start(bf16[2,8,128,128]{3,2,1,0:T(8,128)(2,1)S(1)} %near_message.1), channel_id=1, source_target_pairs={{4,0},{8,4},{12,8},{16,12},{20,16},{24,20},{28,24},{32,28},{36,32}... | collective-permute-start | bytes 1572872 | tf_op jit(solution)/shard_map/ppermute | solution.py:758
  96.9 1.6 %collective-permute-done.22.tile_2 = bf16[16,128]{1,0:T(8,128)(2,1)S(1)} collective-permute-done((bf16[16,128]{1,0:T(8,128)(2,1)S(1)}, bf16[16,128]{1,0:T(8,128)(2,1)S(1)}, u32[]{:S(2)}, u32[]{:S(2)}) %collective-permute-start.22) | collective-permute-done | bytes 4128 | tf_op jit(solution)/shard_map/ppermute | solution.py:681
  99.7 2.7 %collective-permute-start.24 = (bf16[16,128]{1,0:T(8,128)(2,1)S(1)}, bf16[16,128]{1,0:T(8,128)(2,1)S(1)}, u32[]{:S(2)}, u32[]{:S(2)}) collective-permute-start(bf16[16,128]{1,0:T(8,128)(2,1)S(1)} %get-tuple-element.95.factors_ref), channel_id=1, source_target_pairs={{4,0},{8,4},{12,8},{16,12},{20,16},{24,20},{28,24},{32,28},{36,32}... | collective-permute-start | bytes 12296 | tf_op jit(solution)/shard_map/ppermute | solution.py:760
  (56 shorter events, 21.6 us)
Async XLA Ops:
  0.6 5.6 %collective-permute-start = (f32[8,128,128]{2,1,0:T(8,128)}, f32[8,128,128]{2,1,0:T(8,128)S(1)}, u32[]{:S(2)}, u32[]{:S(2)}) collective-permute-start(f32[8,128,128]{2,1,0:T(8,128)} %bitcast.21), channel_id=1, source_target_pairs={{0,4},{4,0},{8,12},{12,8},{16,20},{20,16},{24,28},{28,24},{32,36},... | collective-permute-start | bytes 1572872 | tf_op jit(solution)/shard_map/ppermute | solution.py:721
  7.2 18.7 %all-to-all-start = ((bf16[32,24,128]{2,1,0:T(8,128)(2,1)}), bf16[32,24,128]{2,1,0:T(8,128)(2,1)S(1)}, u32[]{:S(2)}, u32[]{:S(2)}) async-start(bf16[32,24,128]{2,1,0:T(8,128)(2,1)} %chip_maps.1), calls=%async_computation | async-start | bytes 393216 | tf_op jit(solution)/shard_map/all_to_all | solution.py:728
  16.5 18.2 %collective-permute-start.4 = (bf16[8,128,128]{2,1,0:T(8,128)(2,1)S(1)}, bf16[8,128,128]{2,1,0:T(8,128)(2,1)}, u32[]{:S(2)}, u32[]{:S(2)}) collective-permute-start(bf16[8,128,128]{2,1,0:T(8,128)(2,1)S(1)} %get-tuple-element.57.psi_0), channel_id=1, source_target_pairs={{0,3},{1,0},{2,1},{3,2},{4,7},{5,4},{6,5},{7,6},{8,11},{9,8},{10,9... | collective-permute-start | bytes 786440 | tf_op jit(solution)/shard_map/ppermute | solution.py:681
  19.4 15.5 %collective-permute-start.3 = (bf16[8,128,128]{2,1,0:T(8,128)(2,1)S(1)}, bf16[8,128,128]{2,1,0:T(8,128)(2,1)S(1)}, u32[]{:S(2)}, u32[]{:S(2)}) collective-permute-start(bf16[8,128,128]{2,1,0:T(8,128)(2,1)S(1)} %get-tuple-element.57.psi_0), channel_id=1, source_target_pairs={{0,2},{1,3},{2,0},{3,1},{4,6},{5,7},{6,4},{7,5},{8,10},{9,11},{10,... | collective-permute-start | bytes 786440 | tf_op jit(solution)/shard_map/ppermute | solution.py:681
  19.7 16.3 %collective-permute-start.2 = (bf16[8,128,128]{2,1,0:T(8,128)(2,1)S(1)}, bf16[8,128,128]{2,1,0:T(8,128)(2,1)S(1)}, u32[]{:S(2)}, u32[]{:S(2)}) collective-permute-start(bf16[8,128,128]{2,1,0:T(8,128)(2,1)S(1)} %get-tuple-element.57.psi_0), channel_id=1, source_target_pairs={{0,1},{1,2},{2,3},{3,0},{4,5},{5,6},{6,7},{7,4},{8,9},{9,10},{10,1... | collective-permute-start | bytes 786440 | tf_op jit(solution)/shard_map/ppermute | solution.py:681
  21.2 22.4 %collective-permute-start.6 = (bf16[8,128,128]{2,1,0:T(8,128)(2,1)}, bf16[8,128,128]{2,1,0:T(8,128)(2,1)S(1)}, u32[]{:S(2)}, u32[]{:S(2)}) collective-permute-start(bf16[8,128,128]{2,1,0:T(8,128)(2,1)} %get-tuple-element.60), channel_id=1, source_target_pairs={{0,3},{1,0},{2,1},{3,2},{4,7},{5,4},{6,5},{7,6},{8,11},{9,8},{10,9... | collective-permute-start | bytes 786440 | tf_op jit(solution)/shard_map/ppermute | solution.py:681
  23.2 20.4 %collective-permute-start.5 = (bf16[8,128,128]{2,1,0:T(8,128)(2,1)}, bf16[8,128,128]{2,1,0:T(8,128)(2,1)S(1)}, u32[]{:S(2)}, u32[]{:S(2)}) collective-permute-start(bf16[8,128,128]{2,1,0:T(8,128)(2,1)} %get-tuple-element.60), channel_id=1, source_target_pairs={{0,2},{1,3},{2,0},{3,1},{4,6},{5,7},{6,4},{7,5},{8,10},{9,11},{10,... | collective-permute-start | bytes 786440 | tf_op jit(solution)/shard_map/ppermute | solution.py:681
  26.9 17.1 %all-to-all-start.1 = ((bf16[32,16,128]{2,1,0:T(8,128)(2,1)}), bf16[32,16,128]{2,1,0:T(8,128)(2,1)S(1)}, u32[]{:S(2)}, u32[]{:S(2)}) async-start(bf16[32,16,128]{2,1,0:T(8,128)(2,1)} %scan_maps.1), calls=%async_computation.1 | async-start | bytes 262144 | tf_op jit(solution)/shard_map/all_to_all | solution.py:735
  34.8 15.6 %collective-permute-start.8 = (bf16[8,128,128]{2,1,0:T(8,128)(2,1)}, bf16[8,128,128]{2,1,0:T(8,128)(2,1)S(1)}, u32[]{:S(2)}, u32[]{:S(2)}) collective-permute-start(bf16[8,128,128]{2,1,0:T(8,128)(2,1)} %get-tuple-element.60), channel_id=1, source_target_pairs={{0,1},{1,2},{2,3},{3,0},{4,5},{5,6},{6,7},{7,4},{8,9},{9,10},{10,1... | collective-permute-start | bytes 786440 | tf_op jit(solution)/shard_map/ppermute | solution.py:681
  44.0 4.8 %collective-permute-start.7 = (bf16[4,128,128]{2,1,0:T(8,128)(2,1)S(1)}, bf16[4,128,128]{2,1,0:T(8,128)(2,1)S(1)}, u32[]{:S(2)}, u32[]{:S(2)}) collective-permute-start(bf16[4,128,128]{2,1,0:T(8,128)(2,1)S(1)} %bitcast.11), channel_id=1, source_target_pairs={{0,4},{4,0},{8,12},{12,8},{16,20},{20,16},{24,28},{28,24},{32,36},... | collective-permute-start | bytes 393224 | tf_op jit(solution)/shard_map/ppermute | solution.py:739
  50.3 5.2 %collective-permute-start.13 = (bf16[528,128]{1,0:T(8,128)(2,1)S(1)}, bf16[528,128]{1,0:T(8,128)(2,1)S(1)}, u32[]{:S(2)}, u32[]{:S(2)}) collective-permute-start(bf16[528,128]{1,0:T(8,128)(2,1)S(1)} %get-tuple-element.68.lower_0), channel_id=1, source_target_pairs={{0,3},{1,0},{2,1},{3,2},{4,7},{5,4},{6,5},{7,6},{8,11},{9,8},{10,9... | collective-permute-start | bytes 405512 | tf_op jit(solution)/shard_map/ppermute | solution.py:681
  50.9 7.2 %collective-permute-start.10 = (bf16[512,128]{1,0:T(8,128)(2,1)S(1)}, bf16[512,128]{1,0:T(8,128)(2,1)S(1)}, u32[]{:S(2)}, u32[]{:S(2)}) collective-permute-start(bf16[512,128]{1,0:T(8,128)(2,1)S(1)} %get-tuple-element.69), channel_id=1, source_target_pairs={{0,3},{1,0},{2,1},{3,2},{4,7},{5,4},{6,5},{7,6},{8,11},{9,8},{10,9... | collective-permute-start | bytes 393224 | tf_op jit(solution)/shard_map/ppermute | solution.py:681
  52.3 5.8 %collective-permute-start.9 = (bf16[512,128]{1,0:T(8,128)(2,1)S(1)}, bf16[512,128]{1,0:T(8,128)(2,1)S(1)}, u32[]{:S(2)}, u32[]{:S(2)}) collective-permute-start(bf16[512,128]{1,0:T(8,128)(2,1)S(1)} %get-tuple-element.69), channel_id=1, source_target_pairs={{0,1},{1,2},{2,3},{3,0},{4,5},{5,6},{6,7},{7,4},{8,9},{9,10},{10,1... | collective-permute-start | bytes 393224 | tf_op jit(solution)/shard_map/ppermute | solution.py:681
  52.3 8.1 %collective-permute-start.11 = (bf16[528,128]{1,0:T(8,128)(2,1)S(1)}, bf16[528,128]{1,0:T(8,128)(2,1)S(1)}, u32[]{:S(2)}, u32[]{:S(2)}) collective-permute-start(bf16[528,128]{1,0:T(8,128)(2,1)S(1)} %get-tuple-element.68.lower_0), channel_id=1, source_target_pairs={{0,1},{1,2},{2,3},{3,0},{4,5},{5,6},{6,7},{7,4},{8,9},{9,10},{10,1... | collective-permute-start | bytes 405512 | tf_op jit(solution)/shard_map/ppermute | solution.py:681
  55.6 7.5 %collective-permute-start.14 = (bf16[528,128]{1,0:T(8,128)(2,1)S(1)}, bf16[528,128]{1,0:T(8,128)(2,1)S(1)}, u32[]{:S(2)}, u32[]{:S(2)}) collective-permute-start(bf16[528,128]{1,0:T(8,128)(2,1)S(1)} %collective-permute-done.13.lower_3), channel_id=1, source_target_pairs={{0,3},{1,0},{2,1},{3,2},{4,7},{5,4},{6,5},{7,6},{8,11},{9,8},{10,9... | collective-permute-start | bytes 405512 | tf_op jit(solution)/shard_map/ppermute | solution.py:681
  58.0 5.0 %collective-permute-start.12 = (bf16[512,128]{1,0:T(8,128)(2,1)S(1)}, bf16[512,128]{1,0:T(8,128)(2,1)S(1)}, u32[]{:S(2)}, u32[]{:S(2)}) collective-permute-start(bf16[512,128]{1,0:T(8,128)(2,1)S(1)} %collective-permute-done.9.upper_1), channel_id=1, source_target_pairs={{0,1},{1,2},{2,3},{3,0},{4,5},{5,6},{6,7},{7,4},{8,9},{9,10},{10,1... | collective-permute-start | bytes 393224 | tf_op jit(solution)/shard_map/ppermute | solution.py:681
  68.6 5.2 %collective-permute-start.19 = (bf16[528,128]{1,0:T(8,128)(2,1)S(1)}, bf16[528,128]{1,0:T(8,128)(2,1)S(1)}, u32[]{:S(2)}, u32[]{:S(2)}) collective-permute-start(bf16[528,128]{1,0:T(8,128)(2,1)S(1)} %get-tuple-element.83.lower_0), channel_id=1, source_target_pairs={{0,3},{1,0},{2,1},{3,2},{4,7},{5,4},{6,5},{7,6},{8,11},{9,8},{10,9... | collective-permute-start | bytes 405512 | tf_op jit(solution)/shard_map/ppermute | solution.py:681
  69.4 6.4 %collective-permute-start.16 = (bf16[512,128]{1,0:T(8,128)(2,1)S(1)}, bf16[512,128]{1,0:T(8,128)(2,1)S(1)}, u32[]{:S(2)}, u32[]{:S(2)}) collective-permute-start(bf16[512,128]{1,0:T(8,128)(2,1)S(1)} %get-tuple-element.84), channel_id=1, source_target_pairs={{0,3},{1,0},{2,1},{3,2},{4,7},{5,4},{6,5},{7,6},{8,11},{9,8},{10,9... | collective-permute-start | bytes 393224 | tf_op jit(solution)/shard_map/ppermute | solution.py:681
  69.6 6.2 %collective-permute-start.15 = (bf16[512,128]{1,0:T(8,128)(2,1)S(1)}, bf16[512,128]{1,0:T(8,128)(2,1)S(1)}, u32[]{:S(2)}, u32[]{:S(2)}) collective-permute-start(bf16[512,128]{1,0:T(8,128)(2,1)S(1)} %get-tuple-element.84), channel_id=1, source_target_pairs={{0,1},{1,2},{2,3},{3,0},{4,5},{5,6},{6,7},{7,4},{8,9},{9,10},{10,1... | collective-permute-start | bytes 393224 | tf_op jit(solution)/shard_map/ppermute | solution.py:681
  70.9 7.2 %collective-permute-start.17 = (bf16[528,128]{1,0:T(8,128)(2,1)S(1)}, bf16[528,128]{1,0:T(8,128)(2,1)S(1)}, u32[]{:S(2)}, u32[]{:S(2)}) collective-permute-start(bf16[528,128]{1,0:T(8,128)(2,1)S(1)} %get-tuple-element.83.lower_0), channel_id=1, source_target_pairs={{0,1},{1,2},{2,3},{3,0},{4,5},{5,6},{6,7},{7,4},{8,9},{9,10},{10,1... | collective-permute-start | bytes 405512 | tf_op jit(solution)/shard_map/ppermute | solution.py:681
  73.8 7.8 %collective-permute-start.20 = (bf16[528,128]{1,0:T(8,128)(2,1)S(1)}, bf16[528,128]{1,0:T(8,128)(2,1)S(1)}, u32[]{:S(2)}, u32[]{:S(2)}) collective-permute-start(bf16[528,128]{1,0:T(8,128)(2,1)S(1)} %collective-permute-done.19.lower_3), channel_id=1, source_target_pairs={{0,3},{1,0},{2,1},{3,2},{4,7},{5,4},{6,5},{7,6},{8,11},{9,8},{10,9... | collective-permute-start | bytes 405512 | tf_op jit(solution)/shard_map/ppermute | solution.py:681
  75.8 5.8 %collective-permute-start.18 = (bf16[512,128]{1,0:T(8,128)(2,1)S(1)}, bf16[512,128]{1,0:T(8,128)(2,1)S(1)}, u32[]{:S(2)}, u32[]{:S(2)}) collective-permute-start(bf16[512,128]{1,0:T(8,128)(2,1)S(1)} %collective-permute-done.15.upper_1), channel_id=1, source_target_pairs={{0,1},{1,2},{2,3},{3,0},{4,5},{5,6},{6,7},{7,4},{8,9},{9,10},{10,1... | collective-permute-start | bytes 393224 | tf_op jit(solution)/shard_map/ppermute | solution.py:681
  87.3 17.7 %collective-permute-start.25 = (bf16[2,8,128,128]{3,2,1,0:T(8,128)(2,1)S(1)}, bf16[2,8,128,128]{3,2,1,0:T(8,128)(2,1)S(1)}, u32[]{:S(2)}, u32[]{:S(2)}) collective-permute-start(bf16[2,8,128,128]{3,2,1,0:T(8,128)(2,1)S(1)} %near_message.1), channel_id=1, source_target_pairs={{4,0},{8,4},{12,8},{16,12},{20,16},{24,20},{28,24},{32,28},{36,32}... | collective-permute-start | bytes 1572872 | tf_op jit(solution)/shard_map/ppermute | solution.py:758
  99.7 5.3 %collective-permute-start.24 = (bf16[16,128]{1,0:T(8,128)(2,1)S(1)}, bf16[16,128]{1,0:T(8,128)(2,1)S(1)}, u32[]{:S(2)}, u32[]{:S(2)}) collective-permute-start(bf16[16,128]{1,0:T(8,128)(2,1)S(1)} %get-tuple-element.95.factors_ref), channel_id=1, source_target_pairs={{4,0},{8,4},{12,8},{16,12},{20,16},{24,20},{28,24},{32,28},{36,32}... | collective-permute-start | bytes 12296 | tf_op jit(solution)/shard_map/ppermute | solution.py:760
  (8 other events, 65.7 us)

commit v5 on v4

--- a/solution.py
+++ b/solution.py
@@ -464,7 +464,7 @@
         applied[j] = jnp.where(support_of(plan[SIZES + j], cap), result, 0.0)
         return carry
 
-    lax.fori_loop(0, slots, one, 0)
+    lax.fori_loop(0, slots, one, 0, unroll=True)
     close_step(psi_ref, half_ref, applied, a_ref, upper_ref, lower_ref)
 
 

time: 106 us -> 104 us (0.981)
  Pallas kernels: 36.1 us -> 33.2 us
    pallas_call x2, Pallas kernels: 11.1 us -> 8.21 us  [later_step(): pl.pallas_call(functools.partial(later_kernel, last, entries), out_shape=...]
where the time goes in v5:
time: 104 us; the launch traced here: 103 us
  starting transfers between devices  52.8 us (51%)
  Pallas kernels  33.2 us (32%)
  waiting for transfers between devices  15.6 us (15%)
    ppermute x21, starting transfers between devices, around(): lax.ppermute(value, 'blk', [(i, (i + shift) % count) for i in range(count)])  18.7 us
    ppermute x21, waiting for transfers between devices, around(): lax.ppermute(value, 'blk', [(i, (i + shift) % count) for i in range(count)])  11.6 us
    all_to_all x1, starting transfers between devices, shards(): lax.all_to_all(maps, 'sect', 0, 0, tiled=True, axis_index_groups=groups)  9.3 us
    pallas_call x2, Pallas kernels, later_step(): pl.pallas_call(functools.partial(later_kernel, last, entries), out_shape=...  8.21 us
    all_to_all x1, starting transfers between devices, shards(): lax.all_to_all(env, 'sect', 0, 0, tiled=True, axis_index_groups=groups)  7.86 us
    ppermute x1, starting transfers between devices, shards(): near = lax.ppermute(near, 'sect', behind)  6.9 us
    pallas_call x1, Pallas kernels, first_products(): pl.pallas_call(first_kernel, out_shape=[jax.ShapeDtypeStruct((4 * slots,...  6.84 us
    pallas_call x2, Pallas kernels, ready_right(): pl.pallas_call(copy_kernel, out_shape=pltpu.VMEM(right.shape, BF16), in_s...  4.39 us
  transfers between devices with their start and end apart: 28, of which 12 were waited for; matrix products, arithmetic and copies ran while one was open for 0% of the time, Pallas kernels for 22%

profile of v5, /device:TPU:1, one launch (start us, length us, event | category | flops | bytes accessed | tf_op | source)
XLA Modules:
  0.0 103.1 jit_solution(2800421732917861011)
XLA Ops:
  0.6 3.3 %collective-permute-start = (f32[8,128,128]{2,1,0:T(8,128)}, f32[8,128,128]{2,1,0:T(8,128)S(1)}, u32[]{:S(2)}, u32[]{:S(2)}) collective-permute-start(f32[8,128,128]{2,1,0:T(8,128)} %bitcast.21), channel_id=1, source_target_pairs={{0,4},{4,0},{8,12},{12,8},{16,20},{20,16},{24,28},{28,24},{32,36},... | collective-permute-start | bytes 1572872 | tf_op jit(solution)/shard_map/ppermute | solution.py:721
  4.1 2.2 %start.1 = (s32[256]{0:T(256)S(1)}, bf16[8,128,128]{2,1,0:T(8,128)(2,1)S(1)}, f32[4,128,128]{2,1,0:T(8,128)S(1)}, f32[8,128]{1,0:T(8,128)S(1)}, f32[8,128,128]{2,1,0:T(8,128)S(1)}) custom-call(s32[32]{0:T(128)} %slot_hbm.1, s32[16,32]{1,0:T(8,128)} %bitcast.25, s32[1,32]{1,0:T(1,128)} %sizes_hbm.1, s32[1,32]{1,0:T(1,128)} %ranks_hbm.1, ...), custom_call_target="tpu_custom_call" | custom-call | flops 524288 | bytes 524288 | tf_op jit(solution)/shard_map/start/pallas_call | solution.py:108
  7.2 9.3 %all-to-all-start = ((bf16[32,24,128]{2,1,0:T(8,128)(2,1)}), bf16[32,24,128]{2,1,0:T(8,128)(2,1)S(1)}, u32[]{:S(2)}, u32[]{:S(2)}) async-start(bf16[32,24,128]{2,1,0:T(8,128)(2,1)} %chip_maps.1), calls=%async_computation | async-start | bytes 393216 | tf_op jit(solution)/shard_map/all_to_all | solution.py:728
  16.5 2.8 %collective-permute-start.4 = (bf16[8,128,128]{2,1,0:T(8,128)(2,1)S(1)}, bf16[8,128,128]{2,1,0:T(8,128)(2,1)}, u32[]{:S(2)}, u32[]{:S(2)}) collective-permute-start(bf16[8,128,128]{2,1,0:T(8,128)(2,1)S(1)} %get-tuple-element.57.psi_0), channel_id=1, source_target_pairs={{0,3},{1,0},{2,1},{3,2},{4,7},{5,4},{6,5},{7,6},{8,11},{9,8},{10,9... | collective-permute-start | bytes 786440 | tf_op jit(solution)/shard_map/ppermute | solution.py:681
  21.2 2.0 %collective-permute-start.6 = (bf16[8,128,128]{2,1,0:T(8,128)(2,1)}, bf16[8,128,128]{2,1,0:T(8,128)(2,1)S(1)}, u32[]{:S(2)}, u32[]{:S(2)}) collective-permute-start(bf16[8,128,128]{2,1,0:T(8,128)(2,1)} %get-tuple-element.60), channel_id=1, source_target_pairs={{0,3},{1,0},{2,1},{3,2},{4,7},{5,4},{6,5},{7,6},{8,11},{9,8},{10,9... | collective-permute-start | bytes 786440 | tf_op jit(solution)/shard_map/ppermute | solution.py:681
  23.2 1.4 %collective-permute-start.5 = (bf16[8,128,128]{2,1,0:T(8,128)(2,1)}, bf16[8,128,128]{2,1,0:T(8,128)(2,1)S(1)}, u32[]{:S(2)}, u32[]{:S(2)}) collective-permute-start(bf16[8,128,128]{2,1,0:T(8,128)(2,1)} %get-tuple-element.60), channel_id=1, source_target_pairs={{0,2},{1,3},{2,0},{3,1},{4,6},{5,7},{6,4},{7,5},{8,10},{9,11},{10,... | collective-permute-start | bytes 786440 | tf_op jit(solution)/shard_map/ppermute | solution.py:681
  26.9 7.9 %all-to-all-start.1 = ((bf16[32,16,128]{2,1,0:T(8,128)(2,1)}), bf16[32,16,128]{2,1,0:T(8,128)(2,1)S(1)}, u32[]{:S(2)}, u32[]{:S(2)}) async-start(bf16[32,16,128]{2,1,0:T(8,128)(2,1)} %scan_maps.1), calls=%async_computation.1 | async-start | bytes 262144 | tf_op jit(solution)/shard_map/all_to_all | solution.py:735
  36.7 6.8 %first_products.1 = (bf16[32,128,128]{2,1,0:T(8,128)(2,1)S(1)}, f32[8,128,128]{2,1,0:T(8,128)S(1)}) custom-call(s32[256]{0:T(256)S(1)} %get-tuple-element.52.plan, bf16[8,128,128]{2,1,0:T(8,128)(2,1)} %copy-done, bf16[8,128,128]{2,1,0:T(8,128)(2,1)} %copy-done.3, bf16[8,128,128]{2,1,0:T(8,128)(2,1)} %copy-done.2, ...), custom_call_target="tpu_custom_call" | custom-call | flops 2097152 | bytes 131072 | tf_op jit(solution)/shard_map/first_products/pallas_call | solution.py:478
  44.0 3.8 %collective-permute-start.7 = (bf16[4,128,128]{2,1,0:T(8,128)(2,1)S(1)}, bf16[4,128,128]{2,1,0:T(8,128)(2,1)S(1)}, u32[]{:S(2)}, u32[]{:S(2)}) collective-permute-start(bf16[4,128,128]{2,1,0:T(8,128)(2,1)S(1)} %bitcast.11), channel_id=1, source_target_pairs={{0,4},{4,0},{8,12},{12,8},{16,20},{20,16},{24,28},{28,24},{32,36},... | collective-permute-start | bytes 393224 | tf_op jit(solution)/shard_map/ppermute | solution.py:739
  48.8 1.5 %first_close.1 = (bf16[8,128,128]{2,1,0:T(8,128)(2,1)S(1)}, f32[8,128,128]{2,1,0:T(8,128)S(1)}, bf16[512,128]{1,0:T(8,128)(2,1)S(1)}, bf16[528,128]{1,0:T(8,128)(2,1)S(1)}) custom-call(s32[256]{0:T(256)S(1)} %get-tuple-element.52.plan, bf16[32,128,128]{2,1,0:T(8,128)(2,1)S(1)} %get-tuple-element.58.psi_ref.before, ...), custom_call_target="tpu_custom_call" | custom-call | flops 33554432 | bytes 2621440 | tf_op jit(solution)/shard_map/first_close/pallas_call | solution.py:548
  50.9 1.4 %collective-permute-start.10 = (bf16[512,128]{1,0:T(8,128)(2,1)S(1)}, bf16[512,128]{1,0:T(8,128)(2,1)S(1)}, u32[]{:S(2)}, u32[]{:S(2)}) collective-permute-start(bf16[512,128]{1,0:T(8,128)(2,1)S(1)} %get-tuple-element.69), channel_id=1, source_target_pairs={{0,3},{1,0},{2,1},{3,2},{4,7},{5,4},{6,5},{7,6},{8,11},{9,8},{10,9... | collective-permute-start | bytes 393224 | tf_op jit(solution)/shard_map/ppermute | solution.py:681
  53.4 2.2 %ready_left.2 = (bf16[24,128,128]{2,1,0:T(8,128)(2,1)S(1)}, bf16[8,16,128,128]{3,2,1,0:T(8,128)(2,1)S(1)}) custom-call(bf16[8,128,128]{2,1,0:T(8,128)(2,1)S(1)} %collective-permute-done.8.half_1, bf16[8,128,128]{2,1,0:T(8,128)(2,1)S(1)} %collective-permute-done.5.half_2, bf16[8,128,128]{2,1,0:T(8,128)(2,1)S(1)} %collective-permute-done.6.half_3, ...), custom_call_target="tpu_custom_call" | custom-call | flops 393216 | bytes 4194304 | tf_op jit(solution)/shard_map/ready_left/pallas_call | solution.py:512
  55.6 1.7 %collective-permute-start.14 = (bf16[528,128]{1,0:T(8,128)(2,1)S(1)}, bf16[528,128]{1,0:T(8,128)(2,1)S(1)}, u32[]{:S(2)}, u32[]{:S(2)}) collective-permute-start(bf16[528,128]{1,0:T(8,128)(2,1)S(1)} %collective-permute-done.13.lower_3), channel_id=1, source_target_pairs={{0,3},{1,0},{2,1},{3,2},{4,7},{5,4},{6,5},{7,6},{8,11},{9,8},{10,9... | collective-permute-start | bytes 405512 | tf_op jit(solution)/shard_map/ppermute | solution.py:681
  58.1 2.2 %ready_right.2.right_ref = bf16[8,16,128,128]{3,2,1,0:T(8,128)(2,1)S(1)} custom-call(bf16[8,16,128,128]{3,2,1,0:T(8,128)(2,1)} %bitcast.18), custom_call_target="tpu_custom_call" | custom-call | flops 2097152 | bytes 4194304 | tf_op jit(solution)/shard_map/ready_right/pallas_call | solution.py:534
  60.5 2.6 %collective-permute-done.12.upper_2 = bf16[512,128]{1,0:T(8,128)(2,1)S(1)} collective-permute-done((bf16[512,128]{1,0:T(8,128)(2,1)S(1)}, bf16[512,128]{1,0:T(8,128)(2,1)S(1)}, u32[]{:S(2)}, u32[]{:S(2)}) %collective-permute-start.12) | collective-permute-done | bytes 131104 | tf_op jit(solution)/shard_map/ppermute | solution.py:681
  63.1 4.1 %later_step.1 = (bf16[32,128,128]{2,1,0:T(8,128)(2,1)S(1)}, f32[8,128,128]{2,1,0:T(8,128)S(1)}, bf16[512,128]{1,0:T(8,128)(2,1)S(1)}, bf16[528,128]{1,0:T(8,128)(2,1)S(1)}) custom-call(s32[256]{0:T(256)S(1)} %get-tuple-element.52.plan, f32[8,128,128]{2,1,0:T(8,128)S(1)} %get-tuple-element.66.a_own, bf16[528,128]{1,0:T(8,128)(2,1)S(1)} %get-tuple-element.68.lower_0, ...), custom_call_target="tpu_custom_call" | custom-call | flops 1073741824 | bytes 25165824 | tf_op jit(solution)/shard_map/later_step/pallas_call | solution.py:574
  70.2 2.2 %ready_left.3 = (bf16[24,128,128]{2,1,0:T(8,128)(2,1)S(1)}, bf16[8,16,128,128]{3,2,1,0:T(8,128)(2,1)S(1)}) custom-call(bf16[8,128,128]{2,1,0:T(8,128)(2,1)S(1)} %collective-permute-done.8.half_1, bf16[8,128,128]{2,1,0:T(8,128)(2,1)S(1)} %collective-permute-done.5.half_2, bf16[8,128,128]{2,1,0:T(8,128)(2,1)S(1)} %collective-permute-done.6.half_3, ...), custom_call_target="tpu_custom_call" | custom-call | flops 393216 | bytes 4194304 | tf_op jit(solution)/shard_map/ready_left/pallas_call | solution.py:512
  72.4 2.0 %collective-permute-start.20 = (bf16[528,128]{1,0:T(8,128)(2,1)S(1)}, bf16[528,128]{1,0:T(8,128)(2,1)S(1)}, u32[]{:S(2)}, u32[]{:S(2)}) collective-permute-start(bf16[528,128]{1,0:T(8,128)(2,1)S(1)} %collective-permute-done.19.lower_3), channel_id=1, source_target_pairs={{0,3},{1,0},{2,1},{3,2},{4,7},{5,4},{6,5},{7,6},{8,11},{9,8},{10,9... | collective-permute-start | bytes 405512 | tf_op jit(solution)/shard_map/ppermute | solution.py:681
  74.4 2.2 %ready_right.3.right_ref = bf16[8,16,128,128]{3,2,1,0:T(8,128)(2,1)S(1)} custom-call(bf16[8,16,128,128]{3,2,1,0:T(8,128)(2,1)} %bitcast.19), custom_call_target="tpu_custom_call" | custom-call | flops 2097152 | bytes 4194304 | tf_op jit(solution)/shard_map/ready_right/pallas_call | solution.py:534
  76.6 3.6 %collective-permute-done.18.upper_2 = bf16[512,128]{1,0:T(8,128)(2,1)S(1)} collective-permute-done((bf16[512,128]{1,0:T(8,128)(2,1)S(1)}, bf16[512,128]{1,0:T(8,128)(2,1)S(1)}, u32[]{:S(2)}, u32[]{:S(2)}) %collective-permute-start.18) | collective-permute-done | bytes 131104 | tf_op jit(solution)/shard_map/ppermute | solution.py:681
  80.2 4.1 %last_step.1 = (bf16[32,128,128]{2,1,0:T(8,128)(2,1)S(1)}, f32[8,128,128]{2,1,0:T(8,128)S(1)}, bf16[16,128]{1,0:T(8,128)(2,1)S(1)}) custom-call(s32[256]{0:T(256)S(1)} %get-tuple-element.52.plan, f32[8,128,128]{2,1,0:T(8,128)S(1)} %get-tuple-element.82.a_own, bf16[528,128]{1,0:T(8,128)(2,1)S(1)} %get-tuple-element.83.lower_0, ...), custom_call_target="tpu_custom_call" | custom-call | flops 1073741824 | bytes 25165824 | tf_op jit(solution)/shard_map/last_step/pallas_call | solution.py:574
  84.4 6.9 %collective-permute-start.25 = (bf16[2,8,128,128]{3,2,1,0:T(8,128)(2,1)S(1)}, bf16[2,8,128,128]{3,2,1,0:T(8,128)(2,1)S(1)}, u32[]{:S(2)}, u32[]{:S(2)}) collective-permute-start(bf16[2,8,128,128]{3,2,1,0:T(8,128)(2,1)S(1)} %near_message.1), channel_id=1, source_target_pairs={{4,0},{8,4},{12,8},{16,12},{20,16},{24,20},{28,24},{32,28},{36,32}... | collective-permute-start | bytes 1572872 | tf_op jit(solution)/shard_map/ppermute | solution.py:758
  94.0 1.6 %collective-permute-done.22.tile_2 = bf16[16,128]{1,0:T(8,128)(2,1)S(1)} collective-permute-done((bf16[16,128]{1,0:T(8,128)(2,1)S(1)}, bf16[16,128]{1,0:T(8,128)(2,1)S(1)}, u32[]{:S(2)}, u32[]{:S(2)}) %collective-permute-start.22) | collective-permute-done | bytes 4128 | tf_op jit(solution)/shard_map/ppermute | solution.py:681
  96.8 2.7 %collective-permute-start.24 = (bf16[16,128]{1,0:T(8,128)(2,1)S(1)}, bf16[16,128]{1,0:T(8,128)(2,1)S(1)}, u32[]{:S(2)}, u32[]{:S(2)}) collective-permute-start(bf16[16,128]{1,0:T(8,128)(2,1)S(1)} %get-tuple-element.95.factors_ref), channel_id=1, source_target_pairs={{4,0},{8,4},{12,8},{16,12},{20,16},{24,20},{28,24},{32,28},{36,32}... | collective-permute-start | bytes 12296 | tf_op jit(solution)/shard_map/ppermute | solution.py:760
  (56 shorter events, 21.6 us)
Async XLA Ops:
  0.6 5.6 %collective-permute-start = (f32[8,128,128]{2,1,0:T(8,128)}, f32[8,128,128]{2,1,0:T(8,128)S(1)}, u32[]{:S(2)}, u32[]{:S(2)}) collective-permute-start(f32[8,128,128]{2,1,0:T(8,128)} %bitcast.21), channel_id=1, source_target_pairs={{0,4},{4,0},{8,12},{12,8},{16,20},{20,16},{24,28},{28,24},{32,36},... | collective-permute-start | bytes 1572872 | tf_op jit(solution)/shard_map/ppermute | solution.py:721
  7.2 18.7 %all-to-all-start = ((bf16[32,24,128]{2,1,0:T(8,128)(2,1)}), bf16[32,24,128]{2,1,0:T(8,128)(2,1)S(1)}, u32[]{:S(2)}, u32[]{:S(2)}) async-start(bf16[32,24,128]{2,1,0:T(8,128)(2,1)} %chip_maps.1), calls=%async_computation | async-start | bytes 393216 | tf_op jit(solution)/shard_map/all_to_all | solution.py:728
  16.5 18.2 %collective-permute-start.4 = (bf16[8,128,128]{2,1,0:T(8,128)(2,1)S(1)}, bf16[8,128,128]{2,1,0:T(8,128)(2,1)}, u32[]{:S(2)}, u32[]{:S(2)}) collective-permute-start(bf16[8,128,128]{2,1,0:T(8,128)(2,1)S(1)} %get-tuple-element.57.psi_0), channel_id=1, source_target_pairs={{0,3},{1,0},{2,1},{3,2},{4,7},{5,4},{6,5},{7,6},{8,11},{9,8},{10,9... | collective-permute-start | bytes 786440 | tf_op jit(solution)/shard_map/ppermute | solution.py:681
  19.4 15.5 %collective-permute-start.3 = (bf16[8,128,128]{2,1,0:T(8,128)(2,1)S(1)}, bf16[8,128,128]{2,1,0:T(8,128)(2,1)S(1)}, u32[]{:S(2)}, u32[]{:S(2)}) collective-permute-start(bf16[8,128,128]{2,1,0:T(8,128)(2,1)S(1)} %get-tuple-element.57.psi_0), channel_id=1, source_target_pairs={{0,2},{1,3},{2,0},{3,1},{4,6},{5,7},{6,4},{7,5},{8,10},{9,11},{10,... | collective-permute-start | bytes 786440 | tf_op jit(solution)/shard_map/ppermute | solution.py:681
  19.7 16.3 %collective-permute-start.2 = (bf16[8,128,128]{2,1,0:T(8,128)(2,1)S(1)}, bf16[8,128,128]{2,1,0:T(8,128)(2,1)S(1)}, u32[]{:S(2)}, u32[]{:S(2)}) collective-permute-start(bf16[8,128,128]{2,1,0:T(8,128)(2,1)S(1)} %get-tuple-element.57.psi_0), channel_id=1, source_target_pairs={{0,1},{1,2},{2,3},{3,0},{4,5},{5,6},{6,7},{7,4},{8,9},{9,10},{10,1... | collective-permute-start | bytes 786440 | tf_op jit(solution)/shard_map/ppermute | solution.py:681
  21.2 22.4 %collective-permute-start.6 = (bf16[8,128,128]{2,1,0:T(8,128)(2,1)}, bf16[8,128,128]{2,1,0:T(8,128)(2,1)S(1)}, u32[]{:S(2)}, u32[]{:S(2)}) collective-permute-start(bf16[8,128,128]{2,1,0:T(8,128)(2,1)} %get-tuple-element.60), channel_id=1, source_target_pairs={{0,3},{1,0},{2,1},{3,2},{4,7},{5,4},{6,5},{7,6},{8,11},{9,8},{10,9... | collective-permute-start | bytes 786440 | tf_op jit(solution)/shard_map/ppermute | solution.py:681
  23.2 20.4 %collective-permute-start.5 = (bf16[8,128,128]{2,1,0:T(8,128)(2,1)}, bf16[8,128,128]{2,1,0:T(8,128)(2,1)S(1)}, u32[]{:S(2)}, u32[]{:S(2)}) collective-permute-start(bf16[8,128,128]{2,1,0:T(8,128)(2,1)} %get-tuple-element.60), channel_id=1, source_target_pairs={{0,2},{1,3},{2,0},{3,1},{4,6},{5,7},{6,4},{7,5},{8,10},{9,11},{10,... | collective-permute-start | bytes 786440 | tf_op jit(solution)/shard_map/ppermute | solution.py:681
  26.9 17.1 %all-to-all-start.1 = ((bf16[32,16,128]{2,1,0:T(8,128)(2,1)}), bf16[32,16,128]{2,1,0:T(8,128)(2,1)S(1)}, u32[]{:S(2)}, u32[]{:S(2)}) async-start(bf16[32,16,128]{2,1,0:T(8,128)(2,1)} %scan_maps.1), calls=%async_computation.1 | async-start | bytes 262144 | tf_op jit(solution)/shard_map/all_to_all | solution.py:735
  34.8 15.6 %collective-permute-start.8 = (bf16[8,128,128]{2,1,0:T(8,128)(2,1)}, bf16[8,128,128]{2,1,0:T(8,128)(2,1)S(1)}, u32[]{:S(2)}, u32[]{:S(2)}) collective-permute-start(bf16[8,128,128]{2,1,0:T(8,128)(2,1)} %get-tuple-element.60), channel_id=1, source_target_pairs={{0,1},{1,2},{2,3},{3,0},{4,5},{5,6},{6,7},{7,4},{8,9},{9,10},{10,1... | collective-permute-start | bytes 786440 | tf_op jit(solution)/shard_map/ppermute | solution.py:681
  44.0 4.8 %collective-permute-start.7 = (bf16[4,128,128]{2,1,0:T(8,128)(2,1)S(1)}, bf16[4,128,128]{2,1,0:T(8,128)(2,1)S(1)}, u32[]{:S(2)}, u32[]{:S(2)}) collective-permute-start(bf16[4,128,128]{2,1,0:T(8,128)(2,1)S(1)} %bitcast.11), channel_id=1, source_target_pairs={{0,4},{4,0},{8,12},{12,8},{16,20},{20,16},{24,28},{28,24},{32,36},... | collective-permute-start | bytes 393224 | tf_op jit(solution)/shard_map/ppermute | solution.py:739
  50.3 5.2 %collective-permute-start.13 = (bf16[528,128]{1,0:T(8,128)(2,1)S(1)}, bf16[528,128]{1,0:T(8,128)(2,1)S(1)}, u32[]{:S(2)}, u32[]{:S(2)}) collective-permute-start(bf16[528,128]{1,0:T(8,128)(2,1)S(1)} %get-tuple-element.68.lower_0), channel_id=1, source_target_pairs={{0,3},{1,0},{2,1},{3,2},{4,7},{5,4},{6,5},{7,6},{8,11},{9,8},{10,9... | collective-permute-start | bytes 405512 | tf_op jit(solution)/shard_map/ppermute | solution.py:681
  50.9 7.2 %collective-permute-start.10 = (bf16[512,128]{1,0:T(8,128)(2,1)S(1)}, bf16[512,128]{1,0:T(8,128)(2,1)S(1)}, u32[]{:S(2)}, u32[]{:S(2)}) collective-permute-start(bf16[512,128]{1,0:T(8,128)(2,1)S(1)} %get-tuple-element.69), channel_id=1, source_target_pairs={{0,3},{1,0},{2,1},{3,2},{4,7},{5,4},{6,5},{7,6},{8,11},{9,8},{10,9... | collective-permute-start | bytes 393224 | tf_op jit(solution)/shard_map/ppermute | solution.py:681
  52.3 5.8 %collective-permute-start.9 = (bf16[512,128]{1,0:T(8,128)(2,1)S(1)}, bf16[512,128]{1,0:T(8,128)(2,1)S(1)}, u32[]{:S(2)}, u32[]{:S(2)}) collective-permute-start(bf16[512,128]{1,0:T(8,128)(2,1)S(1)} %get-tuple-element.69), channel_id=1, source_target_pairs={{0,1},{1,2},{2,3},{3,0},{4,5},{5,6},{6,7},{7,4},{8,9},{9,10},{10,1... | collective-permute-start | bytes 393224 | tf_op jit(solution)/shard_map/ppermute | solution.py:681
  52.3 8.1 %collective-permute-start.11 = (bf16[528,128]{1,0:T(8,128)(2,1)S(1)}, bf16[528,128]{1,0:T(8,128)(2,1)S(1)}, u32[]{:S(2)}, u32[]{:S(2)}) collective-permute-start(bf16[528,128]{1,0:T(8,128)(2,1)S(1)} %get-tuple-element.68.lower_0), channel_id=1, source_target_pairs={{0,1},{1,2},{2,3},{3,0},{4,5},{5,6},{6,7},{7,4},{8,9},{9,10},{10,1... | collective-permute-start | bytes 405512 | tf_op jit(solution)/shard_map/ppermute | solution.py:681
  55.6 7.5 %collective-permute-start.14 = (bf16[528,128]{1,0:T(8,128)(2,1)S(1)}, bf16[528,128]{1,0:T(8,128)(2,1)S(1)}, u32[]{:S(2)}, u32[]{:S(2)}) collective-permute-start(bf16[528,128]{1,0:T(8,128)(2,1)S(1)} %collective-permute-done.13.lower_3), channel_id=1, source_target_pairs={{0,3},{1,0},{2,1},{3,2},{4,7},{5,4},{6,5},{7,6},{8,11},{9,8},{10,9... | collective-permute-start | bytes 405512 | tf_op jit(solution)/shard_map/ppermute | solution.py:681
  58.0 5.0 %collective-permute-start.12 = (bf16[512,128]{1,0:T(8,128)(2,1)S(1)}, bf16[512,128]{1,0:T(8,128)(2,1)S(1)}, u32[]{:S(2)}, u32[]{:S(2)}) collective-permute-start(bf16[512,128]{1,0:T(8,128)(2,1)S(1)} %collective-permute-done.9.upper_1), channel_id=1, source_target_pairs={{0,1},{1,2},{2,3},{3,0},{4,5},{5,6},{6,7},{7,4},{8,9},{9,10},{10,1... | collective-permute-start | bytes 393224 | tf_op jit(solution)/shard_map/ppermute | solution.py:681
  67.2 5.2 %collective-permute-start.19 = (bf16[528,128]{1,0:T(8,128)(2,1)S(1)}, bf16[528,128]{1,0:T(8,128)(2,1)S(1)}, u32[]{:S(2)}, u32[]{:S(2)}) collective-permute-start(bf16[528,128]{1,0:T(8,128)(2,1)S(1)} %get-tuple-element.83.lower_0), channel_id=1, source_target_pairs={{0,3},{1,0},{2,1},{3,2},{4,7},{5,4},{6,5},{7,6},{8,11},{9,8},{10,9... | collective-permute-start | bytes 405512 | tf_op jit(solution)/shard_map/ppermute | solution.py:681
  68.0 6.4 %collective-permute-start.16 = (bf16[512,128]{1,0:T(8,128)(2,1)S(1)}, bf16[512,128]{1,0:T(8,128)(2,1)S(1)}, u32[]{:S(2)}, u32[]{:S(2)}) collective-permute-start(bf16[512,128]{1,0:T(8,128)(2,1)S(1)} %get-tuple-element.84), channel_id=1, source_target_pairs={{0,3},{1,0},{2,1},{3,2},{4,7},{5,4},{6,5},{7,6},{8,11},{9,8},{10,9... | collective-permute-start | bytes 393224 | tf_op jit(solution)/shard_map/ppermute | solution.py:681
  68.2 6.2 %collective-permute-start.15 = (bf16[512,128]{1,0:T(8,128)(2,1)S(1)}, bf16[512,128]{1,0:T(8,128)(2,1)S(1)}, u32[]{:S(2)}, u32[]{:S(2)}) collective-permute-start(bf16[512,128]{1,0:T(8,128)(2,1)S(1)} %get-tuple-element.84), channel_id=1, source_target_pairs={{0,1},{1,2},{2,3},{3,0},{4,5},{5,6},{6,7},{7,4},{8,9},{9,10},{10,1... | collective-permute-start | bytes 393224 | tf_op jit(solution)/shard_map/ppermute | solution.py:681
  69.4 7.2 %collective-permute-start.17 = (bf16[528,128]{1,0:T(8,128)(2,1)S(1)}, bf16[528,128]{1,0:T(8,128)(2,1)S(1)}, u32[]{:S(2)}, u32[]{:S(2)}) collective-permute-start(bf16[528,128]{1,0:T(8,128)(2,1)S(1)} %get-tuple-element.83.lower_0), channel_id=1, source_target_pairs={{0,1},{1,2},{2,3},{3,0},{4,5},{5,6},{6,7},{7,4},{8,9},{9,10},{10,1... | collective-permute-start | bytes 405512 | tf_op jit(solution)/shard_map/ppermute | solution.py:681
  72.4 7.8 %collective-permute-start.20 = (bf16[528,128]{1,0:T(8,128)(2,1)S(1)}, bf16[528,128]{1,0:T(8,128)(2,1)S(1)}, u32[]{:S(2)}, u32[]{:S(2)}) collective-permute-start(bf16[528,128]{1,0:T(8,128)(2,1)S(1)} %collective-permute-done.19.lower_3), channel_id=1, source_target_pairs={{0,3},{1,0},{2,1},{3,2},{4,7},{5,4},{6,5},{7,6},{8,11},{9,8},{10,9... | collective-permute-start | bytes 405512 | tf_op jit(solution)/shard_map/ppermute | solution.py:681
  74.4 5.8 %collective-permute-start.18 = (bf16[512,128]{1,0:T(8,128)(2,1)S(1)}, bf16[512,128]{1,0:T(8,128)(2,1)S(1)}, u32[]{:S(2)}, u32[]{:S(2)}) collective-permute-start(bf16[512,128]{1,0:T(8,128)(2,1)S(1)} %collective-permute-done.15.upper_1), channel_id=1, source_target_pairs={{0,1},{1,2},{2,3},{3,0},{4,5},{5,6},{6,7},{7,4},{8,9},{9,10},{10,1... | collective-permute-start | bytes 393224 | tf_op jit(solution)/shard_map/ppermute | solution.py:681
  84.4 17.7 %collective-permute-start.25 = (bf16[2,8,128,128]{3,2,1,0:T(8,128)(2,1)S(1)}, bf16[2,8,128,128]{3,2,1,0:T(8,128)(2,1)S(1)}, u32[]{:S(2)}, u32[]{:S(2)}) collective-permute-start(bf16[2,8,128,128]{3,2,1,0:T(8,128)(2,1)S(1)} %near_message.1), channel_id=1, source_target_pairs={{4,0},{8,4},{12,8},{16,12},{20,16},{24,20},{28,24},{32,28},{36,32}... | collective-permute-start | bytes 1572872 | tf_op jit(solution)/shard_map/ppermute | solution.py:758
  96.8 5.3 %collective-permute-start.24 = (bf16[16,128]{1,0:T(8,128)(2,1)S(1)}, bf16[16,128]{1,0:T(8,128)(2,1)S(1)}, u32[]{:S(2)}, u32[]{:S(2)}) collective-permute-start(bf16[16,128]{1,0:T(8,128)(2,1)S(1)} %get-tuple-element.95.factors_ref), channel_id=1, source_target_pairs={{4,0},{8,4},{12,8},{16,12},{20,16},{24,20},{28,24},{32,28},{36,32}... | collective-permute-start | bytes 12296 | tf_op jit(solution)/shard_map/ppermute | solution.py:760
  (8 other events, 64.2 us)

commit v6 on v5

--- a/solution.py
+++ b/solution.py
@@ -275,7 +275,7 @@
     return jnp.sum(jnp.sum(x, axis=0, keepdims=True), axis=1, keepdims=True)
 
 
-AHEAD = 3
+AHEAD = 4
 
 
 def products(j, plan, left_ref, right_ref, psi_ref, inner):
@@ -374,18 +374,21 @@
     for j in range(1, AHEAD):
         begin(j)
 
-    def one(j, carry):
+    def arrive(j):
         for copy in fetch_ops(j):
             copy.wait()
 
-        @pl.when(j + AHEAD < slots)
-        def _():
-            begin(j + AHEAD)
-
-        ops_ref[j] = products(j, plan, left_ref, right_ref, psi_ref, inner)
-        return carry
-
-    lax.fori_loop(0, slots, one, 0)
+    def some(first):
+        for j in range(first, first + AHEAD):
+            ops_ref[j] = products(j, plan, left_ref, right_ref, psi_ref, inner)
+
+    for j in range(AHEAD):
+        arrive(j)
+        begin(AHEAD + j)
+    some(0)
+    for j in range(AHEAD):
+        arrive(AHEAD + j)
+    some(AHEAD)
 
 
 def close_kernel(

time: 104 us -> 104 us (level)
  no operation moved by 1% of the time
where the time goes in v6:
time: 104 us; the launch traced here: 103 us
  starting transfers between devices  52.7 us (51%)
  Pallas kernels  33.2 us (32%)
  waiting for transfers between devices  15.5 us (15%)
    ppermute x21, starting transfers between devices, around(): lax.ppermute(value, 'blk', [(i, (i + shift) % count) for i in range(count)])  18.7 us
    ppermute x21, waiting for transfers between devices, around(): lax.ppermute(value, 'blk', [(i, (i + shift) % count) for i in range(count)])  11.6 us
    all_to_all x1, starting transfers between devices, shards(): lax.all_to_all(maps, 'sect', 0, 0, tiled=True, axis_index_groups=groups)  9.3 us
    pallas_call x2, Pallas kernels, later_step(): pl.pallas_call(functools.partial(later_kernel, last, entries), out_shape=...  8.21 us
    all_to_all x1, starting transfers between devices, shards(): lax.all_to_all(env, 'sect', 0, 0, tiled=True, axis_index_groups=groups)  7.86 us
    ppermute x1, starting transfers between devices, shards(): near = lax.ppermute(near, 'sect', behind)  6.9 us
    pallas_call x1, Pallas kernels, first_products(): pl.pallas_call(first_kernel, out_shape=[jax.ShapeDtypeStruct((4 * slots,...  6.87 us
    pallas_call x2, Pallas kernels, ready_right(): pl.pallas_call(copy_kernel, out_shape=pltpu.VMEM(right.shape, BF16), in_s...  4.39 us
  transfers between devices with their start and end apart: 28, of which 12 were waited for; matrix products, arithmetic and copies ran while one was open for 0% of the time, Pallas kernels for 22%

profile of v6, /device:TPU:1, one launch (start us, length us, event | category | flops | bytes accessed | tf_op | source)
XLA Modules:
  0.0 103.1 jit_solution(11972198791695392913)
XLA Ops:
  0.6 3.3 %collective-permute-start = (f32[8,128,128]{2,1,0:T(8,128)}, f32[8,128,128]{2,1,0:T(8,128)S(1)}, u32[]{:S(2)}, u32[]{:S(2)}) collective-permute-start(f32[8,128,128]{2,1,0:T(8,128)} %bitcast.21), channel_id=1, source_target_pairs={{0,4},{4,0},{8,12},{12,8},{16,20},{20,16},{24,28},{28,24},{32,36},... | collective-permute-start | bytes 1572872 | tf_op jit(solution)/shard_map/ppermute | solution.py:724
  4.1 2.2 %start.1 = (s32[256]{0:T(256)S(1)}, bf16[8,128,128]{2,1,0:T(8,128)(2,1)S(1)}, f32[4,128,128]{2,1,0:T(8,128)S(1)}, f32[8,128]{1,0:T(8,128)S(1)}, f32[8,128,128]{2,1,0:T(8,128)S(1)}) custom-call(s32[32]{0:T(128)} %slot_hbm.1, s32[16,32]{1,0:T(8,128)} %bitcast.25, s32[1,32]{1,0:T(1,128)} %sizes_hbm.1, s32[1,32]{1,0:T(1,128)} %ranks_hbm.1, ...), custom_call_target="tpu_custom_call" | custom-call | flops 524288 | bytes 524288 | tf_op jit(solution)/shard_map/start/pallas_call | solution.py:108
  7.2 9.3 %all-to-all-start = ((bf16[32,24,128]{2,1,0:T(8,128)(2,1)}), bf16[32,24,128]{2,1,0:T(8,128)(2,1)S(1)}, u32[]{:S(2)}, u32[]{:S(2)}) async-start(bf16[32,24,128]{2,1,0:T(8,128)(2,1)} %chip_maps.1), calls=%async_computation | async-start | bytes 393216 | tf_op jit(solution)/shard_map/all_to_all | solution.py:731
  16.5 2.8 %collective-permute-start.4 = (bf16[8,128,128]{2,1,0:T(8,128)(2,1)S(1)}, bf16[8,128,128]{2,1,0:T(8,128)(2,1)}, u32[]{:S(2)}, u32[]{:S(2)}) collective-permute-start(bf16[8,128,128]{2,1,0:T(8,128)(2,1)S(1)} %get-tuple-element.57.psi_0), channel_id=1, source_target_pairs={{0,3},{1,0},{2,1},{3,2},{4,7},{5,4},{6,5},{7,6},{8,11},{9,8},{10,9... | collective-permute-start | bytes 786440 | tf_op jit(solution)/shard_map/ppermute | solution.py:684
  21.2 2.0 %collective-permute-start.6 = (bf16[8,128,128]{2,1,0:T(8,128)(2,1)}, bf16[8,128,128]{2,1,0:T(8,128)(2,1)S(1)}, u32[]{:S(2)}, u32[]{:S(2)}) collective-permute-start(bf16[8,128,128]{2,1,0:T(8,128)(2,1)} %get-tuple-element.60), channel_id=1, source_target_pairs={{0,3},{1,0},{2,1},{3,2},{4,7},{5,4},{6,5},{7,6},{8,11},{9,8},{10,9... | collective-permute-start | bytes 786440 | tf_op jit(solution)/shard_map/ppermute | solution.py:684
  23.2 1.4 %collective-permute-start.5 = (bf16[8,128,128]{2,1,0:T(8,128)(2,1)}, bf16[8,128,128]{2,1,0:T(8,128)(2,1)S(1)}, u32[]{:S(2)}, u32[]{:S(2)}) collective-permute-start(bf16[8,128,128]{2,1,0:T(8,128)(2,1)} %get-tuple-element.60), channel_id=1, source_target_pairs={{0,2},{1,3},{2,0},{3,1},{4,6},{5,7},{6,4},{7,5},{8,10},{9,11},{10,... | collective-permute-start | bytes 786440 | tf_op jit(solution)/shard_map/ppermute | solution.py:684
  26.9 7.9 %all-to-all-start.1 = ((bf16[32,16,128]{2,1,0:T(8,128)(2,1)}), bf16[32,16,128]{2,1,0:T(8,128)(2,1)S(1)}, u32[]{:S(2)}, u32[]{:S(2)}) async-start(bf16[32,16,128]{2,1,0:T(8,128)(2,1)} %scan_maps.1), calls=%async_computation.1 | async-start | bytes 262144 | tf_op jit(solution)/shard_map/all_to_all | solution.py:738
  36.7 6.9 %first_products.1 = (bf16[32,128,128]{2,1,0:T(8,128)(2,1)S(1)}, f32[8,128,128]{2,1,0:T(8,128)S(1)}) custom-call(s32[256]{0:T(256)S(1)} %get-tuple-element.52.plan, bf16[8,128,128]{2,1,0:T(8,128)(2,1)} %copy-done, bf16[8,128,128]{2,1,0:T(8,128)(2,1)} %copy-done.3, bf16[8,128,128]{2,1,0:T(8,128)(2,1)} %copy-done.2, ...), custom_call_target="tpu_custom_call" | custom-call | flops 2097152 | bytes 131072 | tf_op jit(solution)/shard_map/first_products/pallas_call | solution.py:481
  44.0 3.8 %collective-permute-start.7 = (bf16[4,128,128]{2,1,0:T(8,128)(2,1)S(1)}, bf16[4,128,128]{2,1,0:T(8,128)(2,1)S(1)}, u32[]{:S(2)}, u32[]{:S(2)}) collective-permute-start(bf16[4,128,128]{2,1,0:T(8,128)(2,1)S(1)} %bitcast.11), channel_id=1, source_target_pairs={{0,4},{4,0},{8,12},{12,8},{16,20},{20,16},{24,28},{28,24},{32,36},... | collective-permute-start | bytes 393224 | tf_op jit(solution)/shard_map/ppermute | solution.py:742
  48.8 1.5 %first_close.1 = (bf16[8,128,128]{2,1,0:T(8,128)(2,1)S(1)}, f32[8,128,128]{2,1,0:T(8,128)S(1)}, bf16[512,128]{1,0:T(8,128)(2,1)S(1)}, bf16[528,128]{1,0:T(8,128)(2,1)S(1)}) custom-call(s32[256]{0:T(256)S(1)} %get-tuple-element.52.plan, bf16[32,128,128]{2,1,0:T(8,128)(2,1)S(1)} %get-tuple-element.58.psi_ref.before, ...), custom_call_target="tpu_custom_call" | custom-call | flops 33554432 | bytes 2621440 | tf_op jit(solution)/shard_map/first_close/pallas_call | solution.py:551
  50.9 1.4 %collective-permute-start.10 = (bf16[512,128]{1,0:T(8,128)(2,1)S(1)}, bf16[512,128]{1,0:T(8,128)(2,1)S(1)}, u32[]{:S(2)}, u32[]{:S(2)}) collective-permute-start(bf16[512,128]{1,0:T(8,128)(2,1)S(1)} %get-tuple-element.69), channel_id=1, source_target_pairs={{0,3},{1,0},{2,1},{3,2},{4,7},{5,4},{6,5},{7,6},{8,11},{9,8},{10,9... | collective-permute-start | bytes 393224 | tf_op jit(solution)/shard_map/ppermute | solution.py:684
  53.4 2.2 %ready_left.2 = (bf16[24,128,128]{2,1,0:T(8,128)(2,1)S(1)}, bf16[8,16,128,128]{3,2,1,0:T(8,128)(2,1)S(1)}) custom-call(bf16[8,128,128]{2,1,0:T(8,128)(2,1)S(1)} %collective-permute-done.8.half_1, bf16[8,128,128]{2,1,0:T(8,128)(2,1)S(1)} %collective-permute-done.5.half_2, bf16[8,128,128]{2,1,0:T(8,128)(2,1)S(1)} %collective-permute-done.6.half_3, ...), custom_call_target="tpu_custom_call" | custom-call | flops 393216 | bytes 4194304 | tf_op jit(solution)/shard_map/ready_left/pallas_call | solution.py:515
  55.6 1.7 %collective-permute-start.14 = (bf16[528,128]{1,0:T(8,128)(2,1)S(1)}, bf16[528,128]{1,0:T(8,128)(2,1)S(1)}, u32[]{:S(2)}, u32[]{:S(2)}) collective-permute-start(bf16[528,128]{1,0:T(8,128)(2,1)S(1)} %collective-permute-done.13.lower_3), channel_id=1, source_target_pairs={{0,3},{1,0},{2,1},{3,2},{4,7},{5,4},{6,5},{7,6},{8,11},{9,8},{10,9... | collective-permute-start | bytes 405512 | tf_op jit(solution)/shard_map/ppermute | solution.py:684
  58.1 2.2 %ready_right.2.right_ref = bf16[8,16,128,128]{3,2,1,0:T(8,128)(2,1)S(1)} custom-call(bf16[8,16,128,128]{3,2,1,0:T(8,128)(2,1)} %bitcast.18), custom_call_target="tpu_custom_call" | custom-call | flops 2097152 | bytes 4194304 | tf_op jit(solution)/shard_map/ready_right/pallas_call | solution.py:537
  60.5 2.6 %collective-permute-done.12.upper_2 = bf16[512,128]{1,0:T(8,128)(2,1)S(1)} collective-permute-done((bf16[512,128]{1,0:T(8,128)(2,1)S(1)}, bf16[512,128]{1,0:T(8,128)(2,1)S(1)}, u32[]{:S(2)}, u32[]{:S(2)}) %collective-permute-start.12) | collective-permute-done | bytes 131104 | tf_op jit(solution)/shard_map/ppermute | solution.py:684
  63.1 4.1 %later_step.1 = (bf16[32,128,128]{2,1,0:T(8,128)(2,1)S(1)}, f32[8,128,128]{2,1,0:T(8,128)S(1)}, bf16[512,128]{1,0:T(8,128)(2,1)S(1)}, bf16[528,128]{1,0:T(8,128)(2,1)S(1)}) custom-call(s32[256]{0:T(256)S(1)} %get-tuple-element.52.plan, f32[8,128,128]{2,1,0:T(8,128)S(1)} %get-tuple-element.66.a_own, bf16[528,128]{1,0:T(8,128)(2,1)S(1)} %get-tuple-element.68.lower_0, ...), custom_call_target="tpu_custom_call" | custom-call | flops 1073741824 | bytes 25165824 | tf_op jit(solution)/shard_map/later_step/pallas_call | solution.py:577
  70.2 2.2 %ready_left.3 = (bf16[24,128,128]{2,1,0:T(8,128)(2,1)S(1)}, bf16[8,16,128,128]{3,2,1,0:T(8,128)(2,1)S(1)}) custom-call(bf16[8,128,128]{2,1,0:T(8,128)(2,1)S(1)} %collective-permute-done.8.half_1, bf16[8,128,128]{2,1,0:T(8,128)(2,1)S(1)} %collective-permute-done.5.half_2, bf16[8,128,128]{2,1,0:T(8,128)(2,1)S(1)} %collective-permute-done.6.half_3, ...), custom_call_target="tpu_custom_call" | custom-call | flops 393216 | bytes 4194304 | tf_op jit(solution)/shard_map/ready_left/pallas_call | solution.py:515
  72.4 2.0 %collective-permute-start.20 = (bf16[528,128]{1,0:T(8,128)(2,1)S(1)}, bf16[528,128]{1,0:T(8,128)(2,1)S(1)}, u32[]{:S(2)}, u32[]{:S(2)}) collective-permute-start(bf16[528,128]{1,0:T(8,128)(2,1)S(1)} %collective-permute-done.19.lower_3), channel_id=1, source_target_pairs={{0,3},{1,0},{2,1},{3,2},{4,7},{5,4},{6,5},{7,6},{8,11},{9,8},{10,9... | collective-permute-start | bytes 405512 | tf_op jit(solution)/shard_map/ppermute | solution.py:684
  74.4 2.2 %ready_right.3.right_ref = bf16[8,16,128,128]{3,2,1,0:T(8,128)(2,1)S(1)} custom-call(bf16[8,16,128,128]{3,2,1,0:T(8,128)(2,1)} %bitcast.19), custom_call_target="tpu_custom_call" | custom-call | flops 2097152 | bytes 4194304 | tf_op jit(solution)/shard_map/ready_right/pallas_call | solution.py:537
  76.6 3.6 %collective-permute-done.18.upper_2 = bf16[512,128]{1,0:T(8,128)(2,1)S(1)} collective-permute-done((bf16[512,128]{1,0:T(8,128)(2,1)S(1)}, bf16[512,128]{1,0:T(8,128)(2,1)S(1)}, u32[]{:S(2)}, u32[]{:S(2)}) %collective-permute-start.18) | collective-permute-done | bytes 131104 | tf_op jit(solution)/shard_map/ppermute | solution.py:684
  80.2 4.1 %last_step.1 = (bf16[32,128,128]{2,1,0:T(8,128)(2,1)S(1)}, f32[8,128,128]{2,1,0:T(8,128)S(1)}, bf16[16,128]{1,0:T(8,128)(2,1)S(1)}) custom-call(s32[256]{0:T(256)S(1)} %get-tuple-element.52.plan, f32[8,128,128]{2,1,0:T(8,128)S(1)} %get-tuple-element.82.a_own, bf16[528,128]{1,0:T(8,128)(2,1)S(1)} %get-tuple-element.83.lower_0, ...), custom_call_target="tpu_custom_call" | custom-call | flops 1073741824 | bytes 25165824 | tf_op jit(solution)/shard_map/last_step/pallas_call | solution.py:577
  84.4 6.9 %collective-permute-start.25 = (bf16[2,8,128,128]{3,2,1,0:T(8,128)(2,1)S(1)}, bf16[2,8,128,128]{3,2,1,0:T(8,128)(2,1)S(1)}, u32[]{:S(2)}, u32[]{:S(2)}) collective-permute-start(bf16[2,8,128,128]{3,2,1,0:T(8,128)(2,1)S(1)} %near_message.1), channel_id=1, source_target_pairs={{4,0},{8,4},{12,8},{16,12},{20,16},{24,20},{28,24},{32,28},{36,32}... | collective-permute-start | bytes 1572872 | tf_op jit(solution)/shard_map/ppermute | solution.py:761
  94.0 1.6 %collective-permute-done.22.tile_2 = bf16[16,128]{1,0:T(8,128)(2,1)S(1)} collective-permute-done((bf16[16,128]{1,0:T(8,128)(2,1)S(1)}, bf16[16,128]{1,0:T(8,128)(2,1)S(1)}, u32[]{:S(2)}, u32[]{:S(2)}) %collective-permute-start.22) | collective-permute-done | bytes 4128 | tf_op jit(solution)/shard_map/ppermute | solution.py:684
  96.8 2.7 %collective-permute-start.24 = (bf16[16,128]{1,0:T(8,128)(2,1)S(1)}, bf16[16,128]{1,0:T(8,128)(2,1)S(1)}, u32[]{:S(2)}, u32[]{:S(2)}) collective-permute-start(bf16[16,128]{1,0:T(8,128)(2,1)S(1)} %get-tuple-element.95.factors_ref), channel_id=1, source_target_pairs={{4,0},{8,4},{12,8},{16,12},{20,16},{24,20},{28,24},{32,28},{36,32}... | collective-permute-start | bytes 12296 | tf_op jit(solution)/shard_map/ppermute | solution.py:763
  (56 shorter events, 21.6 us)
Async XLA Ops:
  0.6 5.6 %collective-permute-start = (f32[8,128,128]{2,1,0:T(8,128)}, f32[8,128,128]{2,1,0:T(8,128)S(1)}, u32[]{:S(2)}, u32[]{:S(2)}) collective-permute-start(f32[8,128,128]{2,1,0:T(8,128)} %bitcast.21), channel_id=1, source_target_pairs={{0,4},{4,0},{8,12},{12,8},{16,20},{20,16},{24,28},{28,24},{32,36},... | collective-permute-start | bytes 1572872 | tf_op jit(solution)/shard_map/ppermute | solution.py:724
  7.2 18.7 %all-to-all-start = ((bf16[32,24,128]{2,1,0:T(8,128)(2,1)}), bf16[32,24,128]{2,1,0:T(8,128)(2,1)S(1)}, u32[]{:S(2)}, u32[]{:S(2)}) async-start(bf16[32,24,128]{2,1,0:T(8,128)(2,1)} %chip_maps.1), calls=%async_computation | async-start | bytes 393216 | tf_op jit(solution)/shard_map/all_to_all | solution.py:731
  16.5 18.2 %collective-permute-start.4 = (bf16[8,128,128]{2,1,0:T(8,128)(2,1)S(1)}, bf16[8,128,128]{2,1,0:T(8,128)(2,1)}, u32[]{:S(2)}, u32[]{:S(2)}) collective-permute-start(bf16[8,128,128]{2,1,0:T(8,128)(2,1)S(1)} %get-tuple-element.57.psi_0), channel_id=1, source_target_pairs={{0,3},{1,0},{2,1},{3,2},{4,7},{5,4},{6,5},{7,6},{8,11},{9,8},{10,9... | collective-permute-start | bytes 786440 | tf_op jit(solution)/shard_map/ppermute | solution.py:684
  19.4 15.5 %collective-permute-start.3 = (bf16[8,128,128]{2,1,0:T(8,128)(2,1)S(1)}, bf16[8,128,128]{2,1,0:T(8,128)(2,1)S(1)}, u32[]{:S(2)}, u32[]{:S(2)}) collective-permute-start(bf16[8,128,128]{2,1,0:T(8,128)(2,1)S(1)} %get-tuple-element.57.psi_0), channel_id=1, source_target_pairs={{0,2},{1,3},{2,0},{3,1},{4,6},{5,7},{6,4},{7,5},{8,10},{9,11},{10,... | collective-permute-start | bytes 786440 | tf_op jit(solution)/shard_map/ppermute | solution.py:684
  19.7 16.3 %collective-permute-start.2 = (bf16[8,128,128]{2,1,0:T(8,128)(2,1)S(1)}, bf16[8,128,128]{2,1,0:T(8,128)(2,1)S(1)}, u32[]{:S(2)}, u32[]{:S(2)}) collective-permute-start(bf16[8,128,128]{2,1,0:T(8,128)(2,1)S(1)} %get-tuple-element.57.psi_0), channel_id=1, source_target_pairs={{0,1},{1,2},{2,3},{3,0},{4,5},{5,6},{6,7},{7,4},{8,9},{9,10},{10,1... | collective-permute-start | bytes 786440 | tf_op jit(solution)/shard_map/ppermute | solution.py:684
  21.2 22.5 %collective-permute-start.6 = (bf16[8,128,128]{2,1,0:T(8,128)(2,1)}, bf16[8,128,128]{2,1,0:T(8,128)(2,1)S(1)}, u32[]{:S(2)}, u32[]{:S(2)}) collective-permute-start(bf16[8,128,128]{2,1,0:T(8,128)(2,1)} %get-tuple-element.60), channel_id=1, source_target_pairs={{0,3},{1,0},{2,1},{3,2},{4,7},{5,4},{6,5},{7,6},{8,11},{9,8},{10,9... | collective-permute-start | bytes 786440 | tf_op jit(solution)/shard_map/ppermute | solution.py:684
  23.2 20.5 %collective-permute-start.5 = (bf16[8,128,128]{2,1,0:T(8,128)(2,1)}, bf16[8,128,128]{2,1,0:T(8,128)(2,1)S(1)}, u32[]{:S(2)}, u32[]{:S(2)}) collective-permute-start(bf16[8,128,128]{2,1,0:T(8,128)(2,1)} %get-tuple-element.60), channel_id=1, source_target_pairs={{0,2},{1,3},{2,0},{3,1},{4,6},{5,7},{6,4},{7,5},{8,10},{9,11},{10,... | collective-permute-start | bytes 786440 | tf_op jit(solution)/shard_map/ppermute | solution.py:684
  26.9 17.1 %all-to-all-start.1 = ((bf16[32,16,128]{2,1,0:T(8,128)(2,1)}), bf16[32,16,128]{2,1,0:T(8,128)(2,1)S(1)}, u32[]{:S(2)}, u32[]{:S(2)}) async-start(bf16[32,16,128]{2,1,0:T(8,128)(2,1)} %scan_maps.1), calls=%async_computation.1 | async-start | bytes 262144 | tf_op jit(solution)/shard_map/all_to_all | solution.py:738
  34.8 15.6 %collective-permute-start.8 = (bf16[8,128,128]{2,1,0:T(8,128)(2,1)}, bf16[8,128,128]{2,1,0:T(8,128)(2,1)S(1)}, u32[]{:S(2)}, u32[]{:S(2)}) collective-permute-start(bf16[8,128,128]{2,1,0:T(8,128)(2,1)} %get-tuple-element.60), channel_id=1, source_target_pairs={{0,1},{1,2},{2,3},{3,0},{4,5},{5,6},{6,7},{7,4},{8,9},{9,10},{10,1... | collective-permute-start | bytes 786440 | tf_op jit(solution)/shard_map/ppermute | solution.py:684
  44.0 4.8 %collective-permute-start.7 = (bf16[4,128,128]{2,1,0:T(8,128)(2,1)S(1)}, bf16[4,128,128]{2,1,0:T(8,128)(2,1)S(1)}, u32[]{:S(2)}, u32[]{:S(2)}) collective-permute-start(bf16[4,128,128]{2,1,0:T(8,128)(2,1)S(1)} %bitcast.11), channel_id=1, source_target_pairs={{0,4},{4,0},{8,12},{12,8},{16,20},{20,16},{24,28},{28,24},{32,36},... | collective-permute-start | bytes 393224 | tf_op jit(solution)/shard_map/ppermute | solution.py:742
  50.3 5.2 %collective-permute-start.13 = (bf16[528,128]{1,0:T(8,128)(2,1)S(1)}, bf16[528,128]{1,0:T(8,128)(2,1)S(1)}, u32[]{:S(2)}, u32[]{:S(2)}) collective-permute-start(bf16[528,128]{1,0:T(8,128)(2,1)S(1)} %get-tuple-element.68.lower_0), channel_id=1, source_target_pairs={{0,3},{1,0},{2,1},{3,2},{4,7},{5,4},{6,5},{7,6},{8,11},{9,8},{10,9... | collective-permute-start | bytes 405512 | tf_op jit(solution)/shard_map/ppermute | solution.py:684
  50.9 7.2 %collective-permute-start.10 = (bf16[512,128]{1,0:T(8,128)(2,1)S(1)}, bf16[512,128]{1,0:T(8,128)(2,1)S(1)}, u32[]{:S(2)}, u32[]{:S(2)}) collective-permute-start(bf16[512,128]{1,0:T(8,128)(2,1)S(1)} %get-tuple-element.69), channel_id=1, source_target_pairs={{0,3},{1,0},{2,1},{3,2},{4,7},{5,4},{6,5},{7,6},{8,11},{9,8},{10,9... | collective-permute-start | bytes 393224 | tf_op jit(solution)/shard_map/ppermute | solution.py:684
  52.3 5.8 %collective-permute-start.9 = (bf16[512,128]{1,0:T(8,128)(2,1)S(1)}, bf16[512,128]{1,0:T(8,128)(2,1)S(1)}, u32[]{:S(2)}, u32[]{:S(2)}) collective-permute-start(bf16[512,128]{1,0:T(8,128)(2,1)S(1)} %get-tuple-element.69), channel_id=1, source_target_pairs={{0,1},{1,2},{2,3},{3,0},{4,5},{5,6},{6,7},{7,4},{8,9},{9,10},{10,1... | collective-permute-start | bytes 393224 | tf_op jit(solution)/shard_map/ppermute | solution.py:684
  52.3 8.1 %collective-permute-start.11 = (bf16[528,128]{1,0:T(8,128)(2,1)S(1)}, bf16[528,128]{1,0:T(8,128)(2,1)S(1)}, u32[]{:S(2)}, u32[]{:S(2)}) collective-permute-start(bf16[528,128]{1,0:T(8,128)(2,1)S(1)} %get-tuple-element.68.lower_0), channel_id=1, source_target_pairs={{0,1},{1,2},{2,3},{3,0},{4,5},{5,6},{6,7},{7,4},{8,9},{9,10},{10,1... | collective-permute-start | bytes 405512 | tf_op jit(solution)/shard_map/ppermute | solution.py:684
  55.6 7.5 %collective-permute-start.14 = (bf16[528,128]{1,0:T(8,128)(2,1)S(1)}, bf16[528,128]{1,0:T(8,128)(2,1)S(1)}, u32[]{:S(2)}, u32[]{:S(2)}) collective-permute-start(bf16[528,128]{1,0:T(8,128)(2,1)S(1)} %collective-permute-done.13.lower_3), channel_id=1, source_target_pairs={{0,3},{1,0},{2,1},{3,2},{4,7},{5,4},{6,5},{7,6},{8,11},{9,8},{10,9... | collective-permute-start | bytes 405512 | tf_op jit(solution)/shard_map/ppermute | solution.py:684
  58.0 5.0 %collective-permute-start.12 = (bf16[512,128]{1,0:T(8,128)(2,1)S(1)}, bf16[512,128]{1,0:T(8,128)(2,1)S(1)}, u32[]{:S(2)}, u32[]{:S(2)}) collective-permute-start(bf16[512,128]{1,0:T(8,128)(2,1)S(1)} %collective-permute-done.9.upper_1), channel_id=1, source_target_pairs={{0,1},{1,2},{2,3},{3,0},{4,5},{5,6},{6,7},{7,4},{8,9},{9,10},{10,1... | collective-permute-start | bytes 393224 | tf_op jit(solution)/shard_map/ppermute | solution.py:684
  67.2 5.2 %collective-permute-start.19 = (bf16[528,128]{1,0:T(8,128)(2,1)S(1)}, bf16[528,128]{1,0:T(8,128)(2,1)S(1)}, u32[]{:S(2)}, u32[]{:S(2)}) collective-permute-start(bf16[528,128]{1,0:T(8,128)(2,1)S(1)} %get-tuple-element.83.lower_0), channel_id=1, source_target_pairs={{0,3},{1,0},{2,1},{3,2},{4,7},{5,4},{6,5},{7,6},{8,11},{9,8},{10,9... | collective-permute-start | bytes 405512 | tf_op jit(solution)/shard_map/ppermute | solution.py:684
  68.0 6.4 %collective-permute-start.16 = (bf16[512,128]{1,0:T(8,128)(2,1)S(1)}, bf16[512,128]{1,0:T(8,128)(2,1)S(1)}, u32[]{:S(2)}, u32[]{:S(2)}) collective-permute-start(bf16[512,128]{1,0:T(8,128)(2,1)S(1)} %get-tuple-element.84), channel_id=1, source_target_pairs={{0,3},{1,0},{2,1},{3,2},{4,7},{5,4},{6,5},{7,6},{8,11},{9,8},{10,9... | collective-permute-start | bytes 393224 | tf_op jit(solution)/shard_map/ppermute | solution.py:684
  68.2 6.2 %collective-permute-start.15 = (bf16[512,128]{1,0:T(8,128)(2,1)S(1)}, bf16[512,128]{1,0:T(8,128)(2,1)S(1)}, u32[]{:S(2)}, u32[]{:S(2)}) collective-permute-start(bf16[512,128]{1,0:T(8,128)(2,1)S(1)} %get-tuple-element.84), channel_id=1, source_target_pairs={{0,1},{1,2},{2,3},{3,0},{4,5},{5,6},{6,7},{7,4},{8,9},{9,10},{10,1... | collective-permute-start | bytes 393224 | tf_op jit(solution)/shard_map/ppermute | solution.py:684
  69.4 7.2 %collective-permute-start.17 = (bf16[528,128]{1,0:T(8,128)(2,1)S(1)}, bf16[528,128]{1,0:T(8,128)(2,1)S(1)}, u32[]{:S(2)}, u32[]{:S(2)}) collective-permute-start(bf16[528,128]{1,0:T(8,128)(2,1)S(1)} %get-tuple-element.83.lower_0), channel_id=1, source_target_pairs={{0,1},{1,2},{2,3},{3,0},{4,5},{5,6},{6,7},{7,4},{8,9},{9,10},{10,1... | collective-permute-start | bytes 405512 | tf_op jit(solution)/shard_map/ppermute | solution.py:684
  72.4 7.8 %collective-permute-start.20 = (bf16[528,128]{1,0:T(8,128)(2,1)S(1)}, bf16[528,128]{1,0:T(8,128)(2,1)S(1)}, u32[]{:S(2)}, u32[]{:S(2)}) collective-permute-start(bf16[528,128]{1,0:T(8,128)(2,1)S(1)} %collective-permute-done.19.lower_3), channel_id=1, source_target_pairs={{0,3},{1,0},{2,1},{3,2},{4,7},{5,4},{6,5},{7,6},{8,11},{9,8},{10,9... | collective-permute-start | bytes 405512 | tf_op jit(solution)/shard_map/ppermute | solution.py:684
  74.4 5.8 %collective-permute-start.18 = (bf16[512,128]{1,0:T(8,128)(2,1)S(1)}, bf16[512,128]{1,0:T(8,128)(2,1)S(1)}, u32[]{:S(2)}, u32[]{:S(2)}) collective-permute-start(bf16[512,128]{1,0:T(8,128)(2,1)S(1)} %collective-permute-done.15.upper_1), channel_id=1, source_target_pairs={{0,1},{1,2},{2,3},{3,0},{4,5},{5,6},{6,7},{7,4},{8,9},{9,10},{10,1... | collective-permute-start | bytes 393224 | tf_op jit(solution)/shard_map/ppermute | solution.py:684
  84.4 17.7 %collective-permute-start.25 = (bf16[2,8,128,128]{3,2,1,0:T(8,128)(2,1)S(1)}, bf16[2,8,128,128]{3,2,1,0:T(8,128)(2,1)S(1)}, u32[]{:S(2)}, u32[]{:S(2)}) collective-permute-start(bf16[2,8,128,128]{3,2,1,0:T(8,128)(2,1)S(1)} %near_message.1), channel_id=1, source_target_pairs={{4,0},{8,4},{12,8},{16,12},{20,16},{24,20},{28,24},{32,28},{36,32}... | collective-permute-start | bytes 1572872 | tf_op jit(solution)/shard_map/ppermute | solution.py:761
  96.8 5.3 %collective-permute-start.24 = (bf16[16,128]{1,0:T(8,128)(2,1)S(1)}, bf16[16,128]{1,0:T(8,128)(2,1)S(1)}, u32[]{:S(2)}, u32[]{:S(2)}) collective-permute-start(bf16[16,128]{1,0:T(8,128)(2,1)S(1)} %get-tuple-element.95.factors_ref), channel_id=1, source_target_pairs={{4,0},{8,4},{12,8},{16,12},{20,16},{24,20},{28,24},{32,28},{36,32}... | collective-permute-start | bytes 12296 | tf_op jit(solution)/shard_map/ppermute | solution.py:763
  (8 other events, 64.2 us)
